TPU v7x, 128 devices: a whole 4x4x4 slice. The times are simulated.
128 devices in a mesh: wide: 32 (over y, z, core), narrow: 4 (over x).
Axes of the slice: x: 4, y: 4, z: 4, core: 2. Of those that a mesh axis runs over, the one named last changes fastest.
Arguments:
- tensor: float32 [32, 128, 256, 672], P('narrow', 'wide'), may hold values from -6 to 6
- mode2_factor: float32 [128, 96], replicated, may hold values from -0.5 to 0.5
- mode3_factor: float32 [256, 96], replicated, may hold values from -0.375 to 0.375
- mode4_factor: float32 [32, 16], replicated, may hold values from -1 to 1
- start_basis: float32 [672, 96], replicated, may hold values from -6 to 6
Outputs:
- scaled_basis: float32 [672, 96], replicated
All inputs are finite; a program needn't handle non-finite values.
Results may differ from a plain program's by a relative error of at most 0.0003.
Values sent between devices are 32-bit elements; how exact they have to be, the bound alone decides.
No kernel may reach another device: no remote copies, remote signals or barrier semaphores. Data moves between devices by JAX's collectives and lax.ppermute only.
A program may use at most 192 MiB of HBM per device.

v0:
```python
import math

import jax
import jax.numpy as jnp
from jax import lax
from jax.sharding import PartitionSpec as P

I1 = 672
R2 = 96
R3 = 96
R4 = 16
ITERS = 8


def orthonormal(vectors):
    highest = lax.Precision.HIGHEST
    inner = lax.dot_general(vectors, vectors, (((0,), (0,)), ((), ())), precision=highest)
    lower_factor = jnp.linalg.cholesky(inner)
    return lax.linalg.triangular_solve(
        lower_factor, vectors, left_side=False, lower=True, transpose_a=True
    )


def body(tensor, mode2_factor, mode3_factor, mode4_factor, start_basis):
    highest = lax.Precision.HIGHEST
    local_species = tensor.shape[0]
    blocks = tensor.shape[1]
    mode1_cells = tensor.shape[3]
    by_mode3 = jnp.einsum("sbka,kr->sbra", tensor, mode3_factor, precision=highest)
    offset = lax.axis_index("narrow") * local_species
    own_species = lax.dynamic_slice_in_dim(mode4_factor, offset, local_species, 0)
    by_mode4 = lax.psum_scatter(
        jnp.einsum("sbra,sq->rqba", by_mode3, own_species, precision=highest),
        "narrow",
        scatter_dimension=0,
        tiled=True,
    )
    merged = by_mode4.reshape(-1, blocks, mode1_cells)
    core_block = jnp.einsum(
        "osn,si->oin",
        lax.all_to_all(merged, "wide", split_axis=0, concat_axis=1, tiled=True),
        mode2_factor,
        precision=highest,
    )
    columns_flat = core_block.reshape(-1, mode1_cells)
    normalizer = 1.0 / (R2 * R3 * R4)
    basis_now = start_basis
    partial_value = lax.dot_general(
        columns_flat, columns_flat, (((0,), (0,)), ((), ())), precision=highest
    )
    gram_matrix = lax.psum(partial_value, ("wide", "narrow")) * normalizer
    for sweep in range(ITERS):
        basis_now = orthonormal(jnp.dot(gram_matrix, basis_now, precision=highest))
    return basis_now * math.sqrt(I1)


def solution(mesh):
    in_specs = (P("narrow", "wide", None, None), P(), P(), P(), P())
    out_specs = P()
    return jax.shard_map(body, mesh=mesh, in_specs=in_specs, out_specs=out_specs, check_vma=False)
```

profile of v0, /device:TPU:1, one launch (start us, length us, event | category | flops | bytes accessed | tf_op | source)
XLA Modules:
  0.0 647.9 jit_solution(8327086205944534244)
XLA Ops:
  6.5 23.4 %convolution_bitcast_fusion = f32[8,4,96,672]{3,2,1,0:T(8,128)S(1)} fusion(f32[8,4,256,672]{2,3,1,0:T(8,128)} %param.8, f32[256,96]{0,1:T(8,128)} %param.10), kind=kOutput, calls=%fused_computation.6 | convolution fusion | flops 6341787648 | bytes 30375936 | tf_op jit(solution)/shard_map/sbka,kr->sbra/dot_general | solution.py:29
  29.9 20.2 %fusion.2 = f32[96,16,4,672]{3,1,0,2:T(8,128)S(1)} fusion(f32[8,4,96,672]{3,2,1,0:T(8,128)S(1)} %convolution_bitcast_fusion, f32[32,16]{0,1:T(8,128)S(1)} %copy-done.3, s32[]{:T(128)S(6)} %select_n.6), kind=kOutput, calls=%fused_computation.3 | convolution fusion | flops 396361728 | bytes 24774660 | tf_op jit(solution)/shard_map/sbra,sq->rqba/dot_general | solution.py:33
  50.1 6.8 %copy.50 = f32[96,16,4,672]{3,1,2,0:T(8,128)} copy(f32[96,16,4,672]{3,1,0,2:T(8,128)S(1)} %fusion.2) | data formatting | bytes 33030144
  57.0 19.3 %reshape.50 = f32[96,43008]{1,0:T(8,128)} reshape(f32[96,4,16,672]{3,2,1,0:T(8,128)} %bitcast.161) | data formatting | bytes 33030144
  76.4 149.1 %reduce-scatter.4.cloned.1.call-done = f32[24,43008]{1,0:T(8,128)} async-done(((f32[96,43008]{1,0:T(8,128)}), f32[24,43008]{1,0:T(8,128)}) %reduce-scatter.4.cloned.1.call-update) | async-done | bytes 4128784
  225.5 7.2 %reshape.51 = f32[24,4,16,672]{3,2,1,0:T(8,128)} reshape(f32[24,43008]{1,0:T(8,128)} %reduce-scatter.4.cloned.1.call-done) | data formatting | bytes 8257536
  232.7 2.7 copy.43
  235.4 3.0 copy.28
  238.4 64.0 %all_to_all.18 = f32[384,4,672]{2,1,0:T(4,128)S(1)} all-to-all(f32[384,4,672]{2,1,0:T(4,128)S(1)} %copy.28), channel_id=1, replica_groups=mesh['wide'=32,'narrow'=4] {'wide'}, dimensions={0} | all-to-all | bytes 8257536 | tf_op jit(solution)/shard_map/all_to_all | solution.py:41
  302.4 3.2 copy.29
  305.7 6.4 all_to_all.16
  312.1 5.6 fusion.60
  317.7 9.9 %fusion.7 = f32[672,672]{1,0:T(8,128)} fusion(f32[12,672,96]{1,2,0:T(8,128)S(1)} %fusion.60), kind=kOutput, calls=%fused_computation.7 | convolution fusion | flops 6242697216 | bytes 4902912 | tf_op jit(solution)/shard_map/dot_general | solution.py:48
  327.6 146.3 %all-reduce.2.cloned.1.call-done = f32[672,672]{1,0:T(8,128)} async-done(((f32[672,672]{1,0:T(8,128)}), f32[672,672]{1,0:T(8,128)}) %all-reduce.2.cloned.1.call-update) | async-done | bytes 1806352 | tf_op jit(solution)/shard_map/psum | solution.py:51
  473.9 3.7 fusion.24
  478.1 9.0 %cholesky.134 = f32[96,96]{1,0:T(8,128)S(1)} custom-call(f32[96,96]{1,0:T(8,128)S(1)} %fusion.59), custom_call_target="Cholesky" | custom-call | tf_op jit(solution)/shard_map/jit(cholesky)/cholesky | solution.py:18
  488.4 7.4 %custom-call.12 = f32[1,96,96]{1,2,0:T(8,128)S(1)} custom-call(f32[1,96,96]{2,1,0:T(8,128)S(1)} %fusion.36), custom_call_target="InvertDiagBlocksLowerTriangular" | custom-call | tf_op jit(solution)/shard_map/triangular_solve/custom-call.0 | solution.py:19
  496.2 2.0 fusion.22
  498.8 8.8 %cholesky.145 = f32[96,96]{1,0:T(8,128)S(1)} custom-call(f32[96,96]{1,0:T(8,128)S(1)} %fusion.57), custom_call_target="Cholesky" | custom-call | tf_op jit(solution)/shard_map/jit(cholesky)/cholesky | solution.py:18
  508.9 7.4 %custom-call.13 = f32[1,96,96]{1,2,0:T(8,128)S(1)} custom-call(f32[1,96,96]{2,1,0:T(8,128)S(1)} %fusion.37), custom_call_target="InvertDiagBlocksLowerTriangular" | custom-call | tf_op jit(solution)/shard_map/triangular_solve/custom-call.0 | solution.py:19
  519.2 9.2 %cholesky.156 = f32[96,96]{1,0:T(8,128)S(1)} custom-call(f32[96,96]{1,0:T(8,128)S(1)} %fusion.55), custom_call_target="Cholesky" | custom-call | tf_op jit(solution)/shard_map/jit(cholesky)/cholesky | solution.py:18
  529.7 7.4 %custom-call.14 = f32[1,96,96]{1,2,0:T(8,128)S(1)} custom-call(f32[1,96,96]{2,1,0:T(8,128)S(1)} %fusion.38), custom_call_target="InvertDiagBlocksLowerTriangular" | custom-call | tf_op jit(solution)/shard_map/triangular_solve/custom-call.0 | solution.py:19
  540.1 8.8 %cholesky.167 = f32[96,96]{1,0:T(8,128)S(1)} custom-call(f32[96,96]{1,0:T(8,128)S(1)} %fusion.53), custom_call_target="Cholesky" | custom-call | tf_op jit(solution)/shard_map/jit(cholesky)/cholesky | solution.py:18
  550.2 7.4 %custom-call.15 = f32[1,96,96]{1,2,0:T(8,128)S(1)} custom-call(f32[1,96,96]{2,1,0:T(8,128)S(1)} %fusion.39), custom_call_target="InvertDiagBlocksLowerTriangular" | custom-call | tf_op jit(solution)/shard_map/triangular_solve/custom-call.0 | solution.py:19
  560.5 8.9 %cholesky.178 = f32[96,96]{1,0:T(8,128)S(1)} custom-call(f32[96,96]{1,0:T(8,128)S(1)} %fusion.51), custom_call_target="Cholesky" | custom-call | tf_op jit(solution)/shard_map/jit(cholesky)/cholesky | solution.py:18
  570.8 7.4 %custom-call.16 = f32[1,96,96]{1,2,0:T(8,128)S(1)} custom-call(f32[1,96,96]{2,1,0:T(8,128)S(1)} %fusion.40), custom_call_target="InvertDiagBlocksLowerTriangular" | custom-call | tf_op jit(solution)/shard_map/triangular_solve/custom-call.0 | solution.py:19
  581.1 8.8 %cholesky.189 = f32[96,96]{1,0:T(8,128)S(1)} custom-call(f32[96,96]{1,0:T(8,128)S(1)} %fusion.49), custom_call_target="Cholesky" | custom-call | tf_op jit(solution)/shard_map/jit(cholesky)/cholesky | solution.py:18
  591.2 7.4 %custom-call.17 = f32[1,96,96]{1,2,0:T(8,128)S(1)} custom-call(f32[1,96,96]{2,1,0:T(8,128)S(1)} %fusion.41), custom_call_target="InvertDiagBlocksLowerTriangular" | custom-call | tf_op jit(solution)/shard_map/triangular_solve/custom-call.0 | solution.py:19
  601.6 9.0 %cholesky.200 = f32[96,96]{1,0:T(8,128)S(1)} custom-call(f32[96,96]{1,0:T(8,128)S(1)} %fusion.47), custom_call_target="Cholesky" | custom-call | tf_op jit(solution)/shard_map/jit(cholesky)/cholesky | solution.py:18
  611.9 7.4 %custom-call.18 = f32[1,96,96]{1,2,0:T(8,128)S(1)} custom-call(f32[1,96,96]{2,1,0:T(8,128)S(1)} %fusion.42), custom_call_target="InvertDiagBlocksLowerTriangular" | custom-call | tf_op jit(solution)/shard_map/triangular_solve/custom-call.0 | solution.py:19
  622.2 8.8 %cholesky.211 = f32[96,96]{1,0:T(8,128)S(1)} custom-call(f32[96,96]{1,0:T(8,128)S(1)} %fusion.45), custom_call_target="Cholesky" | custom-call | tf_op jit(solution)/shard_map/jit(cholesky)/cholesky | solution.py:18
  632.3 7.4 %custom-call.19 = f32[1,96,96]{1,2,0:T(8,128)S(1)} custom-call(f32[1,96,96]{2,1,0:T(8,128)S(1)} %fusion.43), custom_call_target="InvertDiagBlocksLowerTriangular" | custom-call | tf_op jit(solution)/shard_map/triangular_solve/custom-call.0 | solution.py:19
  (74 shorter events, 30.9 us)
Async XLA Ops:
  6.5 467.3 %copy-start = (f32[672,96]{0,1:T(8,128)S(1)}, f32[672,96]{0,1:T(8,128)}, u32[]{:S(2)}) copy-start(f32[672,96]{0,1:T(8,128)} %param.12) | copy-start | bytes 774148
  6.5 219.0 %reduce-scatter.4.cloned.1.call-start = ((), (), s32[]{:S(2)}) async-start(), calls=%async_computation.3 | async-start | bytes 20643840
  6.5 23.4 %copy-start.3 = (f32[32,16]{0,1:T(8,128)S(1)}, f32[32,16]{0,1:T(8,128)}, u32[]{:S(2)}) copy-start(f32[32,16]{0,1:T(8,128)} %param.11) | copy-start | bytes 6148
  76.3 397.6 %all-reduce.2.cloned.1.call-start = ((), (), s32[]{:S(2)}) async-start(), calls=%async_computation.2 | async-start | bytes 4128768 | tf_op jit(solution)/shard_map/psum | solution.py:51
  305.7 6.4 copy-start.2
  473.9 22.4 %copy-start.1 = (f32[672,672]{1,0:T(8,128)S(1)}, f32[672,672]{1,0:T(8,128)}, u32[]{:S(2)}) copy-start(f32[672,672]{1,0:T(8,128)} %all-reduce.2.cloned.1.call-done) | copy-start | bytes 5419012
Sparse Core Ops, SparseCore 0:
  76.4 149.0 reduce-scatter.3
  327.7 146.1 all-reduce.1
where the time goes:
time: 652 us; the launch traced here: 648 us
  waiting for transfers between devices  295 us (45%)
  other arithmetic  141 us (22%)
  matrix products  84.2 us (13%)
  blocking collectives  64 us (10%)
  local copies, waits for them, and re-layouts  49.4 us (8%)
  between operations  14.1 us (2%)
    unnamed x3, waiting for transfers between devices  149 us
    psum x1, waiting for transfers between devices, body(): gram_matrix = lax.psum(partial_value, ('wide', 'narrow')) * normalizer  146 us
    another operation x24, other arithmetic, orthonormal(): lower_factor = jnp.linalg.cholesky(inner)  76.6 us
    another operation x16, other arithmetic, orthonormal(): lax.linalg.triangular_solve(lower_factor, vectors, left_side=False, lower...  64.1 us
    all_to_all x1, blocking collectives, body(): lax.all_to_all(merged, 'wide', split_axis=0, concat_axis=1, tiled=True)  64 us
    unnamed x12, local copies, waits for them, and re-layouts  36 us
    dot_general x1, matrix products, body(): jnp.einsum('sbka,kr->sbra', tensor, mode3_factor, precision=highest)  23.4 us
    dot_general x1, matrix products, body(): jnp.einsum('sbra,sq->rqba', by_mode3, own_species, precision=highest)  20.2 us
  transfers between devices with their start and end apart: 2, of which 2 were waited for; matrix products, arithmetic and copies ran while one was open for 0% of the time, Pallas kernels for 0%

commit v1 on v0

v1 whole, which is shorter than its diff:
```python
import functools
import math

import jax
import jax.numpy as jnp
from jax import lax
from jax.experimental import pallas as pl
from jax.experimental.pallas import tpu as pltpu
from jax.sharding import PartitionSpec as P

I1 = 672
I2 = 128
I3 = 256
R1 = 96
R2 = 96
R3 = 96
R4 = 16
ITERS = 8
NARROW = 4
WIDE = 32
LANES = 128
FULL = I1 // LANES
TAIL = I1 - FULL * LANES
BODY = FULL * LANES
LOCAL2 = I2 // WIDE
RANKS = R3 // NARROW
PAIRS = RANKS * R4 // WIDE
ORDER = (0, 3, 1, 2)
LAST = LOCAL2 - 1
VMEM = pl.BlockSpec(memory_space=pltpu.VMEM)


def split(x):
    high = x.astype(jnp.bfloat16)
    return high, (x - high.astype(jnp.float32)).astype(jnp.bfloat16)


def product(a, b, contract):
    return lax.dot_general(
        a, b, ((contract), ((), ())), preferred_element_type=jnp.float32
    )


def exact(a, b, contract):
    return lax.dot_general(
        a, b, ((contract), ((), ())),
        preferred_element_type=jnp.float32, precision=lax.Precision.HIGHEST,
    )


def left_product(weights, values):
    rows = weights.shape[0]
    w_high, w_low = split(weights)
    v_high, v_low = split(values)
    both = product(jnp.concatenate([w_high, w_low], axis=0), v_high, ((1,), (0,)))
    return both[:rows] + both[rows:] + product(w_high, v_low, ((1,), (0,)))


def mode3_kernel(tails, factor_ref, slab_ref, *refs):
    if tails:
        tail_ref, outs = refs[0], refs[1:]
        left_over = [tail_ref[0, b, :, :TAIL] for b in range(LOCAL2)]
        slab = jnp.concatenate([slab_ref[0, 0]] + left_over, axis=1)
    else:
        outs = refs
        slab = slab_ref[0, 0]
    done = left_product(factor_ref[...], slab)
    for j, out in enumerate(outs):
        out[0] = done[j * RANKS:(j + 1) * RANKS]


def mode3(tensor, factor_rows, cell):
    species = tensor.shape[0]
    tails = cell == LAST
    width = BODY + (LANES if tails else 0)
    in_specs = [
        pl.BlockSpec((R3, I3), lambda s: (0, 0)),
        pl.BlockSpec((1, 1, I3, BODY), lambda s: (s, cell, 0, 0)),
    ]
    args = [factor_rows, tensor]
    if tails:
        in_specs.append(pl.BlockSpec((1, LOCAL2, I3, LANES), lambda s: (s, 0, 0, FULL)))
        args.append(tensor)
    shape = jax.ShapeDtypeStruct((species, RANKS, width), jnp.float32)
    return pl.pallas_call(
        functools.partial(mode3_kernel, tails),
        grid=(species,),
        in_specs=in_specs,
        out_specs=[pl.BlockSpec((1, RANKS, width), lambda s: (s, 0, 0))] * NARROW,
        out_shape=[shape] * NARROW,
        compiler_params=pltpu.CompilerParams(vmem_limit_bytes=32 << 20),
        cost_estimate=pl.CostEstimate(
            flops=6 * species * R3 * I3 * width,
            bytes_accessed=4 * species * width * (I3 + R3), transcendentals=0),
        name="mode3",
    )(*args)


def species_kernel(tiles, weights_ref, *refs):
    parts, out = refs[:NARROW], refs[NARROW]
    step = pl.program_id(0)
    rows = [p[...].reshape(-1, tiles * LANES) for p in parts]
    done = left_product(weights_ref[...], jnp.concatenate(rows, axis=0))

    def put(dest, first, q, start, count):
        for t in range(tiles):
            out[dest, t * PAIRS + first:t * PAIRS + first + count, :] = done[
                q * 8 + start:q * 8 + start + count, t * LANES:(t + 1) * LANES]

    @pl.when(step == 0)
    def _():
        spare = out.shape[1] - tiles * PAIRS
        if spare:
            out[:, tiles * PAIRS:, :] = jnp.zeros((WIDE, spare, LANES), jnp.float32)
        for q in range(R4):
            put(2 * q, 0, q, 0, 8)

    @pl.when(step == 1)
    def _():
        for q in range(R4):
            put(2 * q, 8, q, 0, 4)
            put(2 * q + 1, 0, q, 4, 4)

    @pl.when(step == 2)
    def _():
        for q in range(R4):
            put(2 * q + 1, 4, q, 0, 8)


def species_sum(parts, weights):
    species, ranks, width = parts[0].shape
    tiles = width // LANES
    rows = -(-tiles * PAIRS // 8) * 8
    return pl.pallas_call(
        functools.partial(species_kernel, tiles),
        grid=(ranks // 8,),
        in_specs=[pl.BlockSpec(weights.shape, lambda i: (0, 0))]
        + [pl.BlockSpec((species, 8, width), lambda i: (0, i, 0))] * NARROW,
        out_specs=pl.BlockSpec((WIDE, rows, LANES), lambda i: (0, 0, 0)),
        out_shape=jax.ShapeDtypeStruct((WIDE, rows, LANES), jnp.float32),
        compiler_params=pltpu.CompilerParams(vmem_limit_bytes=32 << 20),
        cost_estimate=pl.CostEstimate(
            flops=6 * 128 * 256 * 3 * width, bytes_accessed=4 * width * 24 * 48, transcendentals=0),
        name="species",
    )(weights, *parts)


def gram_kernel(factor_ref, *refs):
    parts = refs[:LOCAL2]
    out, high_ref, low_ref, gram_ref = refs[LOCAL2:]
    f_high, f_low = split(factor_ref[...])
    doubled = jnp.concatenate([f_high, f_high], axis=1)
    stride = [p.shape[0] // WIDE for p in parts]
    for i in range(PAIRS):
        tail = parts[LAST][pl.ds(FULL * PAIRS + i, WIDE, stride=stride[LAST]), :]
        cells = []
        for b in range(LOCAL2):
            row = [parts[b][pl.ds(t * PAIRS + i, WIDE, stride=stride[b]), :] for t in range(FULL)]
            row.append(tail[:, b * TAIL:(b + 1) * TAIL])
            cells.append(jnp.concatenate(row, axis=1))
        values = jnp.concatenate(cells, axis=0)
        v_high, v_low = split(values)
        core = product(doubled, jnp.concatenate([v_high, v_low], axis=0), ((1,), (0,)))
        core = core + product(f_low, v_high, ((1,), (0,)))
        c_high, c_low = split(core)
        high_ref[i * R2:(i + 1) * R2, :] = c_high
        low_ref[i * R2:(i + 1) * R2, :] = c_low
    edges = (0, 256, 512, I1)
    for bi in range(3):
        left = slice(edges[bi], edges[bi + 1])
        for bj in range(bi, 3):
            right = slice(edges[bj], edges[bj + 1])
            rows0 = ((0,), (0,))
            gram_ref[left, right] = (
                product(high_ref[:, left], high_ref[:, right], rows0)
                + product(high_ref[:, left], low_ref[:, right], rows0)
                + product(low_ref[:, left], high_ref[:, right], rows0)
            )
    n = 0
    for i in range(FULL):
        for j in range(i, FULL):
            out[n * LANES:(n + 1) * LANES, :] = gram_ref[
                i * LANES:(i + 1) * LANES, j * LANES:(j + 1) * LANES]
            n += 1
    edge = gram_ref[:BODY, BODY:]
    out[n * LANES:(n + 1) * LANES, :] = jnp.concatenate(
        [edge[k * LANES:(k + 1) * LANES] for k in range(4)], axis=1)
    out[64:128, :64] = jnp.concatenate([edge[512:576], edge[576:640]], axis=1)
    out[FULL * LANES + 64:FULL * LANES + 96, :TAIL] = gram_ref[BODY:, BODY:]


def gram_part(parts, factor_rows):
    rows = PAIRS * R2
    return pl.pallas_call(
        gram_kernel,
        in_specs=[VMEM] * (1 + LOCAL2),
        out_specs=VMEM,
        out_shape=jax.ShapeDtypeStruct((16 * LANES, LANES), jnp.float32),
        scratch_shapes=[
            pltpu.VMEM((rows, I1), jnp.bfloat16),
            pltpu.VMEM((rows, I1), jnp.bfloat16),
            pltpu.VMEM((I1, I1), jnp.float32),
        ],
        compiler_params=pltpu.CompilerParams(vmem_limit_bytes=40 << 20),
        name="gram",
    )(factor_rows, *parts)


def add_kernel(x_ref, o_ref):
    devices = x_ref.shape[0]
    total = jnp.sum(x_ref[...], axis=0) * (1.0 / (R2 * R3 * R4))
    o_ref[...] = jnp.broadcast_to(total[None], (devices,) + total.shape)


def add_parts(x):
    return pl.pallas_call(
        add_kernel, in_specs=[VMEM], out_specs=VMEM,
        out_shape=jax.ShapeDtypeStruct(x.shape, jnp.float32),
        compiler_params=pltpu.CompilerParams(vmem_limit_bytes=32 << 20),
        name="add",
    )(x)


def inverse_factor(a):
    n = a.shape[0]
    blocks = n // 8
    rows = [a[8 * i:8 * i + 8, :] for i in range(blocks)]
    lane = lax.broadcasted_iota(jnp.int32, (8, n), 1)
    sub = lax.broadcasted_iota(jnp.int32, (8, n), 0)
    spread = lambda x: jnp.broadcast_to(x, (8, n))
    pivots = []
    for k in range(blocks):
        cols = [[spread(rows[i][:, 8 * k + j:8 * k + j + 1]) for j in range(8)]
                for i in range(k, blocks)]
        inside = (lane >= 8 * k) & (lane < 8 * k + 8)
        rows[k] = jnp.where(inside, jnp.where(lane - 8 * k == sub, 1.0, 0.0), rows[k])
        for i in range(k + 1, blocks):
            rows[i] = jnp.where(inside, 0.0, rows[i])
        pivot = jnp.zeros((8, n), jnp.float32)
        for j in range(8):
            here = cols[0][j]
            pivot = jnp.where(sub == j, here, pivot)
            inverse = 1.0 / spread(here[j:j + 1, :])
            pivot_row = spread(rows[k][j:j + 1, :])
            pivot_cols = {m: spread(cols[0][m][j:j + 1, :]) for m in range(j + 1, 8)}
            for i in range(k, blocks):
                f = cols[i - k][j] * inverse
                if i == k:
                    f = jnp.where(sub > j, f, 0.0)
                rows[i] = rows[i] - f * pivot_row
                for m in range(j + 1, 8):
                    cols[i - k][m] = cols[i - k][m] - f * pivot_cols[m]
        pivots.append(pivot)
    return jnp.concatenate(
        [jnp.where(lane <= sub + 8 * k, rows[k] * lax.rsqrt(pivots[k]), 0.0)
         for k in range(blocks)], axis=0)


def sweep_kernel(packed_ref, start_ref, out_ref, gram_ref, basis_ref):
    n = 0
    row = lax.broadcasted_iota(jnp.int32, (LANES, LANES), 0)
    col = lax.broadcasted_iota(jnp.int32, (LANES, LANES), 1)
    for i in range(FULL):
        for j in range(i, FULL):
            tile = packed_ref[n * LANES:(n + 1) * LANES, :]
            here = slice(i * LANES, (i + 1) * LANES)
            there = slice(j * LANES, (j + 1) * LANES)
            if i == j:
                above = jnp.where(row < col, tile, 0.0)
                gram_ref[here, here] = jnp.where(row <= col, tile, 0.0) + above.T
            else:
                gram_ref[here, there] = tile
                gram_ref[there, here] = tile.T
            n += 1
    last = packed_ref[n * LANES:(n + 1) * LANES, :]
    for k in range(4):
        gram_ref[k * LANES:(k + 1) * LANES, BODY:] = last[:, k * TAIL:(k + 1) * TAIL]
    gram_ref[512:576, BODY:] = packed_ref[64:128, :TAIL]
    gram_ref[576:640, BODY:] = packed_ref[64:128, TAIL:2 * TAIL]
    gram_ref[BODY:, BODY:] = packed_ref[FULL * LANES + 64:FULL * LANES + 96, :TAIL]
    gram_ref[BODY:, :BODY] = gram_ref[:BODY, BODY:].T
    basis_ref[...] = start_ref[...].T

    def sweep(_, carry):
        image = exact(basis_ref[...], gram_ref[...], ((1,), (0,)))
        inner = exact(image, image, ((1,), (1,)))
        basis_ref[...] = exact(inverse_factor(inner), image, ((1,), (0,)))
        return carry

    lax.fori_loop(0, ITERS, sweep, 0)
    out_ref[...] = (basis_ref[...] * math.sqrt(I1)).T


def sweeps(packed, start_basis):
    return pl.pallas_call(
        sweep_kernel, in_specs=[VMEM, VMEM], out_specs=VMEM,
        out_shape=jax.ShapeDtypeStruct((I1, R1), jnp.float32),
        scratch_shapes=[
            pltpu.VMEM((I1, I1), jnp.float32), pltpu.VMEM((R1, I1), jnp.float32)],
        compiler_params=pltpu.CompilerParams(vmem_limit_bytes=32 << 20),
        name="sweeps",
    )(packed, start_basis)


def factors(mode2_factor, mode3_factor, mode4_factor, me):
    turned = jnp.transpose(mode3_factor)
    turned = lax.dynamic_slice_in_dim(
        jnp.concatenate([turned, turned], axis=0), me * RANKS, R3, 0)
    species = mode4_factor.shape[0]
    local = species // NARROW
    blocks = mode4_factor.reshape(NARROW, local, R4)[::-1].reshape(species, R4)
    blocks = lax.dynamic_slice_in_dim(
        jnp.concatenate([blocks, blocks], axis=0), (NARROW - 1 - me) * local, species, 0)
    weights = jnp.transpose(blocks)[:, None, :, None] * jnp.eye(8, dtype=jnp.float32)[None, :, None, :]
    weights = weights.reshape(R4 * 8, species * 8)
    cells = jnp.transpose(mode2_factor.reshape(WIDE, LOCAL2, R2), (2, 1, 0)).reshape(R2, I2)
    return turned, weights, cells


def body(tensor, mode2_factor, mode3_factor, mode4_factor, start_basis):
    me = lax.axis_index("narrow")
    turned, weights, cells = factors(mode2_factor, mode3_factor, mode4_factor, me)
    parts = [None] * LOCAL2
    before = None
    for cell in ORDER:
        blocks = mode3(tensor, turned, cell)
        if before is not None:
            blocks, before = lax.optimization_barrier((blocks, before))
        got = [blocks[0]]
        for j in range(1, NARROW):
            ring = [(i, (i + j) % NARROW) for i in range(NARROW)]
            got.append(lax.ppermute(blocks[j], "narrow", ring))
        before = got[1:]
        sums = species_sum(got, weights)
        sums = lax.all_to_all(sums, "wide", 0, 0, tiled=True)
        parts[cell] = sums.reshape(-1, LANES)
    packed = gram_part(parts, cells)
    everyone = ("wide", "narrow")
    packed = packed.reshape(WIDE * NARROW, -1, LANES)
    packed = add_parts(lax.all_to_all(packed, everyone, 0, 0, tiled=True))
    packed = lax.all_to_all(packed, everyone, 0, 0, tiled=True)
    return sweeps(packed.reshape(-1, LANES), start_basis)


def solution(mesh):
    in_specs = (P("narrow", "wide", None, None), P(), P(), P(), P())
    return jax.shard_map(body, mesh=mesh, in_specs=in_specs, out_specs=P(), check_vma=False)
```

time: 652 us -> 314 us (0.48)
  waiting for transfers between devices: 295 us -> 119 us
  other arithmetic: 141 us -> 1.83 us
  matrix products: 84.2 us -> 0 us
  Pallas kernels: 0 us -> 83.5 us
  starting transfers between devices: 0.04 us -> 55.3 us
  blocking collectives: 64 us -> 24.8 us
  local copies, waits for them, and re-layouts: 49.4 us -> 27.7 us
  between operations: 14.1 us -> 0.16 us
    unnamed x3 -> x0, waiting for transfers between devices: 149 us -> none
    psum x1 -> x0, waiting for transfers between devices: 146 us -> none  [body(): gram_matrix = lax.psum(partial_value, ('wide', 'narrow')) * normalizer]
    another operation x40 -> x0, other arithmetic: 141 us -> none  [the longest x24 76.6 us: orthonormal(): lower_factor = jnp.linalg.cholesky(inner)]
    pallas_call x0 -> x11, Pallas kernels: none -> 83.5 us  [the longest x1 39.5 us: sweeps(): pl.pallas_call(sweep_kernel, in_specs=[VMEM, VMEM], out_specs=VMEM, out_s...]
    ppermute x0 -> x12, waiting for transfers between devices: none -> 82.6 us  [body(): got.append(lax.ppermute(blocks[j], 'narrow', ring))]
    dot_general x20 -> x0, matrix products: 79.9 us -> none  [the longest x1 23.4 us: body(): jnp.einsum('sbka,kr->sbra', tensor, mode3_factor, precision=highest)]
    all_to_all x1, blocking collectives: 64 us -> 24.8 us  [body(): packed = add_parts(lax.all_to_all(packed, everyone, 0, 0, tiled=True))]
    all_to_all x0 -> x5, starting transfers between devices: none -> 37.3 us  [the longest x4 33.7 us: body(): sums = lax.all_to_all(sums, 'wide', 0, 0, tiled=True)]
  transfers between devices with their start and end apart: 2 -> 17, of which waited for: 2 -> 11; matrix products, arithmetic and copies ran while one was open for 0% -> 2% of each run, Pallas kernels for 0% -> 8%
where the time goes in v1:
time: 314 us; the launch traced here: 312 us
  waiting for transfers between devices  119 us (38%)
  Pallas kernels  83.5 us (27%)
  starting transfers between devices  55.3 us (18%)
  local copies, waits for them, and re-layouts  27.7 us (9%)
  blocking collectives  24.8 us (8%)
    ppermute x12, waiting for transfers between devices, body(): got.append(lax.ppermute(blocks[j], 'narrow', ring))  82.6 us
    pallas_call x1, Pallas kernels, sweeps(): pl.pallas_call(sweep_kernel, in_specs=[VMEM, VMEM], out_specs=VMEM, out_s...  39.5 us
    all_to_all x4, starting transfers between devices, body(): sums = lax.all_to_all(sums, 'wide', 0, 0, tiled=True)  33.7 us
    pallas_call x4, Pallas kernels, mode3(): pl.pallas_call(functools.partial(mode3_kernel, tails), grid=(species,), i...  26.4 us
    all_to_all x1, blocking collectives, body(): packed = add_parts(lax.all_to_all(packed, everyone, 0, 0, tiled=True))  24.8 us
    unnamed x12, local copies, waits for them, and re-layouts  23.9 us
    all_to_all x1, waiting for transfers between devices, body(): packed = lax.all_to_all(packed, everyone, 0, 0, tiled=True)  19.7 us
    ppermute x12, starting transfers between devices, body(): got.append(lax.ppermute(blocks[j], 'narrow', ring))  17.9 us
  transfers between devices with their start and end apart: 17, of which 11 were waited for; matrix products, arithmetic and copies ran while one was open for 2% of the time, Pallas kernels for 8%

profile of v1, /device:TPU:1, one launch (start us, length us, event | category | flops | bytes accessed | tf_op | source)
XLA Modules:
  0.0 312.3 jit_solution(6072968728048331329)
XLA Ops:
  0.0 23.6 %copy.31.slab_ref.refs_0_ = f32[8,4,256,672]{3,2,1,0:T(8,128)} copy(f32[8,4,256,672]{2,3,1,0:T(8,128)} %param.5) | data formatting | bytes 44040192 | tf_op args[0]
  23.6 7.0 %mode3.4 = (f32[8,24,640]{2,1,0:T(8,128)S(1)}, f32[8,24,640]{2,1,0:T(8,128)}, f32[8,24,640]{2,1,0:T(8,128)S(1)}, f32[8,24,640]{2,1,0:T(8,128)S(1)}) custom-call(f32[96,256]{1,0:T(8,128)S(1)} %fusion.factor_ref, f32[8,4,256,672]{3,2,1,0:T(8,128)} %copy.31.slab_ref.refs_0_), custom_call_target="tpu_custom_call" | custom-call | flops 754974720 | bytes 7208960 | tf_op jit(solution)/shard_map/mode3/pallas_call | solution.py:85
  30.6 2.0 collective-permute-start
  32.7 2.4 collective-permute-start.1
  38.2 2.8 mul.27.weights_ref
  41.0 3.6 %collective-permute-done.refs_1_ = f32[8,24,640]{2,1,0:T(8,128)S(1)} collective-permute-done((f32[8,24,640]{2,1,0:T(8,128)}, f32[8,24,640]{2,1,0:T(8,128)S(1)}, u32[]{:S(2)}, u32[]{:S(2)}) %collective-permute-start) | collective-permute-done | bytes 491552 | tf_op jit(solution)/shard_map/ppermute | solution.py:332
  44.6 11.8 %collective-permute-done.1.refs_2_ = f32[8,24,640]{2,1,0:T(8,128)S(1)} collective-permute-done((f32[8,24,640]{2,1,0:T(8,128)S(1)}, f32[8,24,640]{2,1,0:T(8,128)S(1)}, u32[]{:S(2)}, u32[]{:S(2)}) %collective-permute-start.1) | collective-permute-done | bytes 491552 | tf_op jit(solution)/shard_map/ppermute | solution.py:332
  56.5 2.3 species.4
  58.8 9.6 %all-to-all-start = ((f32[32,64,128]{2,1,0:T(8,128)}), f32[32,64,128]{2,1,0:T(8,128)S(1)}, u32[]{:S(2)}, u32[]{:S(2)}) async-start(f32[32,64,128]{2,1,0:T(8,128)} %species.4), calls=%async_computation | async-start | bytes 2097152 | tf_op jit(solution)/shard_map/all_to_all | solution.py:335
  68.4 7.2 %mode3.6 = (f32[8,24,768]{2,1,0:T(8,128)S(1)}, f32[8,24,768]{2,1,0:T(8,128)S(1)}, f32[8,24,768]{2,1,0:T(8,128)S(1)}, f32[8,24,768]{2,1,0:T(8,128)S(1)}) custom-call(f32[96,256]{1,0:T(8,128)S(1)} %fusion.factor_ref, f32[8,4,256,672]{3,2,1,0:T(8,128)} %copy.31.slab_ref.refs_0_, f32[8,4,256,672]{3,2,1,0:T(8,128)} %copy.31.slab_ref.refs_0_), custom_call_target="tpu_custom_call" | custom-call | flops 905969664 | bytes 8650752 | tf_op jit(solution)/shard_map/mode3/pallas_call | solution.py:85
  76.6 2.1 collective-permute-start.4
  80.0 11.7 %collective-permute-done.3.refs_1_ = f32[8,24,768]{2,1,0:T(8,128)S(1)} collective-permute-done((f32[8,24,768]{2,1,0:T(8,128)S(1)}, f32[8,24,768]{2,1,0:T(8,128)S(1)}, u32[]{:S(2)}, u32[]{:S(2)}) %collective-permute-start.3) | collective-permute-done | bytes 589856 | tf_op jit(solution)/shard_map/ppermute | solution.py:332
  91.6 12.9 %collective-permute-done.4.refs_2_ = f32[8,24,768]{2,1,0:T(8,128)S(1)} collective-permute-done((f32[8,24,768]{2,1,0:T(8,128)S(1)}, f32[8,24,768]{2,1,0:T(8,128)S(1)}, u32[]{:S(2)}, u32[]{:S(2)}) %collective-permute-start.4) | collective-permute-done | bytes 589856 | tf_op jit(solution)/shard_map/ppermute | solution.py:332
  104.6 2.4 species.7
  107.0 8.4 %all-to-all-start.3 = ((f32[32,72,128]{2,1,0:T(8,128)}), f32[32,72,128]{2,1,0:T(8,128)S(1)}, u32[]{:S(2)}, u32[]{:S(2)}) async-start(f32[32,72,128]{2,1,0:T(8,128)} %species.7), calls=%async_computation.3 | async-start | bytes 2359296 | tf_op jit(solution)/shard_map/all_to_all | solution.py:335
  115.4 6.1 %mode3.5 = (f32[8,24,640]{2,1,0:T(8,128)S(1)}, f32[8,24,640]{2,1,0:T(8,128)S(1)}, f32[8,24,640]{2,1,0:T(8,128)S(1)}, f32[8,24,640]{2,1,0:T(8,128)S(1)}) custom-call(f32[96,256]{1,0:T(8,128)S(1)} %fusion.factor_ref, f32[8,4,256,672]{3,2,1,0:T(8,128)} %copy.31.slab_ref.refs_0_), custom_call_target="tpu_custom_call" | custom-call | flops 754974720 | bytes 7208960 | tf_op jit(solution)/shard_map/mode3/pallas_call | solution.py:85
  123.0 2.1 collective-permute-start.7
  125.8 9.6 %collective-permute-done.6.refs_1_ = f32[8,24,640]{2,1,0:T(8,128)S(1)} collective-permute-done((f32[8,24,640]{2,1,0:T(8,128)S(1)}, f32[8,24,640]{2,1,0:T(8,128)S(1)}, u32[]{:S(2)}, u32[]{:S(2)}) %collective-permute-start.6) | collective-permute-done | bytes 491552 | tf_op jit(solution)/shard_map/ppermute | solution.py:332
  135.4 11.4 %collective-permute-done.7.refs_2_ = f32[8,24,640]{2,1,0:T(8,128)S(1)} collective-permute-done((f32[8,24,640]{2,1,0:T(8,128)S(1)}, f32[8,24,640]{2,1,0:T(8,128)S(1)}, u32[]{:S(2)}, u32[]{:S(2)}) %collective-permute-start.7) | collective-permute-done | bytes 491552 | tf_op jit(solution)/shard_map/ppermute | solution.py:332
  146.8 2.3 species.5
  149.1 8.1 %all-to-all-start.1 = ((f32[32,64,128]{2,1,0:T(8,128)}), f32[32,64,128]{2,1,0:T(8,128)S(1)}, u32[]{:S(2)}, u32[]{:S(2)}) async-start(f32[32,64,128]{2,1,0:T(8,128)} %species.5), calls=%async_computation.1 | async-start | bytes 2097152 | tf_op jit(solution)/shard_map/all_to_all | solution.py:335
  157.2 6.1 %mode3.7 = (f32[8,24,640]{2,1,0:T(8,128)S(1)}, f32[8,24,640]{2,1,0:T(8,128)S(1)}, f32[8,24,640]{2,1,0:T(8,128)S(1)}, f32[8,24,640]{2,1,0:T(8,128)S(1)}) custom-call(f32[96,256]{1,0:T(8,128)S(1)} %fusion.factor_ref, f32[8,4,256,672]{3,2,1,0:T(8,128)} %copy.31.slab_ref.refs_0_), custom_call_target="tpu_custom_call" | custom-call | flops 754974720 | bytes 7208960 | tf_op jit(solution)/shard_map/mode3/pallas_call | solution.py:85
  166.9 10.6 %collective-permute-done.10.refs_2_ = f32[8,24,640]{2,1,0:T(8,128)S(1)} collective-permute-done((f32[8,24,640]{2,1,0:T(8,128)S(1)}, f32[8,24,640]{2,1,0:T(8,128)S(1)}, u32[]{:S(2)}, u32[]{:S(2)}) %collective-permute-start.10) | collective-permute-done | bytes 491552 | tf_op jit(solution)/shard_map/ppermute | solution.py:332
  177.5 10.2 %collective-permute-done.11.refs_3_ = f32[8,24,640]{2,1,0:T(8,128)S(1)} collective-permute-done((f32[8,24,640]{2,1,0:T(8,128)S(1)}, f32[8,24,640]{2,1,0:T(8,128)S(1)}, u32[]{:S(2)}, u32[]{:S(2)}) %collective-permute-start.11) | collective-permute-done | bytes 491552 | tf_op jit(solution)/shard_map/ppermute | solution.py:332
  188.5 2.3 species.6
  190.8 7.6 %all-to-all-start.2 = ((f32[32,64,128]{2,1,0:T(8,128)}), f32[32,64,128]{2,1,0:T(8,128)}, u32[]{:S(2)}, u32[]{:S(2)}) async-start(f32[32,64,128]{2,1,0:T(8,128)} %species.6), calls=%async_computation.2 | async-start | bytes 2097152 | tf_op jit(solution)/shard_map/all_to_all | solution.py:335
  198.6 16.7 %all-to-all-done.2 = f32[32,64,128]{2,1,0:T(8,128)} async-done(((f32[32,64,128]{2,1,0:T(8,128)}), f32[32,64,128]{2,1,0:T(8,128)}, u32[]{:S(2)}, u32[]{:S(2)}) %all-to-all-start.2) | async-done | bytes 1048608 | tf_op jit(solution)/shard_map/all_to_all | solution.py:335
  215.4 7.1 %gram.1 = f32[2048,128]{1,0:T(8,128)S(1)} custom-call(f32[96,128]{1,0:T(8,128)S(1)} %copy.36.factor_ref, f32[2048,128]{1,0:T(8,128)S(1)} %bitcast.20, f32[2048,128]{1,0:T(8,128)S(1)} %bitcast.21, f32[2048,128]{1,0:T(8,128)} %bitcast.9.refs_2_, f32[2304,128]{1,0:T(8,128)S(1)} %bitcast.18), custom_call_target="tpu_custom_call" | custom-call | tf_op jit(solution)/shard_map/gram/pallas_call | solution.py:194
  222.4 24.8 %all_to_all.30.x_ref = f32[128,16,128]{2,1,0:T(8,128)S(1)} all-to-all(f32[128,16,128]{2,1,0:T(8,128)S(1)} %bitcast.22), channel_id=1, replica_groups=mesh['wide'=32,'narrow'=4] {'wide','narrow'}, dimensions={0} | all-to-all | bytes 2097152 | tf_op jit(solution)/shard_map/all_to_all | solution.py:340
  248.4 3.7 %all-to-all-start.5 = ((f32[128,16,128]{2,1,0:T(8,128)}), f32[128,16,128]{2,1,0:T(8,128)S(1)}, u32[]{:S(2)}, u32[]{:S(2)}) async-start(f32[128,16,128]{2,1,0:T(8,128)} %add.9), calls=%async_computation.5 | async-start | bytes 2097152 | tf_op jit(solution)/shard_map/all_to_all | solution.py:341
  252.2 19.7 %all-to-all-done.5 = f32[128,16,128]{2,1,0:T(8,128)S(1)} async-done(((f32[128,16,128]{2,1,0:T(8,128)}), f32[128,16,128]{2,1,0:T(8,128)S(1)}, u32[]{:S(2)}, u32[]{:S(2)}) %all-to-all-start.5) | async-done | bytes 1048608 | tf_op jit(solution)/shard_map/all_to_all | solution.py:341
  271.9 39.5 %sweeps.1 = f32[672,96]{1,0:T(8,128)S(1)} custom-call(f32[2048,128]{1,0:T(8,128)S(1)} %bitcast.19, f32[672,96]{1,0:T(8,128)S(1)} %copy.37.start_ref), custom_call_target="tpu_custom_call" | custom-call | tf_op jit(solution)/shard_map/sweeps/pallas_call | solution.py:295
  (36 shorter events, 14.5 us)
Async XLA Ops:
  0.0 23.6 %copy-start.1 = (f32[256,96]{0,1:T(8,128)S(1)}, f32[256,96]{0,1:T(8,128)}, u32[]{:S(2)}) copy-start(f32[256,96]{0,1:T(8,128)} %param.7) | copy-start | bytes 294916
  23.6 12.7 %copy-start.3 = (f32[32,16]{0,1:T(8,128)S(1)}, f32[32,16]{0,1:T(8,128)}, u32[]{:S(2)}) copy-start(f32[32,16]{0,1:T(8,128)} %param.8) | copy-start | bytes 6148
  30.6 14.0 %collective-permute-start = (f32[8,24,640]{2,1,0:T(8,128)}, f32[8,24,640]{2,1,0:T(8,128)S(1)}, u32[]{:S(2)}, u32[]{:S(2)}) collective-permute-start(f32[8,24,640]{2,1,0:T(8,128)} %get-tuple-element.34), channel_id=1, source_target_pairs={{0,1},{1,2},{2,3},{3,0},{4,5},{5,6},{6,7},{7,4},{8,9},{9,10},{10,1... | collective-permute-start | bytes 1474568 | tf_op jit(solution)/shard_map/ppermute | solution.py:332
  32.7 23.8 %collective-permute-start.1 = (f32[8,24,640]{2,1,0:T(8,128)S(1)}, f32[8,24,640]{2,1,0:T(8,128)S(1)}, u32[]{:S(2)}, u32[]{:S(2)}) collective-permute-start(f32[8,24,640]{2,1,0:T(8,128)S(1)} %get-tuple-element.35), channel_id=1, source_target_pairs={{0,2},{1,3},{2,0},{3,1},{4,6},{5,7},{6,4},{7,5},{8,10},{9,11},{10,... | collective-permute-start | bytes 1474568 | tf_op jit(solution)/shard_map/ppermute | solution.py:332
  35.1 21.4 %collective-permute-start.2 = (f32[8,24,640]{2,1,0:T(8,128)S(1)}, f32[8,24,640]{2,1,0:T(8,128)S(1)}, u32[]{:S(2)}, u32[]{:S(2)}) collective-permute-start(f32[8,24,640]{2,1,0:T(8,128)S(1)} %get-tuple-element.36), channel_id=1, source_target_pairs={{0,3},{1,0},{2,1},{3,2},{4,7},{5,4},{6,5},{7,6},{8,11},{9,8},{10,9... | collective-permute-start | bytes 1474568 | tf_op jit(solution)/shard_map/ppermute | solution.py:332
  58.8 48.3 %all-to-all-start = ((f32[32,64,128]{2,1,0:T(8,128)}), f32[32,64,128]{2,1,0:T(8,128)S(1)}, u32[]{:S(2)}, u32[]{:S(2)}) async-start(f32[32,64,128]{2,1,0:T(8,128)} %species.4), calls=%async_computation | async-start | bytes 2097152 | tf_op jit(solution)/shard_map/all_to_all | solution.py:335
  75.7 16.0 %collective-permute-start.3 = (f32[8,24,768]{2,1,0:T(8,128)S(1)}, f32[8,24,768]{2,1,0:T(8,128)S(1)}, u32[]{:S(2)}, u32[]{:S(2)}) collective-permute-start(f32[8,24,768]{2,1,0:T(8,128)S(1)} %get-tuple-element.45), channel_id=1, source_target_pairs={{0,1},{1,2},{2,3},{3,0},{4,5},{5,6},{6,7},{7,4},{8,9},{9,10},{10,1... | collective-permute-start | bytes 1769480 | tf_op jit(solution)/shard_map/ppermute | solution.py:332
  76.6 28.0 %collective-permute-start.4 = (f32[8,24,768]{2,1,0:T(8,128)S(1)}, f32[8,24,768]{2,1,0:T(8,128)S(1)}, u32[]{:S(2)}, u32[]{:S(2)}) collective-permute-start(f32[8,24,768]{2,1,0:T(8,128)S(1)} %get-tuple-element.46), channel_id=1, source_target_pairs={{0,2},{1,3},{2,0},{3,1},{4,6},{5,7},{6,4},{7,5},{8,10},{9,11},{10,... | collective-permute-start | bytes 1769480 | tf_op jit(solution)/shard_map/ppermute | solution.py:332
  78.7 25.9 %collective-permute-start.5 = (f32[8,24,768]{2,1,0:T(8,128)S(1)}, f32[8,24,768]{2,1,0:T(8,128)S(1)}, u32[]{:S(2)}, u32[]{:S(2)}) collective-permute-start(f32[8,24,768]{2,1,0:T(8,128)S(1)} %get-tuple-element.47), channel_id=1, source_target_pairs={{0,3},{1,0},{2,1},{3,2},{4,7},{5,4},{6,5},{7,6},{8,11},{9,8},{10,9... | collective-permute-start | bytes 1769480 | tf_op jit(solution)/shard_map/ppermute | solution.py:332
  107.0 42.0 %all-to-all-start.3 = ((f32[32,72,128]{2,1,0:T(8,128)}), f32[32,72,128]{2,1,0:T(8,128)S(1)}, u32[]{:S(2)}, u32[]{:S(2)}) async-start(f32[32,72,128]{2,1,0:T(8,128)} %species.7), calls=%async_computation.3 | async-start | bytes 2359296 | tf_op jit(solution)/shard_map/all_to_all | solution.py:335
  121.5 13.9 %collective-permute-start.6 = (f32[8,24,640]{2,1,0:T(8,128)S(1)}, f32[8,24,640]{2,1,0:T(8,128)S(1)}, u32[]{:S(2)}, u32[]{:S(2)}) collective-permute-start(f32[8,24,640]{2,1,0:T(8,128)S(1)} %get-tuple-element.49), channel_id=1, source_target_pairs={{0,1},{1,2},{2,3},{3,0},{4,5},{5,6},{6,7},{7,4},{8,9},{9,10},{10,1... | collective-permute-start | bytes 1474568 | tf_op jit(solution)/shard_map/ppermute | solution.py:332
  123.0 23.8 %collective-permute-start.7 = (f32[8,24,640]{2,1,0:T(8,128)S(1)}, f32[8,24,640]{2,1,0:T(8,128)S(1)}, u32[]{:S(2)}, u32[]{:S(2)}) collective-permute-start(f32[8,24,640]{2,1,0:T(8,128)S(1)} %get-tuple-element.50), channel_id=1, source_target_pairs={{0,2},{1,3},{2,0},{3,1},{4,6},{5,7},{6,4},{7,5},{8,10},{9,11},{10,... | collective-permute-start | bytes 1474568 | tf_op jit(solution)/shard_map/ppermute | solution.py:332
  125.1 21.7 %collective-permute-start.8 = (f32[8,24,640]{2,1,0:T(8,128)S(1)}, f32[8,24,640]{2,1,0:T(8,128)S(1)}, u32[]{:S(2)}, u32[]{:S(2)}) collective-permute-start(f32[8,24,640]{2,1,0:T(8,128)S(1)} %get-tuple-element.51), channel_id=1, source_target_pairs={{0,3},{1,0},{2,1},{3,2},{4,7},{5,4},{6,5},{7,6},{8,11},{9,8},{10,9... | collective-permute-start | bytes 1474568 | tf_op jit(solution)/shard_map/ppermute | solution.py:332
  149.1 41.7 %all-to-all-start.1 = ((f32[32,64,128]{2,1,0:T(8,128)}), f32[32,64,128]{2,1,0:T(8,128)S(1)}, u32[]{:S(2)}, u32[]{:S(2)}) async-start(f32[32,64,128]{2,1,0:T(8,128)} %species.5), calls=%async_computation.1 | async-start | bytes 2097152 | tf_op jit(solution)/shard_map/all_to_all | solution.py:335
  163.2 35.2 %copy-start.2 = (f32[128,96]{0,1:T(8,128)S(1)}, f32[128,96]{0,1:T(8,128)}, u32[]{:S(2)}) copy-start(f32[128,96]{0,1:T(8,128)} %param.6) | copy-start | bytes 147460
  163.2 14.2 %collective-permute-start.10 = (f32[8,24,640]{2,1,0:T(8,128)S(1)}, f32[8,24,640]{2,1,0:T(8,128)S(1)}, u32[]{:S(2)}, u32[]{:S(2)}) collective-permute-start(f32[8,24,640]{2,1,0:T(8,128)S(1)} %get-tuple-element.58), channel_id=1, source_target_pairs={{0,2},{1,3},{2,0},{3,1},{4,6},{5,7},{6,4},{7,5},{8,10},{9,11},{10,... | collective-permute-start | bytes 1474568 | tf_op jit(solution)/shard_map/ppermute | solution.py:332
  165.2 22.4 %collective-permute-start.11 = (f32[8,24,640]{2,1,0:T(8,128)S(1)}, f32[8,24,640]{2,1,0:T(8,128)S(1)}, u32[]{:S(2)}, u32[]{:S(2)}) collective-permute-start(f32[8,24,640]{2,1,0:T(8,128)S(1)} %get-tuple-element.59), channel_id=1, source_target_pairs={{0,3},{1,0},{2,1},{3,2},{4,7},{5,4},{6,5},{7,6},{8,11},{9,8},{10,9... | collective-permute-start | bytes 1474568 | tf_op jit(solution)/shard_map/ppermute | solution.py:332
  166.9 21.6 %collective-permute-start.9 = (f32[8,24,640]{2,1,0:T(8,128)S(1)}, f32[8,24,640]{2,1,0:T(8,128)S(1)}, u32[]{:S(2)}, u32[]{:S(2)}) collective-permute-start(f32[8,24,640]{2,1,0:T(8,128)S(1)} %get-tuple-element.57), channel_id=1, source_target_pairs={{0,1},{1,2},{2,3},{3,0},{4,5},{5,6},{6,7},{7,4},{8,9},{9,10},{10,1... | collective-permute-start | bytes 1474568 | tf_op jit(solution)/shard_map/ppermute | solution.py:332
  190.8 24.5 %all-to-all-start.2 = ((f32[32,64,128]{2,1,0:T(8,128)}), f32[32,64,128]{2,1,0:T(8,128)}, u32[]{:S(2)}, u32[]{:S(2)}) async-start(f32[32,64,128]{2,1,0:T(8,128)} %species.6), calls=%async_computation.2 | async-start | bytes 2097152 | tf_op jit(solution)/shard_map/all_to_all | solution.py:335
  247.2 4.9 %copy-start = (f32[672,96]{0,1:T(8,128)S(1)}, f32[672,96]{0,1:T(8,128)}, u32[]{:S(2)}) copy-start(f32[672,96]{0,1:T(8,128)} %param.9) | copy-start | bytes 774148
  248.4 23.6 %all-to-all-start.5 = ((f32[128,16,128]{2,1,0:T(8,128)}), f32[128,16,128]{2,1,0:T(8,128)S(1)}, u32[]{:S(2)}, u32[]{:S(2)}) async-start(f32[128,16,128]{2,1,0:T(8,128)} %add.9), calls=%async_computation.5 | async-start | bytes 2097152 | tf_op jit(solution)/shard_map/all_to_all | solution.py:341

commit v2 on v1

v2 whole, which is shorter than its diff:
```python
import functools
import math

import jax
import jax.numpy as jnp
from jax import lax
from jax.experimental import pallas as pl
from jax.experimental.pallas import tpu as pltpu
from jax.sharding import PartitionSpec as P

I1 = 672
I2 = 128
I3 = 256
R1 = 96
R2 = 96
R3 = 96
R4 = 16
ITERS = 8
NARROW = 4
WIDE = 32
LANES = 128
FULL = I1 // LANES
TAIL = I1 - FULL * LANES
BODY = FULL * LANES
LOCAL2 = I2 // WIDE
RANKS = R3 // NARROW
PAIRS = RANKS * R4 // WIDE
CHUNKS = ((0, 1), (2, 3), (4,))
FIRST = FULL - 1
SPECIES_COST = 10 ** 11
VMEM = pl.BlockSpec(memory_space=pltpu.VMEM)


def whole(x):
    return pl.BlockSpec(x.shape, lambda i: (0,) * len(x.shape))


def split(x):
    high = x.astype(jnp.bfloat16)
    return high, (x - high.astype(jnp.float32)).astype(jnp.bfloat16)


def product(a, b, contract):
    return lax.dot_general(
        a, b, ((contract), ((), ())), preferred_element_type=jnp.float32
    )


def exact(a, b, contract):
    return lax.dot_general(
        a, b, ((contract), ((), ())),
        preferred_element_type=jnp.float32, precision=lax.Precision.HIGHEST,
    )


def left_product(weights, values):
    rows = weights.shape[0]
    w_high, w_low = split(weights)
    v_high, v_low = split(values)
    both = product(jnp.concatenate([w_high, w_low], axis=0), v_high, ((1,), (0,)))
    return both[:rows] + both[rows:] + product(w_high, v_low, ((1,), (0,)))


def mode3_kernel(factor_ref, *refs):
    outs, slabs = refs[-NARROW:], refs[:-NARROW]
    f_high, f_low = split(factor_ref[...])
    lanes = ((1,), (1,))
    for s in range(outs[0].shape[0]):
        rows = [slab[s].reshape(-1, I3) for slab in slabs]
        rows = rows[0] if len(rows) == 1 else jnp.concatenate(rows, axis=0)
        r_high, r_low = split(rows)
        both = product(jnp.concatenate([f_high, f_low], axis=0), r_high, lanes)
        done = both[:R3] + both[R3:] + product(f_high, r_low, lanes)
        for j, out in enumerate(outs):
            out[s] = done[j * RANKS:(j + 1) * RANKS]


def mode3(field, factor_rows, chunk):
    species = field.shape[0]
    count = len(chunk)
    index = chunk[0] // count
    width = LOCAL2 * LANES * count
    some = species // 2 // count
    in_specs = [
        pl.BlockSpec((R3, I3), lambda s: (0, 0)),
        pl.BlockSpec((some, LOCAL2, LANES * count, I3), lambda s: (s, 0, index, 0)),
    ]
    args = [factor_rows, field]
    if chunk == CHUNKS[-1]:
        width += LANES
        in_specs.append(pl.BlockSpec((some, LOCAL2, TAIL, I3), lambda s: (s, 0, BODY // TAIL, 0)))
        args.append(field)
    shape = jax.ShapeDtypeStruct((species, RANKS, width), jnp.float32)
    return pl.pallas_call(
        mode3_kernel,
        grid=(species // some,),
        in_specs=in_specs,
        out_specs=[pl.BlockSpec((some, RANKS, width), lambda s: (s, 0, 0))] * NARROW,
        out_shape=[shape] * NARROW,
        compiler_params=pltpu.CompilerParams(vmem_limit_bytes=48 << 20),
        cost_estimate=pl.CostEstimate(
            flops=6 * species * R3 * I3 * width,
            bytes_accessed=4 * species * width * (I3 + R3), transcendentals=0),
        name="mode3",
    )(*args)


def species_kernel(tiles, weights_ref, *refs):
    parts, out = refs[:NARROW], refs[NARROW]
    step = pl.program_id(0)
    rows = [p[...].reshape(-1, tiles * LANES) for p in parts]
    done = left_product(weights_ref[...], jnp.concatenate(rows, axis=0))

    def put(dest, first, q, start, count):
        for t in range(tiles):
            out[dest, t * PAIRS + first:t * PAIRS + first + count, :] = done[
                q * 8 + start:q * 8 + start + count, t * LANES:(t + 1) * LANES]

    @pl.when(step == 0)
    def _():
        spare = out.shape[1] - tiles * PAIRS
        if spare:
            out[:, tiles * PAIRS:, :] = jnp.zeros((WIDE, spare, LANES), jnp.float32)
        for q in range(R4):
            put(2 * q, 0, q, 0, 8)

    @pl.when(step == 1)
    def _():
        for q in range(R4):
            put(2 * q, 8, q, 0, 4)
            put(2 * q + 1, 0, q, 4, 4)

    @pl.when(step == 2)
    def _():
        for q in range(R4):
            put(2 * q + 1, 4, q, 0, 8)


def species_sum(parts, weights):
    species, ranks, width = parts[0].shape
    tiles = width // LANES
    rows = -(-tiles * PAIRS // 8) * 8
    return pl.pallas_call(
        functools.partial(species_kernel, tiles),
        grid=(ranks // 8,),
        in_specs=[pl.BlockSpec(weights.shape, lambda i: (0, 0))]
        + [pl.BlockSpec((species, 8, width), lambda i: (0, i, 0))] * NARROW,
        out_specs=pl.BlockSpec((WIDE, rows, LANES), lambda i: (0, 0, 0)),
        out_shape=jax.ShapeDtypeStruct((WIDE, rows, LANES), jnp.float32),
        compiler_params=pltpu.CompilerParams(vmem_limit_bytes=20 << 20),
        cost_estimate=pl.CostEstimate(
            flops=SPECIES_COST, bytes_accessed=4 * width * 24 * 48, transcendentals=0),
        name="species",
    )(weights, *parts)


def core_columns(factor, parts, last, store):
    f_high, f_low = split(factor)
    doubled = jnp.concatenate([f_high, f_high], axis=1)
    strides = [p.shape[0] // WIDE for p in parts]
    counts = [len(tiles) for tiles in (CHUNKS[-1:] if last else CHUNKS[:-1])]

    def piece(p, place):
        return parts[p][pl.ds(place, WIDE, stride=strides[p]), :]

    for i in range(PAIRS):
        cells = []
        if last:
            tail = piece(0, LOCAL2 * counts[0] * PAIRS + i)
        for b in range(LOCAL2):
            row = [piece(p, (b * n + t) * PAIRS + i) for p, n in enumerate(counts) for t in range(n)]
            if last:
                row.append(tail[:, b * TAIL:(b + 1) * TAIL])
            cells.append(jnp.concatenate(row, axis=1))
        v_high, v_low = split(jnp.concatenate(cells, axis=0))
        core = product(doubled, jnp.concatenate([v_high, v_low], axis=0), ((1,), (0,)))
        store(i, *split(core + product(f_low, v_high, ((1,), (0,)))))


def inner_product(a_high, a_low, b_high, b_low):
    rows = ((0,), (0,))
    return product(a_high, b_high, rows) + product(a_high, b_low, rows) + product(a_low, b_high, rows)


def gram_first_kernel(factor_ref, *refs):
    parts, (out, core_ref) = refs[:-2], refs[-2:]
    half = PAIRS * R2

    def store(i, high, low):
        core_ref[i * R2:(i + 1) * R2, :] = high
        core_ref[half + i * R2:half + (i + 1) * R2, :] = low

    core_columns(factor_ref[...], parts, False, store)
    place = 0
    for i in range(FIRST):
        left = slice(i * LANES, (i + 1) * LANES)
        right = slice(i * LANES, FIRST * LANES)
        block = inner_product(core_ref[:half, left], core_ref[half:, left],
                              core_ref[:half, right], core_ref[half:, right])
        for j in range(FIRST - i):
            out[place:place + LANES, :] = block[:, j * LANES:(j + 1) * LANES]
            place += LANES


def gram_last_kernel(factor_ref, part_ref, core_ref, tiles_ref, out, high_ref, low_ref):
    half = PAIRS * R2

    def store(i, high, low):
        high_ref[i * R2:(i + 1) * R2, :] = high
        low_ref[i * R2:(i + 1) * R2, :] = low

    core_columns(factor_ref[...], [part_ref], True, store)
    place = tiles_ref.shape[0]
    out[:place, :] = tiles_ref[...]
    high, low = high_ref[...], low_ref[...]
    above = inner_product(core_ref[:half, :], core_ref[half:, :], high, low)
    own = inner_product(high, low, high, low)
    out[place:place + FIRST * LANES, :] = above[:, :LANES]
    place += FIRST * LANES
    out[place:place + LANES, :] = own[:LANES, :LANES]
    edge = own[:LANES, LANES:]
    out[place + 64:place + LANES, :64] = jnp.concatenate([edge[:64], edge[64:]], axis=1)
    out[64:96, :TAIL] = own[LANES:, LANES:]
    place += LANES
    out[place:place + LANES, :] = jnp.concatenate(
        [above[i * LANES:(i + 1) * LANES, LANES:] for i in range(FIRST)], axis=1)


def gram_call(kernel, args, out_shape, scratch, flops):
    some = isinstance(out_shape, list)
    return pl.pallas_call(
        kernel, grid=(1,), in_specs=[whole(x) for x in args],
        out_specs=[whole(x) for x in out_shape] if some else whole(out_shape),
        out_shape=out_shape, scratch_shapes=scratch,
        compiler_params=pltpu.CompilerParams(vmem_limit_bytes=48 << 20),
        cost_estimate=pl.CostEstimate(flops=flops, bytes_accessed=8 << 20, transcendentals=0),
        name="gram",
    )(*args)


def gram_first(parts, factor_rows):
    rows = PAIRS * R2
    columns = FIRST * LANES
    tiles = FIRST * (FIRST + 1) // 2
    return gram_call(
        gram_first_kernel, [factor_rows, *parts],
        [jax.ShapeDtypeStruct((tiles * LANES, LANES), jnp.float32),
         jax.ShapeDtypeStruct((2 * rows, columns), jnp.bfloat16)],
        [], 4 * rows * columns * columns)


def gram_last(part, core, tiles, factor_rows):
    half = pltpu.VMEM((PAIRS * R2, LANES + TAIL), jnp.bfloat16)
    return gram_call(
        gram_last_kernel, [factor_rows, part, core, tiles],
        jax.ShapeDtypeStruct((16 * LANES, LANES), jnp.float32),
        [half, half], 6 * PAIRS * R2 * I1 * (LANES + TAIL))


def add_kernel(x_ref, o_ref):
    devices = x_ref.shape[0]
    total = jnp.sum(x_ref[...], axis=0) * (1.0 / (R2 * R3 * R4))
    o_ref[...] = jnp.broadcast_to(total[None], (devices,) + total.shape)


def add_parts(x):
    return pl.pallas_call(
        add_kernel, in_specs=[VMEM], out_specs=VMEM,
        out_shape=jax.ShapeDtypeStruct(x.shape, jnp.float32),
        compiler_params=pltpu.CompilerParams(vmem_limit_bytes=20 << 20),
        name="add",
    )(x)


def inverse_factor(a):
    n = a.shape[0]
    blocks = n // 8
    rows = [a[8 * i:8 * i + 8, :] for i in range(blocks)]
    lane = lax.broadcasted_iota(jnp.int32, (8, n), 1)
    sub = lax.broadcasted_iota(jnp.int32, (8, n), 0)
    spread = lambda x: jnp.broadcast_to(x, (8, n))
    pivots = []
    for k in range(blocks):
        cols = [[spread(rows[i][:, 8 * k + j:8 * k + j + 1]) for j in range(8)]
                for i in range(k, blocks)]
        inside = (lane >= 8 * k) & (lane < 8 * k + 8)
        rows[k] = jnp.where(inside, jnp.where(lane - 8 * k == sub, 1.0, 0.0), rows[k])
        for i in range(k + 1, blocks):
            rows[i] = jnp.where(inside, 0.0, rows[i])
        pivot = jnp.zeros((8, n), jnp.float32)
        for j in range(8):
            here = cols[0][j]
            pivot = jnp.where(sub == j, here, pivot)
            inverse = 1.0 / spread(here[j:j + 1, :])
            pivot_row = spread(rows[k][j:j + 1, :])
            pivot_cols = {m: spread(cols[0][m][j:j + 1, :]) for m in range(j + 1, 8)}
            for i in range(k, blocks):
                f = cols[i - k][j] * inverse
                if i == k:
                    f = jnp.where(sub > j, f, 0.0)
                rows[i] = rows[i] - f * pivot_row
                for m in range(j + 1, 8):
                    cols[i - k][m] = cols[i - k][m] - f * pivot_cols[m]
        pivots.append(pivot)
    return jnp.concatenate(
        [jnp.where(lane <= sub + 8 * k, rows[k] * lax.rsqrt(pivots[k]), 0.0)
         for k in range(blocks)], axis=0)


def sweep_kernel(packed_ref, start_ref, out_ref, gram_ref):
    row = lax.broadcasted_iota(jnp.int32, (LANES, LANES), 0)
    col = lax.broadcasted_iota(jnp.int32, (LANES, LANES), 1)
    place = 0
    pairs = [(i, j) for i in range(FIRST) for j in range(i, FIRST)]
    pairs += [(i, FIRST) for i in range(FIRST + 1)]
    for i, j in pairs:
        tile = packed_ref[place:place + LANES, :]
        here = slice(i * LANES, (i + 1) * LANES)
        there = slice(j * LANES, (j + 1) * LANES)
        if i == j:
            above = jnp.where(row < col, tile, 0.0)
            gram_ref[here, here] = jnp.where(row <= col, tile, 0.0) + above.T
        else:
            gram_ref[here, there] = tile
            gram_ref[there, here] = tile.T
        place += LANES
    last = packed_ref[place:place + LANES, :]
    for k in range(FIRST):
        gram_ref[k * LANES:(k + 1) * LANES, BODY:] = last[:, k * TAIL:(k + 1) * TAIL]
    gram_ref[512:576, BODY:] = packed_ref[place - 64:place, :TAIL]
    gram_ref[576:640, BODY:] = packed_ref[place - 64:place, TAIL:2 * TAIL]
    gram_ref[BODY:, BODY:] = packed_ref[64:96, :TAIL]
    gram_ref[BODY:, :BODY] = gram_ref[:BODY, BODY:].T
    out_ref[...] = start_ref[...]

    def sweep(_, carry):
        image = exact(out_ref[...], gram_ref[...], ((1,), (0,)))
        inner = exact(image, image, ((1,), (1,)))
        out_ref[...] = exact(inverse_factor(inner), image, ((1,), (0,)))
        return carry

    lax.fori_loop(0, ITERS, sweep, 0)
    out_ref[...] = out_ref[...] * math.sqrt(I1)


def sweeps(packed, start_rows):
    return pl.pallas_call(
        sweep_kernel, in_specs=[VMEM, VMEM], out_specs=VMEM,
        out_shape=jax.ShapeDtypeStruct((R1, I1), jnp.float32),
        scratch_shapes=[pltpu.VMEM((I1, I1), jnp.float32)],
        compiler_params=pltpu.CompilerParams(vmem_limit_bytes=20 << 20),
        name="sweeps",
    )(packed, start_rows)


def factors(mode2_factor, mode3_factor, mode4_factor, me):
    turned = jnp.transpose(mode3_factor)
    turned = lax.dynamic_slice_in_dim(
        jnp.concatenate([turned, turned], axis=0), me * RANKS, R3, 0)
    species = mode4_factor.shape[0]
    local = species // NARROW
    blocks = mode4_factor.reshape(NARROW, local, R4)[::-1].reshape(species, R4)
    blocks = lax.dynamic_slice_in_dim(
        jnp.concatenate([blocks, blocks], axis=0), (NARROW - 1 - me) * local, species, 0)
    weights = jnp.transpose(blocks)[:, None, :, None] * jnp.eye(8, dtype=jnp.float32)[None, :, None, :]
    weights = weights.reshape(R4 * 8, species * 8)
    cells = jnp.transpose(mode2_factor.reshape(WIDE, LOCAL2, R2), (2, 1, 0)).reshape(R2, I2)
    return turned, weights, cells


def body(tensor, mode2_factor, mode3_factor, mode4_factor, start_basis):
    me = lax.axis_index("narrow")
    turned, weights, cells = factors(mode2_factor, mode3_factor, mode4_factor, me)
    field = jnp.transpose(tensor, (0, 1, 3, 2))

    def send(blocks):
        got = [blocks[0]]
        for j in range(1, NARROW):
            ring = [(i, (i + j) % NARROW) for i in range(NARROW)]
            got.append(lax.ppermute(blocks[j], "narrow", ring))
        return got

    count = len(CHUNKS)
    got = send(mode3(field, turned, CHUNKS[0]))
    parts = []
    for index in range(count):
        if index + 1 < count:
            blocks = mode3(field, turned, CHUNKS[index + 1])
            coming = send(blocks)
            got, blocks = lax.optimization_barrier((got, blocks))
        sums = lax.all_to_all(species_sum(got, weights), "wide", 0, 0, tiled=True)
        got = coming
        parts.append(sums.reshape(-1, LANES))
    tiles, core = gram_first(parts[:-1], cells)
    packed = gram_last(parts[-1], core, tiles, cells)
    everyone = ("wide", "narrow")
    packed = packed.reshape(WIDE * NARROW, -1, LANES)
    packed = add_parts(lax.all_to_all(packed, everyone, 0, 0, tiled=True))
    packed = lax.all_to_all(packed, everyone, 0, 0, tiled=True)
    return jnp.transpose(sweeps(packed.reshape(-1, LANES), jnp.transpose(start_basis)))


def solution(mesh):
    in_specs = (P("narrow", "wide", None, None), P(), P(), P(), P())
    return jax.shard_map(body, mesh=mesh, in_specs=in_specs, out_specs=P(), check_vma=False)
```

time: 314 us -> 242 us (0.77)
  waiting for transfers between devices: 119 us -> 44.3 us
  blocking collectives: 24.8 us -> 58.3 us
  local copies, waits for them, and re-layouts: 27.7 us -> 7.26 us
  Pallas kernels: 83.5 us -> 78.5 us
  starting transfers between devices: 55.3 us -> 50.3 us
    ppermute x12 -> x9, waiting for transfers between devices: 82.6 us -> 20 us  [send(): got.append(lax.ppermute(blocks[j], 'narrow', ring))]
    all_to_all x0 -> x1, blocking collectives: none -> 22.9 us  [body(): packed = lax.all_to_all(packed, everyone, 0, 0, tiled=True)]
    unnamed x12 -> x22, local copies, waits for them, and re-layouts: 23.9 us -> 4.31 us
    all_to_all x5 -> x3, starting transfers between devices: 37.3 us -> 24.3 us  [body(): sums = lax.all_to_all(species_sum(got, weights), 'wide', 0, 0, tiled=True)]
    all_to_all x5 -> x3, waiting for transfers between devices: 36.5 us -> 24.3 us  [body(): sums = lax.all_to_all(species_sum(got, weights), 'wide', 0, 0, tiled=True)]
    all_to_all x1, blocking collectives: 24.8 us -> 35.3 us  [body(): packed = add_parts(lax.all_to_all(packed, everyone, 0, 0, tiled=True))]
    ppermute x12 -> x9, starting transfers between devices: 17.9 us -> 26.1 us  [send(): got.append(lax.ppermute(blocks[j], 'narrow', ring))]
    pallas_call x5, Pallas kernels: 33.4 us -> 26 us  [the longest x3 17.9 us: mode3(): pl.pallas_call(mode3_kernel, grid=(species // some,), in_specs=in_specs,...]
  transfers between devices with their start and end apart: 17 -> 12, of which waited for: 11 -> 7; matrix products, arithmetic and copies ran while one was open for 2% -> 2% of each run, Pallas kernels for 8% -> 12%
where the time goes in v2:
time: 242 us; the launch traced here: 241 us
  Pallas kernels  78.5 us (32%)
  blocking collectives  58.3 us (24%)
  starting transfers between devices  50.3 us (21%)
  waiting for transfers between devices  44.3 us (18%)
  local copies, waits for them, and re-layouts  7.26 us (3%)
  other arithmetic  2.68 us (1%)
    pallas_call x1, Pallas kernels, sweeps(): pl.pallas_call(sweep_kernel, in_specs=[VMEM, VMEM], out_specs=VMEM, out_s...  40 us
    all_to_all x1, blocking collectives, body(): packed = add_parts(lax.all_to_all(packed, everyone, 0, 0, tiled=True))  35.3 us
    ppermute x9, starting transfers between devices, send(): got.append(lax.ppermute(blocks[j], 'narrow', ring))  26.1 us
    all_to_all x3, waiting for transfers between devices, body(): sums = lax.all_to_all(species_sum(got, weights), 'wide', 0, 0, tiled=True)  24.3 us
    all_to_all x3, starting transfers between devices, body(): sums = lax.all_to_all(species_sum(got, weights), 'wide', 0, 0, tiled=True)  24.3 us
    all_to_all x1, blocking collectives, body(): packed = lax.all_to_all(packed, everyone, 0, 0, tiled=True)  22.9 us
    ppermute x9, waiting for transfers between devices, send(): got.append(lax.ppermute(blocks[j], 'narrow', ring))  20 us
    pallas_call x3, Pallas kernels, mode3(): pl.pallas_call(mode3_kernel, grid=(species // some,), in_specs=in_specs,...  17.9 us
  transfers between devices with their start and end apart: 12, of which 7 were waited for; matrix products, arithmetic and copies ran while one was open for 2% of the time, Pallas kernels for 12%

profile of v2, /device:TPU:1, one launch (start us, length us, event | category | flops | bytes accessed | tf_op | source)
XLA Modules:
  0.0 241.5 jit_solution(6450692499844544181)
XLA Ops:
  0.0 0.9 fusion.factor_ref
  0.9 6.8 %mode3.5 = (f32[8,24,1024]{2,1,0:T(8,128)S(1)}, f32[8,24,1024]{2,1,0:T(8,128)}, f32[8,24,1024]{2,1,0:T(8,128)}, f32[8,24,1024]{2,1,0:T(8,128)}) custom-call(f32[96,256]{1,0:T(8,128)S(1)} %fusion.factor_ref, f32[8,4,672,256]{3,2,1,0:T(8,128)} %bitcast.25), custom_call_target="tpu_custom_call" | custom-call | flops 1207959552 | bytes 11534336 | tf_op jit(solution)/shard_map/mode3/pallas_call | solution.py:94
  7.7 2.0 collective-permute-start.6
  9.8 2.5 %collective-permute-start.7 = (f32[8,24,1024]{2,1,0:T(8,128)}, f32[8,24,1024]{2,1,0:T(8,128)}, u32[]{:S(2)}, u32[]{:S(2)}) collective-permute-start(f32[8,24,1024]{2,1,0:T(8,128)} %get-tuple-element.37), channel_id=1, source_target_pairs={{0,2},{1,3},{2,0},{3,1},{4,6},{5,7},{6,4},{7,5},{8,10},{9,11},{10,... | collective-permute-start | bytes 2359304 | tf_op jit(solution)/shard_map/ppermute | solution.py:380
  12.2 1.1 collective-permute-start.8
  13.3 6.8 %mode3.4 = (f32[8,24,1024]{2,1,0:T(8,128)S(1)}, f32[8,24,1024]{2,1,0:T(8,128)}, f32[8,24,1024]{2,1,0:T(8,128)}, f32[8,24,1024]{2,1,0:T(8,128)}) custom-call(f32[96,256]{1,0:T(8,128)S(1)} %fusion.factor_ref, f32[8,4,672,256]{3,2,1,0:T(8,128)} %bitcast.26), custom_call_target="tpu_custom_call" | custom-call | flops 1207959552 | bytes 11534336 | tf_op jit(solution)/shard_map/mode3/pallas_call | solution.py:94
  20.5 0.8 collective-permute-start.4
  21.5 1.7 broadcast_multiply_fusion
  23.2 2.8 %mul.27.weights_ref = f32[128,256]{1,0:T(8,128)S(1)} reshape(f32[16,8,32,8]{3,2,1,0:T(8,128)} %broadcast_multiply_fusion) | data formatting | bytes 262144 | tf_op jit(solution)/shard_map/mul | solution.py:365
  26.0 4.3 %mode3.3 = (f32[8,24,640]{2,1,0:T(8,128)S(1)}, f32[8,24,640]{2,1,0:T(8,128)}, f32[8,24,640]{2,1,0:T(8,128)}, f32[8,24,640]{2,1,0:T(8,128)S(1)}) custom-call(f32[96,256]{1,0:T(8,128)S(1)} %fusion.factor_ref, f32[8,4,672,256]{3,2,1,0:T(8,128)} %bitcast.27, f32[8,4,672,256]{3,2,1,0:T(8,128)} %bitcast.28), custom_call_target="tpu_custom_call" | custom-call | flops 754974720 | bytes 7208960 | tf_op jit(solution)/shard_map/mode3/pallas_call | solution.py:94
  31.1 1.6 collective-permute-start.5
  32.7 13.7 %collective-permute-done.7.refs_2_ = f32[8,24,1024]{2,1,0:T(8,128)} collective-permute-done((f32[8,24,1024]{2,1,0:T(8,128)}, f32[8,24,1024]{2,1,0:T(8,128)}, u32[]{:S(2)}, u32[]{:S(2)}) %collective-permute-start.7) | collective-permute-done | bytes 786464 | tf_op jit(solution)/shard_map/ppermute | solution.py:380
  46.7 1.7 collective-permute-start.1
  48.4 4.2 %species.5 = f32[32,96,128]{2,1,0:T(8,128)} custom-call(f32[128,256]{1,0:T(8,128)S(1)} %mul.27.weights_ref, f32[8,24,1024]{2,1,0:T(8,128)S(1)} %get-tuple-element.43.refs_0_, f32[8,24,1024]{2,1,0:T(8,128)} %collective-permute-done.6.refs_1_, f32[8,24,1024]{2,1,0:T(8,128)} %collective-permute-done.7.refs_2_, f32[8,24,1024]{2,1,0:T(8,128)} %collective-permute-done.8.refs_3_), custom_call_target="tpu_custom_call" | custom-call | flops 99999997952 | bytes 4718592 | tf_op jit(solution)/shard_map/species/pallas_call | solution.py:143
  52.6 11.6 %all-to-all-start.2 = ((f32[32,96,128]{2,1,0:T(8,128)}), f32[32,96,128]{2,1,0:T(8,128)S(1)}, u32[]{:S(2)}, u32[]{:S(2)}) async-start(f32[32,96,128]{2,1,0:T(8,128)} %species.5), calls=%async_computation.2 | async-start | bytes 3145728 | tf_op jit(solution)/shard_map/all_to_all | solution.py:391
  64.2 16.1 %collective-permute-start.2 = (f32[8,24,640]{2,1,0:T(8,128)}, f32[8,24,640]{2,1,0:T(8,128)}, u32[]{:S(2)}, u32[]{:S(2)}) collective-permute-start(f32[8,24,640]{2,1,0:T(8,128)} %copy-done.7), channel_id=1, source_target_pairs={{0,3},{1,0},{2,1},{3,2},{4,7},{5,4},{6,5},{7,6},{8,11},{9,8},{10,9... | collective-permute-start | bytes 1474568 | tf_op jit(solution)/shard_map/ppermute | solution.py:380
  80.4 4.1 %species.4 = f32[32,96,128]{2,1,0:T(8,128)} custom-call(f32[128,256]{1,0:T(8,128)S(1)} %mul.27.weights_ref, f32[8,24,1024]{2,1,0:T(8,128)S(1)} %get-tuple-element.39.refs_0_, f32[8,24,1024]{2,1,0:T(8,128)S(1)} %collective-permute-done.3.refs_1_, f32[8,24,1024]{2,1,0:T(8,128)} %collective-permute-done.4.refs_2_, f32[8,24,1024]{2,1,0:T(8,128)} %collective-permute-done.5.refs_3_), custom_call_target="tpu_custom_call" | custom-call | flops 99999997952 | bytes 4718592 | tf_op jit(solution)/shard_map/species/pallas_call | solution.py:143
  84.5 2.4 all-to-all-done.2
  86.9 8.4 %all-to-all-start.1 = ((f32[32,96,128]{2,1,0:T(8,128)}), f32[32,96,128]{2,1,0:T(8,128)}, u32[]{:S(2)}, u32[]{:S(2)}) async-start(f32[32,96,128]{2,1,0:T(8,128)} %species.4), calls=%async_computation.1 | async-start | bytes 3145728 | tf_op jit(solution)/shard_map/all_to_all | solution.py:391
  95.3 5.9 %collective-permute-done.1.refs_2_ = f32[8,24,640]{2,1,0:T(8,128)} collective-permute-done((f32[8,24,640]{2,1,0:T(8,128)}, f32[8,24,640]{2,1,0:T(8,128)}, u32[]{:S(2)}, u32[]{:S(2)}) %collective-permute-start.1) | collective-permute-done | bytes 491552 | tf_op jit(solution)/shard_map/ppermute | solution.py:380
  101.2 3.9 %species.3 = f32[32,64,128]{2,1,0:T(8,128)} custom-call(f32[128,256]{1,0:T(8,128)S(1)} %mul.27.weights_ref, f32[8,24,640]{2,1,0:T(8,128)S(1)} %copy-done.6, f32[8,24,640]{2,1,0:T(8,128)} %collective-permute-done.refs_1_, f32[8,24,640]{2,1,0:T(8,128)} %collective-permute-done.1.refs_2_, f32[8,24,640]{2,1,0:T(8,128)} %collective-permute-done.2.refs_3_), custom_call_target="tpu_custom_call" | custom-call | flops 99999997952 | bytes 2949120 | tf_op jit(solution)/shard_map/species/pallas_call | solution.py:143
  105.2 12.9 %all-to-all-done.1 = f32[32,96,128]{2,1,0:T(8,128)} async-done(((f32[32,96,128]{2,1,0:T(8,128)}), f32[32,96,128]{2,1,0:T(8,128)}, u32[]{:S(2)}, u32[]{:S(2)}) %all-to-all-start.1) | async-done | bytes 1572896 | tf_op jit(solution)/shard_map/all_to_all | solution.py:391
  118.0 4.3 %all-to-all-start = ((f32[32,64,128]{2,1,0:T(8,128)}), f32[32,64,128]{2,1,0:T(8,128)S(1)}, u32[]{:S(2)}, u32[]{:S(2)}) async-start(f32[32,64,128]{2,1,0:T(8,128)} %species.3), calls=%async_computation | async-start | bytes 2097152 | tf_op jit(solution)/shard_map/all_to_all | solution.py:391
  122.5 1.4 copy-done.1
  123.9 5.4 %gram.2 = (f32[1280,128]{1,0:T(8,128)S(1)}, bf16[2304,512]{1,0:T(8,128)(2,1)S(1)}) custom-call(f32[96,128]{1,0:T(8,128)S(1)} %copy.19.factor_ref, f32[3072,128]{1,0:T(8,128)} %bitcast.9.refs_0_, f32[3072,128]{1,0:T(8,128)S(1)} %bitcast.23), custom_call_target="tpu_custom_call" | custom-call | flops 1207959552 | bytes 8388608 | tf_op jit(solution)/shard_map/gram/pallas_call | solution.py:231
  129.4 0.8 copy-done.2
  130.2 9.1 %all-to-all-done = f32[32,64,128]{2,1,0:T(8,128)S(1)} async-done(((f32[32,64,128]{2,1,0:T(8,128)}), f32[32,64,128]{2,1,0:T(8,128)S(1)}, u32[]{:S(2)}, u32[]{:S(2)}) %all-to-all-start) | async-done | bytes 1048608 | tf_op jit(solution)/shard_map/all_to_all | solution.py:391
  139.3 1.1 copy-done.3
  140.4 2.6 %gram.3 = f32[2048,128]{1,0:T(8,128)S(1)} custom-call(f32[96,128]{1,0:T(8,128)S(1)} %copy.19.factor_ref, f32[2048,128]{1,0:T(8,128)S(1)} %bitcast.20, bf16[2304,512]{1,0:T(8,128)(2,1)S(1)} %get-tuple-element.47.core_ref, f32[1280,128]{1,0:T(8,128)S(1)} %copy-done.3), custom_call_target="tpu_custom_call" | custom-call | flops 743178240 | bytes 8388608 | tf_op jit(solution)/shard_map/gram/pallas_call | solution.py:231
  143.0 35.3 %all_to_all.25.x_ref = f32[128,16,128]{2,1,0:T(8,128)S(1)} all-to-all(f32[128,16,128]{2,1,0:T(8,128)S(1)} %bitcast.21), channel_id=1, replica_groups=mesh['wide'=32,'narrow'=4] {'wide','narrow'}, dimensions={0} | all-to-all | bytes 2097152 | tf_op jit(solution)/shard_map/all_to_all | solution.py:398
  178.6 22.9 %all_to_all.26 = f32[128,16,128]{2,1,0:T(8,128)S(1)} all-to-all(f32[128,16,128]{2,1,0:T(8,128)S(1)} %add.9), channel_id=1, replica_groups=mesh['wide'=32,'narrow'=4] {'wide','narrow'}, dimensions={0} | all-to-all | bytes 2097152 | tf_op jit(solution)/shard_map/all_to_all | solution.py:399
  201.5 40.0 %sweeps.1 = f32[96,672]{1,0:T(8,128)} custom-call(f32[2048,128]{1,0:T(8,128)S(1)} %bitcast.22, f32[96,672]{1,0:T(8,128)S(1)} %bitcast.24), custom_call_target="tpu_custom_call" | custom-call | tf_op jit(solution)/shard_map/sweeps/pallas_call | solution.py:347
  (35 shorter events, 2.2 us)
Async XLA Ops:
  7.7 23.4 %collective-permute-start.6 = (f32[8,24,1024]{2,1,0:T(8,128)}, f32[8,24,1024]{2,1,0:T(8,128)}, u32[]{:S(2)}, u32[]{:S(2)}) collective-permute-start(f32[8,24,1024]{2,1,0:T(8,128)} %get-tuple-element.36), channel_id=1, source_target_pairs={{0,1},{1,2},{2,3},{3,0},{4,5},{5,6},{6,7},{7,4},{8,9},{9,10},{10,1... | collective-permute-start | bytes 2359304 | tf_op jit(solution)/shard_map/ppermute | solution.py:380
  9.8 36.6 %collective-permute-start.7 = (f32[8,24,1024]{2,1,0:T(8,128)}, f32[8,24,1024]{2,1,0:T(8,128)}, u32[]{:S(2)}, u32[]{:S(2)}) collective-permute-start(f32[8,24,1024]{2,1,0:T(8,128)} %get-tuple-element.37), channel_id=1, source_target_pairs={{0,2},{1,3},{2,0},{3,1},{4,6},{5,7},{6,4},{7,5},{8,10},{9,11},{10,... | collective-permute-start | bytes 2359304 | tf_op jit(solution)/shard_map/ppermute | solution.py:380
  12.2 9.1 %copy-start.9 = (f32[32,16]{0,1:T(8,128)S(1)}, f32[32,16]{0,1:T(8,128)}, u32[]{:S(2)}) copy-start(f32[32,16]{0,1:T(8,128)} %param.8) | copy-start | bytes 6148
  12.2 34.5 %collective-permute-start.8 = (f32[8,24,1024]{2,1,0:T(8,128)}, f32[8,24,1024]{2,1,0:T(8,128)}, u32[]{:S(2)}, u32[]{:S(2)}) collective-permute-start(f32[8,24,1024]{2,1,0:T(8,128)} %get-tuple-element.38), channel_id=1, source_target_pairs={{0,3},{1,0},{2,1},{3,2},{4,7},{5,4},{6,5},{7,6},{8,11},{9,8},{10,9... | collective-permute-start | bytes 2359304 | tf_op jit(solution)/shard_map/ppermute | solution.py:380
  20.1 44.1 %collective-permute-start.3 = (f32[8,24,1024]{2,1,0:T(8,128)}, f32[8,24,1024]{2,1,0:T(8,128)S(1)}, u32[]{:S(2)}, u32[]{:S(2)}) collective-permute-start(f32[8,24,1024]{2,1,0:T(8,128)} %get-tuple-element.32), channel_id=1, source_target_pairs={{0,1},{1,2},{2,3},{3,0},{4,5},{5,6},{6,7},{7,4},{8,9},{9,10},{10,1... | collective-permute-start | bytes 2359304 | tf_op jit(solution)/shard_map/ppermute | solution.py:380
  20.5 59.8 %collective-permute-start.4 = (f32[8,24,1024]{2,1,0:T(8,128)}, f32[8,24,1024]{2,1,0:T(8,128)}, u32[]{:S(2)}, u32[]{:S(2)}) collective-permute-start(f32[8,24,1024]{2,1,0:T(8,128)} %get-tuple-element.33), channel_id=1, source_target_pairs={{0,2},{1,3},{2,0},{3,1},{4,6},{5,7},{6,4},{7,5},{8,10},{9,11},{10,... | collective-permute-start | bytes 2359304 | tf_op jit(solution)/shard_map/ppermute | solution.py:380
  30.3 0.8 copy-start.5
  31.1 21.5 %copy-start.7 = (f32[8,24,640]{2,1,0:T(8,128)}, f32[8,24,640]{2,1,0:T(8,128)S(1)}, u32[]{:S(2)}) copy-start(f32[8,24,640]{2,1,0:T(8,128)S(1)} %get-tuple-element.30) | copy-start | bytes 1474564
  31.1 49.3 %collective-permute-start.5 = (f32[8,24,1024]{2,1,0:T(8,128)}, f32[8,24,1024]{2,1,0:T(8,128)}, u32[]{:S(2)}, u32[]{:S(2)}) collective-permute-start(f32[8,24,1024]{2,1,0:T(8,128)} %get-tuple-element.34), channel_id=1, source_target_pairs={{0,3},{1,0},{2,1},{3,2},{4,7},{5,4},{6,5},{7,6},{8,11},{9,8},{10,9... | collective-permute-start | bytes 2359304 | tf_op jit(solution)/shard_map/ppermute | solution.py:380
  46.4 48.9 %collective-permute-start = (f32[8,24,640]{2,1,0:T(8,128)}, f32[8,24,640]{2,1,0:T(8,128)}, u32[]{:S(2)}, u32[]{:S(2)}) collective-permute-start(f32[8,24,640]{2,1,0:T(8,128)} %get-tuple-element.28), channel_id=1, source_target_pairs={{0,1},{1,2},{2,3},{3,0},{4,5},{5,6},{6,7},{7,4},{8,9},{9,10},{10,1... | collective-permute-start | bytes 1474568 | tf_op jit(solution)/shard_map/ppermute | solution.py:380
  46.7 54.5 %collective-permute-start.1 = (f32[8,24,640]{2,1,0:T(8,128)}, f32[8,24,640]{2,1,0:T(8,128)}, u32[]{:S(2)}, u32[]{:S(2)}) collective-permute-start(f32[8,24,640]{2,1,0:T(8,128)} %get-tuple-element.29), channel_id=1, source_target_pairs={{0,2},{1,3},{2,0},{3,1},{4,6},{5,7},{6,4},{7,5},{8,10},{9,11},{10,... | collective-permute-start | bytes 1474568 | tf_op jit(solution)/shard_map/ppermute | solution.py:380
  52.6 34.3 %all-to-all-start.2 = ((f32[32,96,128]{2,1,0:T(8,128)}), f32[32,96,128]{2,1,0:T(8,128)S(1)}, u32[]{:S(2)}, u32[]{:S(2)}) async-start(f32[32,96,128]{2,1,0:T(8,128)} %species.5), calls=%async_computation.2 | async-start | bytes 3145728 | tf_op jit(solution)/shard_map/all_to_all | solution.py:391
  64.2 37.0 %collective-permute-start.2 = (f32[8,24,640]{2,1,0:T(8,128)}, f32[8,24,640]{2,1,0:T(8,128)}, u32[]{:S(2)}, u32[]{:S(2)}) collective-permute-start(f32[8,24,640]{2,1,0:T(8,128)} %copy-done.7), channel_id=1, source_target_pairs={{0,3},{1,0},{2,1},{3,2},{4,7},{5,4},{6,5},{7,6},{8,11},{9,8},{10,9... | collective-permute-start | bytes 1474568 | tf_op jit(solution)/shard_map/ppermute | solution.py:380
  84.5 16.7 %copy-start.6 = (f32[8,24,640]{2,1,0:T(8,128)S(1)}, f32[8,24,640]{2,1,0:T(8,128)}, u32[]{:S(2)}) copy-start(f32[8,24,640]{2,1,0:T(8,128)} %copy-done.5) | copy-start | bytes 1474564
  86.9 18.3 %copy-start = (f32[32,96,128]{2,1,0:T(8,128)}, f32[32,96,128]{2,1,0:T(8,128)S(1)}, u32[]{:S(2)}) copy-start(f32[32,96,128]{2,1,0:T(8,128)S(1)} %all-to-all-done.2) | copy-start | bytes 4718596
  86.9 31.1 %all-to-all-start.1 = ((f32[32,96,128]{2,1,0:T(8,128)}), f32[32,96,128]{2,1,0:T(8,128)}, u32[]{:S(2)}, u32[]{:S(2)}) async-start(f32[32,96,128]{2,1,0:T(8,128)} %species.4), calls=%async_computation.1 | async-start | bytes 3145728 | tf_op jit(solution)/shard_map/all_to_all | solution.py:391
  105.2 17.1 %copy-start.8 = (f32[128,96]{0,1:T(8,128)S(1)}, f32[128,96]{0,1:T(8,128)}, u32[]{:S(2)}) copy-start(f32[128,96]{0,1:T(8,128)} %param.6) | copy-start | bytes 147460
  118.0 21.3 %all-to-all-start = ((f32[32,64,128]{2,1,0:T(8,128)}), f32[32,64,128]{2,1,0:T(8,128)S(1)}, u32[]{:S(2)}, u32[]{:S(2)}) async-start(f32[32,64,128]{2,1,0:T(8,128)} %species.3), calls=%async_computation | async-start | bytes 2097152 | tf_op jit(solution)/shard_map/all_to_all | solution.py:391
  122.5 1.4 copy-start.1
  129.4 0.8 copy-start.2
  139.3 1.1 copy-start.3
  178.4 23.1 %copy-start.4 = (f32[672,96]{0,1:T(8,128)S(1)}, f32[672,96]{0,1:T(8,128)}, u32[]{:S(2)}) copy-start(f32[672,96]{0,1:T(8,128)} %param.9) | copy-start | bytes 774148

commit v3 on v2

--- a/solution.py
+++ b/solution.py
@@ -18,6 +18,8 @@
 ITERS = 8
 NARROW = 4
 WIDE = 32
+WIDE_AXES = ("y", "z", "core")
+CHIPS = 64
 LANES = 128
 FULL = I1 // LANES
 TAIL = I1 - FULL * LANES
@@ -25,8 +27,11 @@
 LOCAL2 = I2 // WIDE
 RANKS = R3 // NARROW
 PAIRS = RANKS * R4 // WIDE
-CHUNKS = ((0, 1), (2, 3), (4,))
-FIRST = FULL - 1
+CHUNKS = ((4,), (0, 1), (2, 3))
+EARLY = 3 * LANES + TAIL
+LATE = 2 * LANES
+EARLY_TILES = ((0, 0), (0, 1), (1, 1), (0, 4), (1, 4), (4, 4))
+LATE_TILES = ((0, 2), (0, 3), (1, 2), (1, 3), (4, 2), (4, 3), (2, 2), (2, 3), (3, 3))
 SPECIES_COST = 10 ** 11
 VMEM = pl.BlockSpec(memory_space=pltpu.VMEM)
 
@@ -86,7 +91,7 @@
         pl.BlockSpec((some, LOCAL2, LANES * count, I3), lambda s: (s, 0, index, 0)),
     ]
     args = [factor_rows, field]
-    if chunk == CHUNKS[-1]:
+    if chunk == CHUNKS[0]:
         width += LANES
         in_specs.append(pl.BlockSpec((some, LOCAL2, TAIL, I3), lambda s: (s, 0, BODY // TAIL, 0)))
         args.append(field)
@@ -154,23 +159,22 @@
     )(weights, *parts)
 
 
-def core_columns(factor, parts, last, store):
+def core_columns(factor, parts, store):
     f_high, f_low = split(factor)
     doubled = jnp.concatenate([f_high, f_high], axis=1)
-    strides = [p.shape[0] // WIDE for p in parts]
-    counts = [len(tiles) for tiles in (CHUNKS[-1:] if last else CHUNKS[:-1])]
-
-    def piece(p, place):
-        return parts[p][pl.ds(place, WIDE, stride=strides[p]), :]
+
+    def piece(ref, place):
+        return ref[pl.ds(place, WIDE, stride=ref.shape[0] // WIDE), :]
 
     for i in range(PAIRS):
         cells = []
-        if last:
-            tail = piece(0, LOCAL2 * counts[0] * PAIRS + i)
         for b in range(LOCAL2):
-            row = [piece(p, (b * n + t) * PAIRS + i) for p, n in enumerate(counts) for t in range(n)]
-            if last:
-                row.append(tail[:, b * TAIL:(b + 1) * TAIL])
+            row = []
+            for ref, count, tail in parts:
+                row += [piece(ref, (b * count + t) * PAIRS + i) for t in range(count)]
+                if tail:
+                    last = piece(ref, LOCAL2 * count * PAIRS + i)
+                    row.append(last[:, b * TAIL:(b + 1) * TAIL])
             cells.append(jnp.concatenate(row, axis=1))
         v_high, v_low = split(jnp.concatenate(cells, axis=0))
         core = product(doubled, jnp.concatenate([v_high, v_low], axis=0), ((1,), (0,)))
@@ -182,54 +186,66 @@
     return product(a_high, b_high, rows) + product(a_high, b_low, rows) + product(a_low, b_high, rows)
 
 
-def gram_first_kernel(factor_ref, *refs):
-    parts, (out, core_ref) = refs[:-2], refs[-2:]
+def tile_of(block, i, j):
+    return block[i * LANES:(i + 1) * LANES, j * LANES:(j + 1) * LANES]
+
+
+def gram_first_kernel(factor_ref, edge_ref, part_ref, out, core_ref):
     half = PAIRS * R2
 
     def store(i, high, low):
         core_ref[i * R2:(i + 1) * R2, :] = high
         core_ref[half + i * R2:half + (i + 1) * R2, :] = low
 
-    core_columns(factor_ref[...], parts, False, store)
-    place = 0
-    for i in range(FIRST):
-        left = slice(i * LANES, (i + 1) * LANES)
-        right = slice(i * LANES, FIRST * LANES)
-        block = inner_product(core_ref[:half, left], core_ref[half:, left],
-                              core_ref[:half, right], core_ref[half:, right])
-        for j in range(FIRST - i):
-            out[place:place + LANES, :] = block[:, j * LANES:(j + 1) * LANES]
-            place += LANES
-
-
-def gram_last_kernel(factor_ref, part_ref, core_ref, tiles_ref, out, high_ref, low_ref):
+    core_columns(factor_ref[...], ((part_ref, 2, False), (edge_ref, 1, True)), store)
+    two = slice(0, LATE)
+    rest = slice(LATE, EARLY)
+    top = inner_product(core_ref[:half, two], core_ref[half:, two], core_ref[:half, :], core_ref[half:, :])
+    own = inner_product(core_ref[:half, rest], core_ref[half:, rest],
+                        core_ref[:half, rest], core_ref[half:, rest])
+    tiles = [tile_of(top, 0, 0), tile_of(top, 0, 1), tile_of(top, 1, 1),
+             tile_of(top, 0, 2), tile_of(top, 1, 2), own[:LANES, :LANES]]
+    for n, tile in enumerate(tiles):
+        out[n * LANES:(n + 1) * LANES, :] = tile
+    edges = [top[:LANES, 3 * LANES:], top[LANES:, 3 * LANES:], own[:LANES, LANES:]]
+    corner = own[LANES:, LANES:]
+    edges.append(jnp.concatenate([corner] * (LANES // TAIL), axis=0))
+    out[len(tiles) * LANES:, :] = jnp.concatenate(edges, axis=1)
+
+
+def gram_last_kernel(me_ref, factor_ref, part_ref, core_ref, early_ref, keep, give, high_ref, low_ref, out):
     half = PAIRS * R2
 
     def store(i, high, low):
         high_ref[i * R2:(i + 1) * R2, :] = high
         low_ref[i * R2:(i + 1) * R2, :] = low
 
-    core_columns(factor_ref[...], [part_ref], True, store)
-    place = tiles_ref.shape[0]
-    out[:place, :] = tiles_ref[...]
+    core_columns(factor_ref[...], ((part_ref, 2, False),), store)
+    place = early_ref.shape[0]
+    out[:place, :] = early_ref[...]
     high, low = high_ref[...], low_ref[...]
     above = inner_product(core_ref[:half, :], core_ref[half:, :], high, low)
     own = inner_product(high, low, high, low)
-    out[place:place + FIRST * LANES, :] = above[:, :LANES]
-    place += FIRST * LANES
-    out[place:place + LANES, :] = own[:LANES, :LANES]
-    edge = own[:LANES, LANES:]
-    out[place + 64:place + LANES, :64] = jnp.concatenate([edge[:64], edge[64:]], axis=1)
-    out[64:96, :TAIL] = own[LANES:, LANES:]
-    place += LANES
-    out[place:place + LANES, :] = jnp.concatenate(
-        [above[i * LANES:(i + 1) * LANES, LANES:] for i in range(FIRST)], axis=1)
+    tiles = [tile_of(above, i, j) for i in range(3) for j in range(2)]
+    tiles += [tile_of(own, 0, 0), tile_of(own, 0, 1), tile_of(own, 1, 1)]
+    for n, tile in enumerate(tiles):
+        out[place + n * LANES:place + (n + 1) * LANES, :] = tile
+    left = above[3 * LANES:, :]
+    for j, n in ((0, 6), (1, 8)):
+        corner = place + n * LANES + 64
+        out[corner:corner + TAIL, :64] = left[:, j * LANES:j * LANES + 64]
+        out[corner + TAIL:corner + 2 * TAIL, :64] = left[:, j * LANES + 64:(j + 1) * LANES]
+    rows = keep.shape[0]
+    me = me_ref[0]
+    keep[...] = out[pl.ds(pl.multiple_of(me * rows, rows), rows), :]
+    give[...] = out[pl.ds(pl.multiple_of((1 - me) * rows, rows), rows), :]
 
 
 def gram_call(kernel, args, out_shape, scratch, flops):
     some = isinstance(out_shape, list)
     return pl.pallas_call(
-        kernel, grid=(1,), in_specs=[whole(x) for x in args],
+        kernel, grid=(1,),
+        in_specs=[pl.BlockSpec(memory_space=pltpu.SMEM) if x.ndim == 1 else whole(x) for x in args],
         out_specs=[whole(x) for x in out_shape] if some else whole(out_shape),
         out_shape=out_shape, scratch_shapes=scratch,
         compiler_params=pltpu.CompilerParams(vmem_limit_bytes=48 << 20),
@@ -240,21 +256,20 @@
 
 def gram_first(parts, factor_rows):
     rows = PAIRS * R2
-    columns = FIRST * LANES
-    tiles = FIRST * (FIRST + 1) // 2
     return gram_call(
         gram_first_kernel, [factor_rows, *parts],
-        [jax.ShapeDtypeStruct((tiles * LANES, LANES), jnp.float32),
-         jax.ShapeDtypeStruct((2 * rows, columns), jnp.bfloat16)],
-        [], 4 * rows * columns * columns)
-
-
-def gram_last(part, core, tiles, factor_rows):
-    half = pltpu.VMEM((PAIRS * R2, LANES + TAIL), jnp.bfloat16)
+        [jax.ShapeDtypeStruct(((len(EARLY_TILES) + 1) * LANES, LANES), jnp.float32),
+         jax.ShapeDtypeStruct((2 * rows, EARLY), jnp.bfloat16)],
+        [], 4 * rows * EARLY * EARLY)
+
+
+def gram_last(me, part, core, early, factor_rows):
+    half = pltpu.VMEM((PAIRS * R2, LATE), jnp.bfloat16)
     return gram_call(
-        gram_last_kernel, [factor_rows, part, core, tiles],
-        jax.ShapeDtypeStruct((16 * LANES, LANES), jnp.float32),
-        [half, half], 6 * PAIRS * R2 * I1 * (LANES + TAIL))
+        gram_last_kernel, [me, factor_rows, part, core, early],
+        [jax.ShapeDtypeStruct((8 * LANES, LANES), jnp.float32)] * 2,
+        [half, half, pltpu.VMEM((16 * LANES, LANES), jnp.float32)],
+        6 * PAIRS * R2 * I1 * LATE)
 
 
 def add_kernel(x_ref, o_ref):
@@ -270,6 +285,29 @@
         compiler_params=pltpu.CompilerParams(vmem_limit_bytes=20 << 20),
         name="add",
     )(x)
+
+
+def three(x):
+    high = x.astype(jnp.bfloat16)
+    rest = x - high.astype(jnp.float32)
+    middle = rest.astype(jnp.bfloat16)
+    return high, middle, (rest - middle.astype(jnp.float32)).astype(jnp.bfloat16)
+
+
+def times(x, parts):
+    n = x.shape[0]
+    x1, x2, x3 = three(x)
+    rows = ((1,), (0,))
+    a = product(jnp.concatenate([x1, x2, x3], axis=0), parts[0][...], rows)
+    b = product(jnp.concatenate([x1, x2], axis=0), parts[1][...], rows)
+    c = product(x1, parts[2][...], rows)
+    return a[:n] + ((a[n:2 * n] + b[:n]) + (a[2 * n:] + b[n:] + c))
+
+
+def inner_rows(x):
+    high, low = split(x)
+    lanes = ((1,), (1,))
+    return product(high, high, lanes) + (product(high, low, lanes) + product(low, high, lanes))
 
 
 def inverse_factor(a):
@@ -288,69 +326,89 @@
         for i in range(k + 1, blocks):
             rows[i] = jnp.where(inside, 0.0, rows[i])
         pivot = jnp.zeros((8, n), jnp.float32)
-        for j in range(8):
-            here = cols[0][j]
-            pivot = jnp.where(sub == j, here, pivot)
-            inverse = 1.0 / spread(here[j:j + 1, :])
-            pivot_row = spread(rows[k][j:j + 1, :])
-            pivot_cols = {m: spread(cols[0][m][j:j + 1, :]) for m in range(j + 1, 8)}
+        for j in range(0, 8, 2):
+            p = spread(cols[0][j][j:j + 1, :])
+            q = spread(cols[0][j][j + 1:j + 2, :])
+            s = spread(cols[0][j + 1][j + 1:j + 2, :])
+            det = p * s - q * q
+            over_p, over_det = 1.0 / p, 1.0 / det
+            row0, row1 = spread(rows[k][j:j + 1, :]), spread(rows[k][j + 1:j + 2, :])
+            pivot = jnp.where(sub == j, p, jnp.where(sub == j + 1, det * over_p, pivot))
+            u0, u1, u2 = s * over_det, q * over_det, p * over_det
+            pair = {m: (spread(cols[0][m][j:j + 1, :]), spread(cols[0][m][j + 1:j + 2, :]))
+                    for m in range(j + 2, 8)}
             for i in range(k, blocks):
-                f = cols[i - k][j] * inverse
+                c0, c1 = cols[i - k][j], cols[i - k][j + 1]
+                f0, f1 = c0 * u0 - c1 * u1, c1 * u2 - c0 * u1
                 if i == k:
-                    f = jnp.where(sub > j, f, 0.0)
-                rows[i] = rows[i] - f * pivot_row
-                for m in range(j + 1, 8):
-                    cols[i - k][m] = cols[i - k][m] - f * pivot_cols[m]
+                    f0 = jnp.where(sub > j + 1, f0, jnp.where(sub == j + 1, q * over_p, 0.0))
+                    f1 = jnp.where(sub > j + 1, f1, 0.0)
+                rows[i] = rows[i] - (f0 * row0 + f1 * row1)
+                for m in range(j + 2, 8):
+                    cols[i - k][m] = cols[i - k][m] - (f0 * pair[m][0] + f1 * pair[m][1])
         pivots.append(pivot)
     return jnp.concatenate(
         [jnp.where(lane <= sub + 8 * k, rows[k] * lax.rsqrt(pivots[k]), 0.0)
          for k in range(blocks)], axis=0)
 
 
-def sweep_kernel(packed_ref, start_ref, out_ref, gram_ref):
+def sweep_kernel(core_ref, mine_ref, other_ref, start_ref, out_ref, packed_ref, gram_ref, image_ref, *parts):
+    half = mine_ref.shape[0]
+    me = core_ref[0]
+    packed_ref[pl.ds(pl.multiple_of(me * half, half), half), :] = mine_ref[...]
+    packed_ref[pl.ds(pl.multiple_of((1 - me) * half, half), half), :] = other_ref[...]
     row = lax.broadcasted_iota(jnp.int32, (LANES, LANES), 0)
     col = lax.broadcasted_iota(jnp.int32, (LANES, LANES), 1)
-    place = 0
-    pairs = [(i, j) for i in range(FIRST) for j in range(i, FIRST)]
-    pairs += [(i, FIRST) for i in range(FIRST + 1)]
-    for i, j in pairs:
-        tile = packed_ref[place:place + LANES, :]
-        here = slice(i * LANES, (i + 1) * LANES)
-        there = slice(j * LANES, (j + 1) * LANES)
+    span = lambda i: slice(i * LANES, (i + 1) * LANES)
+    edge = packed_ref[span(len(EARLY_TILES)), :]
+    for n, pair in enumerate(EARLY_TILES + (None,) + LATE_TILES):
+        if pair is None:
+            continue
+        i, j = pair
+        tile = packed_ref[span(n), :]
         if i == j:
             above = jnp.where(row < col, tile, 0.0)
-            gram_ref[here, here] = jnp.where(row <= col, tile, 0.0) + above.T
+            gram_ref[span(i), span(i)] = jnp.where(row <= col, tile, 0.0) + above.T
         else:
-            gram_ref[here, there] = tile
-            gram_ref[there, here] = tile.T
-        place += LANES
-    last = packed_ref[place:place + LANES, :]
-    for k in range(FIRST):
-        gram_ref[k * LANES:(k + 1) * LANES, BODY:] = last[:, k * TAIL:(k + 1) * TAIL]
-    gram_ref[512:576, BODY:] = packed_ref[place - 64:place, :TAIL]
-    gram_ref[576:640, BODY:] = packed_ref[place - 64:place, TAIL:2 * TAIL]
-    gram_ref[BODY:, BODY:] = packed_ref[64:96, :TAIL]
-    gram_ref[BODY:, :BODY] = gram_ref[:BODY, BODY:].T
-    out_ref[...] = start_ref[...]
+            gram_ref[span(i), span(j)] = tile
+            gram_ref[span(j), span(i)] = tile.T
+        if i == j and i in (2, 3):
+            gram_ref[BODY:, i * LANES:i * LANES + 64] = tile[64:64 + TAIL, :64]
+            gram_ref[BODY:, i * LANES + 64:(i + 1) * LANES] = tile[64 + TAIL:, :64]
+    for k, i in enumerate((0, 1, 4)):
+        gram_ref[span(i), BODY:] = edge[:, k * TAIL:(k + 1) * TAIL]
+    gram_ref[BODY:, BODY:] = edge[:TAIL, 3 * TAIL:]
+    gram_ref[BODY:, :LATE] = gram_ref[:LATE, BODY:].T
+    gram_ref[BODY:, span(4)] = gram_ref[span(4), BODY:].T
+    gram_ref[LATE:2 * LATE, BODY:] = gram_ref[BODY:, LATE:2 * LATE].T
+    for part, value in zip(parts, three(gram_ref[...])):
+        part[...] = value
+
+    image_ref[...] = times(start_ref[...], parts)
 
     def sweep(_, carry):
-        image = exact(out_ref[...], gram_ref[...], ((1,), (0,)))
-        inner = exact(image, image, ((1,), (1,)))
-        out_ref[...] = exact(inverse_factor(inner), image, ((1,), (0,)))
+        image = image_ref[...]
+        ahead = times(image, parts)
+        image_ref[...] = exact(inverse_factor(inner_rows(image)), ahead, ((1,), (0,)))
         return carry
 
-    lax.fori_loop(0, ITERS, sweep, 0)
-    out_ref[...] = out_ref[...] * math.sqrt(I1)
-
-
-def sweeps(packed, start_rows):
+    lax.fori_loop(0, ITERS - 1, sweep, 0)
+    image = image_ref[...]
+    inner = exact(image, image, ((1,), (1,)))
+    out_ref[...] = exact(inverse_factor(inner), image, ((1,), (0,))) * math.sqrt(I1)
+
+
+def sweeps(core, mine, other, start_rows):
     return pl.pallas_call(
-        sweep_kernel, in_specs=[VMEM, VMEM], out_specs=VMEM,
+        sweep_kernel,
+        in_specs=[pl.BlockSpec(memory_space=pltpu.SMEM), VMEM, VMEM, VMEM], out_specs=VMEM,
         out_shape=jax.ShapeDtypeStruct((R1, I1), jnp.float32),
-        scratch_shapes=[pltpu.VMEM((I1, I1), jnp.float32)],
-        compiler_params=pltpu.CompilerParams(vmem_limit_bytes=20 << 20),
+        scratch_shapes=[
+            pltpu.VMEM((16 * LANES, LANES), jnp.float32), pltpu.VMEM((I1, I1), jnp.float32),
+            pltpu.VMEM((R1, I1), jnp.float32)] + [pltpu.VMEM((I1, I1), jnp.bfloat16)] * 3,
+        compiler_params=pltpu.CompilerParams(vmem_limit_bytes=32 << 20),
         name="sweeps",
-    )(packed, start_rows)
+    )(core, mine, other, start_rows)
 
 
 def factors(mode2_factor, mode3_factor, mode4_factor, me):
@@ -374,10 +432,10 @@
     field = jnp.transpose(tensor, (0, 1, 3, 2))
 
     def send(blocks):
-        got = [blocks[0]]
-        for j in range(1, NARROW):
+        got = list(blocks)
+        for j in (1, 3, 2):
             ring = [(i, (i + j) % NARROW) for i in range(NARROW)]
-            got.append(lax.ppermute(blocks[j], "narrow", ring))
+            got[j] = lax.ppermute(blocks[j], "narrow", ring)
         return got
 
     count = len(CHUNKS)
@@ -386,20 +444,28 @@
     for index in range(count):
         if index + 1 < count:
             blocks = mode3(field, turned, CHUNKS[index + 1])
+            near = [got[1], got[3]]
+            near, blocks = lax.optimization_barrier((near, blocks))
+            got[1], got[3] = near
             coming = send(blocks)
-            got, blocks = lax.optimization_barrier((got, blocks))
-        sums = lax.all_to_all(species_sum(got, weights), "wide", 0, 0, tiled=True)
+        sums = lax.all_to_all(species_sum(got, weights), WIDE_AXES, 0, 0, tiled=True)
         got = coming
         parts.append(sums.reshape(-1, LANES))
-    tiles, core = gram_first(parts[:-1], cells)
-    packed = gram_last(parts[-1], core, tiles, cells)
-    everyone = ("wide", "narrow")
-    packed = packed.reshape(WIDE * NARROW, -1, LANES)
-    packed = add_parts(lax.all_to_all(packed, everyone, 0, 0, tiled=True))
-    packed = lax.all_to_all(packed, everyone, 0, 0, tiled=True)
-    return jnp.transpose(sweeps(packed.reshape(-1, LANES), jnp.transpose(start_basis)))
+    early, core = gram_first(parts[:-1], cells)
+    core_index = lax.axis_index("core").reshape(1)
+    swap = [(0, 1), (1, 0)]
+    keep, give = gram_last(core_index, parts[-1], core, early, cells)
+    half = keep + lax.ppermute(give, "core", swap)
+    chips = ("y", "z", "narrow")
+    half = half.reshape(CHIPS, -1, LANES)
+    half = add_parts(lax.all_to_all(half, chips, 0, 0, tiled=True))
+    mine = lax.all_to_all(half, chips, 0, 0, tiled=True).reshape(-1, LANES)
+    other = lax.ppermute(mine, "core", swap)
+    return jnp.transpose(sweeps(core_index, mine, other, jnp.transpose(start_basis)))
 
 
 def solution(mesh):
-    in_specs = (P("narrow", "wide", None, None), P(), P(), P(), P())
-    return jax.shard_map(body, mesh=mesh, in_specs=in_specs, out_specs=P(), check_vma=False)
+    fine = jax.sharding.Mesh(
+        mesh.devices.reshape(4, 4, 2, NARROW), ("y", "z", "core", "narrow"))
+    in_specs = (P("narrow", WIDE_AXES, None, None), P(), P(), P(), P())
+    return jax.shard_map(body, mesh=fine, in_specs=in_specs, out_specs=P(), check_vma=False)

time: 242 us -> 224 us (0.926)
  blocking collectives: 58.3 us -> 33 us
  starting transfers between devices: 50.3 us -> 60.5 us
  Pallas kernels: 78.5 us -> 69.5 us
  local copies, waits for them, and re-layouts: 7.26 us -> 11.4 us
    all_to_all x2, blocking collectives: 58.3 us -> 33 us  [the longest x1 17.5 us: body(): half = add_parts(lax.all_to_all(half, chips, 0, 0, tiled=True))]
    all_to_all x3, starting transfers between devices: 24.3 us -> 44.7 us  [body(): lax.all_to_all(species_sum(got, weights), WIDE_AXES, 0, 0, tiled=True)]
    ppermute x9 -> x11, starting transfers between devices: 26.1 us -> 15.8 us  [the longest x9 11.8 us: send(): got[j] = lax.ppermute(blocks[j], 'narrow', ring)]
    all_to_all x3, waiting for transfers between devices: 24.3 us -> 34 us  [body(): lax.all_to_all(species_sum(got, weights), WIDE_AXES, 0, 0, tiled=True)]
    pallas_call x3, Pallas kernels: 48.1 us -> 40.2 us  [the longest x1 33.8 us: sweeps(): pl.pallas_call(sweep_kernel, in_specs=[pl.BlockSpec(memory_space=pltpu.SM...]
    ppermute x9 -> x11, waiting for transfers between devices: 20 us -> 12.2 us  [the longest x9 9.17 us: send(): got[j] = lax.ppermute(blocks[j], 'narrow', ring)]
    unnamed x22, local copies, waits for them, and re-layouts: 4.31 us -> 8.42 us
  transfers between devices with their start and end apart: 12 -> 14, of which waited for: 7 -> 5; matrix products, arithmetic and copies ran while one was open for 2% -> 2% of each run, Pallas kernels for 12% -> 13%
where the time goes in v3:
time: 224 us; the launch traced here: 223 us
  Pallas kernels  69.5 us (31%)
  starting transfers between devices  60.5 us (27%)
  waiting for transfers between devices  46.2 us (21%)
  blocking collectives  33 us (15%)
  local copies, waits for them, and re-layouts  11.4 us (5%)
  other arithmetic  2.74 us (1%)
    all_to_all x3, starting transfers between devices, body(): lax.all_to_all(species_sum(got, weights), WIDE_AXES, 0, 0, tiled=True)  44.7 us
    all_to_all x3, waiting for transfers between devices, body(): lax.all_to_all(species_sum(got, weights), WIDE_AXES, 0, 0, tiled=True)  34 us
    pallas_call x1, Pallas kernels, sweeps(): pl.pallas_call(sweep_kernel, in_specs=[pl.BlockSpec(memory_space=pltpu.SM...  33.8 us
    pallas_call x3, Pallas kernels, mode3(): pl.pallas_call(mode3_kernel, grid=(species // some,), in_specs=in_specs,...  17.9 us
    all_to_all x1, blocking collectives, body(): half = add_parts(lax.all_to_all(half, chips, 0, 0, tiled=True))  17.5 us
    all_to_all x1, blocking collectives, body(): mine = lax.all_to_all(half, chips, 0, 0, tiled=True).reshape(-1, LANES)  15.4 us
    ppermute x9, starting transfers between devices, send(): got[j] = lax.ppermute(blocks[j], 'narrow', ring)  11.8 us
    pallas_call x3, Pallas kernels, species_sum(): pl.pallas_call(functools.partial(species_kernel, tiles), grid=(ranks // 8...  11.3 us
  transfers between devices with their start and end apart: 14, of which 5 were waited for; matrix products, arithmetic and copies ran while one was open for 2% of the time, Pallas kernels for 13%

profile of v3, /device:TPU:1, one launch (start us, length us, event | category | flops | bytes accessed | tf_op | source)
XLA Modules:
  0.0 223.4 jit_solution(9148712035752052492)
XLA Ops:
  0.9 4.5 %mode3.3 = (f32[8,24,640]{2,1,0:T(8,128)S(1)}, f32[8,24,640]{2,1,0:T(8,128)}, f32[8,24,640]{2,1,0:T(8,128)}, f32[8,24,640]{2,1,0:T(8,128)}) custom-call(f32[96,256]{1,0:T(8,128)S(1)} %fusion.factor_ref, f32[8,4,672,256]{3,2,1,0:T(8,128)} %bitcast.27, f32[8,4,672,256]{3,2,1,0:T(8,128)} %bitcast.28), custom_call_target="tpu_custom_call" | custom-call | flops 754974720 | bytes 7208960 | tf_op jit(solution)/shard_map/mode3/pallas_call | solution.py:99
  5.4 2.0 collective-permute-start
  7.4 1.3 collective-permute-start.1
  8.7 1.6 collective-permute-start.7
  10.6 1.7 broadcast_multiply_fusion
  12.3 2.8 %mul.27.weights_ref = f32[128,256]{1,0:T(8,128)S(1)} reshape(f32[16,8,32,8]{3,2,1,0:T(8,128)} %broadcast_multiply_fusion) | data formatting | bytes 262144 | tf_op jit(solution)/shard_map/mul | solution.py:423
  15.1 6.8 %mode3.4 = (f32[8,24,1024]{2,1,0:T(8,128)S(1)}, f32[8,24,1024]{2,1,0:T(8,128)}, f32[8,24,1024]{2,1,0:T(8,128)}, f32[8,24,1024]{2,1,0:T(8,128)}) custom-call(f32[96,256]{1,0:T(8,128)S(1)} %fusion.factor_ref, f32[8,4,672,256]{3,2,1,0:T(8,128)} %bitcast.29), custom_call_target="tpu_custom_call" | custom-call | flops 1207959552 | bytes 11534336 | tf_op jit(solution)/shard_map/mode3/pallas_call | solution.py:99
  21.9 6.6 %mode3.5 = (f32[8,24,1024]{2,1,0:T(8,128)S(1)}, f32[8,24,1024]{2,1,0:T(8,128)}, f32[8,24,1024]{2,1,0:T(8,128)}, f32[8,24,1024]{2,1,0:T(8,128)S(1)}) custom-call(f32[96,256]{1,0:T(8,128)S(1)} %fusion.factor_ref, f32[8,4,672,256]{3,2,1,0:T(8,128)} %bitcast.30), custom_call_target="tpu_custom_call" | custom-call | flops 1207959552 | bytes 11534336 | tf_op jit(solution)/shard_map/mode3/pallas_call | solution.py:99
  29.0 2.3 %collective-permute-start.3 = (f32[8,24,1024]{2,1,0:T(8,128)}, f32[8,24,1024]{2,1,0:T(8,128)}, u32[]{:S(2)}, u32[]{:S(2)}) collective-permute-start(f32[8,24,1024]{2,1,0:T(8,128)} %get-tuple-element.40), channel_id=1, source_target_pairs={{0,3},{1,0},{2,1},{3,2},{4,7},{5,4},{6,5},{7,6},{8,11},{9,8},{10,9... | collective-permute-start | bytes 2359304 | tf_op jit(solution)/shard_map/ppermute | solution.py:438
  31.4 4.0 %species.4 = f32[32,64,128]{2,1,0:T(8,128)} custom-call(f32[128,256]{1,0:T(8,128)S(1)} %mul.27.weights_ref, f32[8,24,640]{2,1,0:T(8,128)S(1)} %get-tuple-element.49.refs_0_, f32[8,24,640]{2,1,0:T(8,128)} %collective-permute-done.refs_1_, f32[8,24,640]{2,1,0:T(8,128)} %collective-permute-done.7.refs_2_, f32[8,24,640]{2,1,0:T(8,128)} %collective-permute-done.1.refs_3_), custom_call_target="tpu_custom_call" | custom-call | flops 99999997952 | bytes 2949120 | tf_op jit(solution)/shard_map/species/pallas_call | solution.py:148
  35.4 13.1 %all-to-all-start.1 = ((f32[32,64,128]{2,1,0:T(8,128)}), f32[32,64,128]{2,1,0:T(8,128)S(1)}, u32[]{:S(2)}, u32[]{:S(2)}) async-start(f32[32,64,128]{2,1,0:T(8,128)} %species.4), calls=%async_computation.1 | async-start | bytes 2097152 | tf_op jit(solution)/shard_map/all_to_all | solution.py:451
  48.5 1.2 collective-permute-start.4
  50.4 2.0 collective-permute-start.6
  52.4 9.1 %collective-permute-done.8.refs_2_ = f32[8,24,1024]{2,1,0:T(8,128)} collective-permute-done((f32[8,24,1024]{2,1,0:T(8,128)}, f32[8,24,1024]{2,1,0:T(8,128)}, u32[]{:S(2)}, u32[]{:S(2)}) %collective-permute-start.8) | collective-permute-done | bytes 786464 | tf_op jit(solution)/shard_map/ppermute | solution.py:438
  61.5 4.2 %species.5 = f32[32,96,128]{2,1,0:T(8,128)} custom-call(f32[128,256]{1,0:T(8,128)S(1)} %mul.27.weights_ref, f32[8,24,1024]{2,1,0:T(8,128)S(1)} %get-tuple-element.53.refs_0_, f32[8,24,1024]{2,1,0:T(8,128)} %collective-permute-done.2.refs_1_, f32[8,24,1024]{2,1,0:T(8,128)} %collective-permute-done.8.refs_2_, f32[8,24,1024]{2,1,0:T(8,128)} %collective-permute-done.3.refs_3_), custom_call_target="tpu_custom_call" | custom-call | flops 99999997952 | bytes 4718592 | tf_op jit(solution)/shard_map/species/pallas_call | solution.py:148
  66.7 27.3 %all-to-all-start.2 = ((f32[32,96,128]{2,1,0:T(8,128)}), f32[32,96,128]{2,1,0:T(8,128)S(1)}, u32[]{:S(2)}, u32[]{:S(2)}) async-start(f32[32,96,128]{2,1,0:T(8,128)} %species.5), calls=%async_computation.2 | async-start | bytes 3145728 | tf_op jit(solution)/shard_map/all_to_all | solution.py:451
  94.1 3.1 %species.3 = f32[32,96,128]{2,1,0:T(8,128)S(1)} custom-call(f32[128,256]{1,0:T(8,128)S(1)} %mul.27.weights_ref, f32[8,24,1024]{2,1,0:T(8,128)S(1)} %get-tuple-element.45.refs_0_, f32[8,24,1024]{2,1,0:T(8,128)} %collective-permute-done.4.refs_1_, f32[8,24,1024]{2,1,0:T(8,128)} %collective-permute-done.5.refs_2_, f32[8,24,1024]{2,1,0:T(8,128)} %collective-permute-done.6.refs_3_), custom_call_target="tpu_custom_call" | custom-call | flops 99999997952 | bytes 4718592 | tf_op jit(solution)/shard_map/species/pallas_call | solution.py:148
  97.2 1.2 copy-done.2
  98.4 18.4 %all-to-all-done.2 = f32[32,96,128]{2,1,0:T(8,128)S(1)} async-done(((f32[32,96,128]{2,1,0:T(8,128)}), f32[32,96,128]{2,1,0:T(8,128)S(1)}, u32[]{:S(2)}, u32[]{:S(2)}) %all-to-all-start.2) | async-done | bytes 1572896 | tf_op jit(solution)/shard_map/all_to_all | solution.py:451
  116.7 4.3 %all-to-all-start = ((f32[32,96,128]{2,1,0:T(8,128)}), f32[32,96,128]{2,1,0:T(8,128)S(1)}, u32[]{:S(2)}, u32[]{:S(2)}) async-start(f32[32,96,128]{2,1,0:T(8,128)} %copy-done.2), calls=%async_computation | async-start | bytes 3145728 | tf_op jit(solution)/shard_map/all_to_all | solution.py:451
  121.3 1.2 copy-done.4
  122.5 3.5 %gram.2 = (f32[896,128]{1,0:T(8,128)S(1)}, bf16[2304,416]{1,0:T(8,128)(2,1)S(1)}) custom-call(f32[96,128]{1,0:T(8,128)S(1)} %copy.19.factor_ref, f32[2048,128]{1,0:T(8,128)S(1)} %bitcast.25, f32[3072,128]{1,0:T(8,128)S(1)} %bitcast.24), custom_call_target="tpu_custom_call" | custom-call | flops 797442048 | bytes 8388608 | tf_op jit(solution)/shard_map/gram/pallas_call | solution.py:246
  126.0 1.4 copy-done
  128.2 15.6 %all-to-all-done = f32[32,96,128]{2,1,0:T(8,128)S(1)} async-done(((f32[32,96,128]{2,1,0:T(8,128)}), f32[32,96,128]{2,1,0:T(8,128)S(1)}, u32[]{:S(2)}, u32[]{:S(2)}) %all-to-all-start) | async-done | bytes 1572896 | tf_op jit(solution)/shard_map/all_to_all | solution.py:451
  143.8 1.7 copy-done.1
  146.5 2.9 %gram.3 = (f32[1024,128]{1,0:T(8,128)S(1)}, f32[1024,128]{1,0:T(8,128)S(1)}) custom-call(s32[1]{0:T(128)} %bitcast.me_ref.core_ref, f32[96,128]{1,0:T(8,128)S(1)} %copy.19.factor_ref, f32[3072,128]{1,0:T(8,128)S(1)} %bitcast.21, bf16[2304,416]{1,0:T(8,128)(2,1)S(1)} %copy-done.1, f32[896,128]{1,0:T(8,128)S(1)} %copy-done.6), custom_call_target="tpu_custom_call" | custom-call | flops 1189085184 | bytes 8388608 | tf_op jit(solution)/shard_map/gram/pallas_call | solution.py:246
  150.2 1.5 collective-permute-done.9
  151.8 17.5 %all_to_all.25.x_ref = f32[64,16,128]{2,1,0:T(8,128)S(1)} all-to-all(f32[64,16,128]{2,1,0:T(8,128)S(1)} %bitcast.31), channel_id=1, replica_groups=mesh['y'=4,'z'=4,'core'=2,'narrow'=4] {'y','z','narrow'}, dimensions={0} | all-to-all | bytes 1048576 | tf_op jit(solution)/shard_map/all_to_all | solution.py:461
  169.4 15.4 %all_to_all.26 = f32[64,16,128]{2,1,0:T(8,128)S(1)} all-to-all(f32[64,16,128]{2,1,0:T(8,128)S(1)} %add.13), channel_id=1, replica_groups=mesh['y'=4,'z'=4,'core'=2,'narrow'=4] {'y','z','narrow'}, dimensions={0} | all-to-all | bytes 1048576 | tf_op jit(solution)/shard_map/all_to_all | solution.py:462
  184.8 3.3 %collective-permute-start.10 = (f32[1024,128]{1,0:T(8,128)S(1)}, f32[1024,128]{1,0:T(8,128)S(1)}, u32[]{:S(2)}, u32[]{:S(2)}) collective-permute-start(f32[1024,128]{1,0:T(8,128)S(1)} %bitcast.22), channel_id=1, source_target_pairs={{0,4},{4,0},{1,5},{5,1},{2,6},{6,2},{3,7},{7,3},{8,12},{12,8},{9,1... | collective-permute-start | bytes 1572872 | tf_op jit(solution)/shard_map/ppermute | solution.py:463
  188.1 1.5 collective-permute-done.10.other_ref
  189.6 33.8 %sweeps.1 = f32[96,672]{1,0:T(8,128)} custom-call(s32[1]{0:T(128)} %bitcast.me_ref.core_ref, f32[1024,128]{1,0:T(8,128)S(1)} %bitcast.23, f32[1024,128]{1,0:T(8,128)S(1)} %collective-permute-done.10.other_ref, f32[96,672]{1,0:T(8,128)S(1)} %bitcast.26), custom_call_target="tpu_custom_call" | custom-call | tf_op jit(solution)/shard_map/sweeps/pallas_call | solution.py:402
  (40 shorter events, 6.4 us)
Async XLA Ops:
  0.9 9.5 %copy-start.9 = (f32[32,16]{0,1:T(8,128)S(1)}, f32[32,16]{0,1:T(8,128)}, u32[]{:S(2)}) copy-start(f32[32,16]{0,1:T(8,128)} %param.8) | copy-start | bytes 6148
  5.4 23.1 %collective-permute-start = (f32[8,24,640]{2,1,0:T(8,128)}, f32[8,24,640]{2,1,0:T(8,128)}, u32[]{:S(2)}, u32[]{:S(2)}) collective-permute-start(f32[8,24,640]{2,1,0:T(8,128)} %get-tuple-element.33), channel_id=1, source_target_pairs={{0,1},{1,2},{2,3},{3,0},{4,5},{5,6},{6,7},{7,4},{8,9},{9,10},{10,1... | collective-permute-start | bytes 1474568 | tf_op jit(solution)/shard_map/ppermute | solution.py:438
  7.4 21.1 %collective-permute-start.1 = (f32[8,24,640]{2,1,0:T(8,128)}, f32[8,24,640]{2,1,0:T(8,128)}, u32[]{:S(2)}, u32[]{:S(2)}) collective-permute-start(f32[8,24,640]{2,1,0:T(8,128)} %get-tuple-element.34), channel_id=1, source_target_pairs={{0,3},{1,0},{2,1},{3,2},{4,7},{5,4},{6,5},{7,6},{8,11},{9,8},{10,9... | collective-permute-start | bytes 1474568 | tf_op jit(solution)/shard_map/ppermute | solution.py:438
  8.7 22.7 %collective-permute-start.7 = (f32[8,24,640]{2,1,0:T(8,128)}, f32[8,24,640]{2,1,0:T(8,128)}, u32[]{:S(2)}, u32[]{:S(2)}) collective-permute-start(f32[8,24,640]{2,1,0:T(8,128)} %get-tuple-element.51), channel_id=1, source_target_pairs={{0,2},{1,3},{2,0},{3,1},{4,6},{5,7},{6,4},{7,5},{8,10},{9,11},{10,... | collective-permute-start | bytes 1474568 | tf_op jit(solution)/shard_map/ppermute | solution.py:438
  28.5 19.9 %collective-permute-start.2 = (f32[8,24,1024]{2,1,0:T(8,128)}, f32[8,24,1024]{2,1,0:T(8,128)}, u32[]{:S(2)}, u32[]{:S(2)}) collective-permute-start(f32[8,24,1024]{2,1,0:T(8,128)} %get-tuple-element.39), channel_id=1, source_target_pairs={{0,1},{1,2},{2,3},{3,0},{4,5},{5,6},{6,7},{7,4},{8,9},{9,10},{10,1... | collective-permute-start | bytes 2359304 | tf_op jit(solution)/shard_map/ppermute | solution.py:438
  29.0 19.5 %collective-permute-start.3 = (f32[8,24,1024]{2,1,0:T(8,128)}, f32[8,24,1024]{2,1,0:T(8,128)}, u32[]{:S(2)}, u32[]{:S(2)}) collective-permute-start(f32[8,24,1024]{2,1,0:T(8,128)} %get-tuple-element.40), channel_id=1, source_target_pairs={{0,3},{1,0},{2,1},{3,2},{4,7},{5,4},{6,5},{7,6},{8,11},{9,8},{10,9... | collective-permute-start | bytes 2359304 | tf_op jit(solution)/shard_map/ppermute | solution.py:438
  31.3 30.3 %collective-permute-start.8 = (f32[8,24,1024]{2,1,0:T(8,128)}, f32[8,24,1024]{2,1,0:T(8,128)}, u32[]{:S(2)}, u32[]{:S(2)}) collective-permute-start(f32[8,24,1024]{2,1,0:T(8,128)} %get-tuple-element.55), channel_id=1, source_target_pairs={{0,2},{1,3},{2,0},{3,1},{4,6},{5,7},{6,4},{7,5},{8,10},{9,11},{10,... | collective-permute-start | bytes 2359304 | tf_op jit(solution)/shard_map/ppermute | solution.py:438
  35.4 30.4 %all-to-all-start.1 = ((f32[32,64,128]{2,1,0:T(8,128)}), f32[32,64,128]{2,1,0:T(8,128)S(1)}, u32[]{:S(2)}, u32[]{:S(2)}) async-start(f32[32,64,128]{2,1,0:T(8,128)} %species.4), calls=%async_computation.1 | async-start | bytes 2097152 | tf_op jit(solution)/shard_map/all_to_all | solution.py:451
  48.5 45.6 %collective-permute-start.4 = (f32[8,24,1024]{2,1,0:T(8,128)}, f32[8,24,1024]{2,1,0:T(8,128)}, u32[]{:S(2)}, u32[]{:S(2)}) collective-permute-start(f32[8,24,1024]{2,1,0:T(8,128)} %get-tuple-element.46), channel_id=1, source_target_pairs={{0,1},{1,2},{2,3},{3,0},{4,5},{5,6},{6,7},{7,4},{8,9},{9,10},{10,1... | collective-permute-start | bytes 2359304 | tf_op jit(solution)/shard_map/ppermute | solution.py:438
  49.7 44.4 %collective-permute-start.5 = (f32[8,24,1024]{2,1,0:T(8,128)}, f32[8,24,1024]{2,1,0:T(8,128)}, u32[]{:S(2)}, u32[]{:S(2)}) collective-permute-start(f32[8,24,1024]{2,1,0:T(8,128)} %get-tuple-element.47), channel_id=1, source_target_pairs={{0,2},{1,3},{2,0},{3,1},{4,6},{5,7},{6,4},{7,5},{8,10},{9,11},{10,... | collective-permute-start | bytes 2359304 | tf_op jit(solution)/shard_map/ppermute | solution.py:438
  50.4 43.6 %collective-permute-start.6 = (f32[8,24,1024]{2,1,0:T(8,128)S(1)}, f32[8,24,1024]{2,1,0:T(8,128)}, u32[]{:S(2)}, u32[]{:S(2)}) collective-permute-start(f32[8,24,1024]{2,1,0:T(8,128)S(1)} %get-tuple-element.48), channel_id=1, source_target_pairs={{0,3},{1,0},{2,1},{3,2},{4,7},{5,4},{6,5},{7,6},{8,11},{9,8},{10,9... | collective-permute-start | bytes 2359304 | tf_op jit(solution)/shard_map/ppermute | solution.py:438
  65.8 1.0 copy-start.3
  66.7 50.0 %all-to-all-start.2 = ((f32[32,96,128]{2,1,0:T(8,128)}), f32[32,96,128]{2,1,0:T(8,128)S(1)}, u32[]{:S(2)}, u32[]{:S(2)}) async-start(f32[32,96,128]{2,1,0:T(8,128)} %species.5), calls=%async_computation.2 | async-start | bytes 3145728 | tf_op jit(solution)/shard_map/all_to_all | solution.py:451
  97.2 1.2 copy-start.2
  98.4 22.7 %copy-start.8 = (f32[128,96]{0,1:T(8,128)S(1)}, f32[128,96]{0,1:T(8,128)}, u32[]{:S(2)}) copy-start(f32[128,96]{0,1:T(8,128)} %param.6) | copy-start | bytes 147460
  116.7 27.1 %all-to-all-start = ((f32[32,96,128]{2,1,0:T(8,128)}), f32[32,96,128]{2,1,0:T(8,128)S(1)}, u32[]{:S(2)}, u32[]{:S(2)}) async-start(f32[32,96,128]{2,1,0:T(8,128)} %copy-done.2), calls=%async_computation | async-start | bytes 3145728 | tf_op jit(solution)/shard_map/all_to_all | solution.py:451
  121.3 1.2 copy-start.4
  126.0 1.4 copy-start
  127.4 0.8 copy-start.5
  143.8 1.7 copy-start.1
  145.5 1.0 copy-start.6
  149.4 2.3 %collective-permute-start.9 = (f32[1024,128]{1,0:T(8,128)S(1)}, f32[1024,128]{1,0:T(8,128)S(1)}, u32[]{:S(2)}, u32[]{:S(2)}) collective-permute-start(f32[1024,128]{1,0:T(8,128)S(1)} %get-tuple-element.60), channel_id=1, source_target_pairs={{0,4},{4,0},{1,5},{5,1},{2,6},{6,2},{3,7},{7,3},{8,12},{12,8},{9,1... | collective-permute-start | bytes 1572872 | tf_op jit(solution)/shard_map/ppermute | solution.py:458
  151.7 37.9 %copy-start.7 = (f32[672,96]{0,1:T(8,128)S(1)}, f32[672,96]{0,1:T(8,128)}, u32[]{:S(2)}) copy-start(f32[672,96]{0,1:T(8,128)} %param.9) | copy-start | bytes 774148
  184.8 4.8 %collective-permute-start.10 = (f32[1024,128]{1,0:T(8,128)S(1)}, f32[1024,128]{1,0:T(8,128)S(1)}, u32[]{:S(2)}, u32[]{:S(2)}) collective-permute-start(f32[1024,128]{1,0:T(8,128)S(1)} %bitcast.22), channel_id=1, source_target_pairs={{0,4},{4,0},{1,5},{5,1},{2,6},{6,2},{3,7},{7,3},{8,12},{12,8},{9,1... | collective-permute-start | bytes 1572872 | tf_op jit(solution)/shard_map/ppermute | solution.py:463

commit v4 on v3

--- a/solution.py
+++ b/solution.py
@@ -25,9 +25,14 @@
 TAIL = I1 - FULL * LANES
 BODY = FULL * LANES
 LOCAL2 = I2 // WIDE
-RANKS = R3 // NARROW
+WIDE_RANKS = WIDE
+NARROW_RANKS = R3 - WIDE_RANKS
+RANKS = NARROW_RANKS // NARROW
 PAIRS = RANKS * R4 // WIDE
-CHUNKS = ((4,), (0, 1), (2, 3))
+SPECIES = 32
+LOCAL4 = SPECIES // NARROW
+SHARE = R2 // NARROW
+CHUNKS = ((0, 1, 4), (2, 3))
 EARLY = 3 * LANES + TAIL
 LATE = 2 * LANES
 EARLY_TILES = ((0, 0), (0, 1), (1, 1), (0, 4), (1, 4), (4, 4))
@@ -67,47 +72,52 @@
 
 
 def mode3_kernel(factor_ref, *refs):
-    outs, slabs = refs[-NARROW:], refs[:-NARROW]
+    outs, rest_out, slabs = refs[-NARROW - 1:-1], refs[-1], refs[:-NARROW - 1]
     f_high, f_low = split(factor_ref[...])
     lanes = ((1,), (1,))
-    for s in range(outs[0].shape[0]):
-        rows = [slab[s].reshape(-1, I3) for slab in slabs]
-        rows = rows[0] if len(rows) == 1 else jnp.concatenate(rows, axis=0)
+    some = outs[0].shape[0]
+    stride = rest_out.shape[0] // WIDE
+    for s in range(some):
+        rows = jnp.concatenate([slab[s].reshape(-1, I3) for slab in slabs], axis=0)
         r_high, r_low = split(rows)
         both = product(jnp.concatenate([f_high, f_low], axis=0), r_high, lanes)
         done = both[:R3] + both[R3:] + product(f_high, r_low, lanes)
         for j, out in enumerate(outs):
             out[s] = done[j * RANKS:(j + 1) * RANKS]
+        place = pl.program_id(0) * some + s
+        for u in range(stride // LOCAL4):
+            rest_out[pl.ds(u * LOCAL4 + place, WIDE, stride=stride), :] = done[
+                NARROW_RANKS:, u * LANES:(u + 1) * LANES]
 
 
 def mode3(field, factor_rows, chunk):
     species = field.shape[0]
     count = len(chunk)
-    index = chunk[0] // count
     width = LOCAL2 * LANES * count
-    some = species // 2 // count
-    in_specs = [
-        pl.BlockSpec((R3, I3), lambda s: (0, 0)),
-        pl.BlockSpec((some, LOCAL2, LANES * count, I3), lambda s: (s, 0, index, 0)),
-    ]
-    args = [factor_rows, field]
+    some = 2
+    in_specs = [pl.BlockSpec((R3, I3), lambda s: (0, 0))]
+    for tile in chunk:
+        in_specs.append(pl.BlockSpec((some, LOCAL2, LANES, I3), lambda s, tile=tile: (s, 0, tile, 0)))
     if chunk == CHUNKS[0]:
         width += LANES
         in_specs.append(pl.BlockSpec((some, LOCAL2, TAIL, I3), lambda s: (s, 0, BODY // TAIL, 0)))
-        args.append(field)
+    args = [factor_rows] + [field] * (len(in_specs) - 1)
     shape = jax.ShapeDtypeStruct((species, RANKS, width), jnp.float32)
-    return pl.pallas_call(
+    rest = (WIDE * species * width // LANES, LANES)
+    out = pl.pallas_call(
         mode3_kernel,
         grid=(species // some,),
         in_specs=in_specs,
-        out_specs=[pl.BlockSpec((some, RANKS, width), lambda s: (s, 0, 0))] * NARROW,
-        out_shape=[shape] * NARROW,
+        out_specs=[pl.BlockSpec((some, RANKS, width), lambda s: (s, 0, 0))] * NARROW
+        + [pl.BlockSpec(rest, lambda s: (0, 0))],
+        out_shape=[shape] * NARROW + [jax.ShapeDtypeStruct(rest, jnp.float32)],
         compiler_params=pltpu.CompilerParams(vmem_limit_bytes=48 << 20),
         cost_estimate=pl.CostEstimate(
             flops=6 * species * R3 * I3 * width,
             bytes_accessed=4 * species * width * (I3 + R3), transcendentals=0),
         name="mode3",
     )(*args)
+    return out[:NARROW], out[NARROW].reshape(WIDE, -1, LANES)
 
 
 def species_kernel(tiles, weights_ref, *refs):
@@ -115,36 +125,16 @@
     step = pl.program_id(0)
     rows = [p[...].reshape(-1, tiles * LANES) for p in parts]
     done = left_product(weights_ref[...], jnp.concatenate(rows, axis=0))
-
-    def put(dest, first, q, start, count):
+    for q in range(R4):
         for t in range(tiles):
-            out[dest, t * PAIRS + first:t * PAIRS + first + count, :] = done[
-                q * 8 + start:q * 8 + start + count, t * LANES:(t + 1) * LANES]
-
-    @pl.when(step == 0)
-    def _():
-        spare = out.shape[1] - tiles * PAIRS
-        if spare:
-            out[:, tiles * PAIRS:, :] = jnp.zeros((WIDE, spare, LANES), jnp.float32)
-        for q in range(R4):
-            put(2 * q, 0, q, 0, 8)
-
-    @pl.when(step == 1)
-    def _():
-        for q in range(R4):
-            put(2 * q, 8, q, 0, 4)
-            put(2 * q + 1, 0, q, 4, 4)
-
-    @pl.when(step == 2)
-    def _():
-        for q in range(R4):
-            put(2 * q + 1, 4, q, 0, 8)
-
-
-def species_sum(parts, weights):
+            out[2 * q + step, t * PAIRS:(t + 1) * PAIRS, :] = done[
+                q * 8:(q + 1) * 8, t * LANES:(t + 1) * LANES]
+
+
+def species_sum(parts, weights, cost):
     species, ranks, width = parts[0].shape
     tiles = width // LANES
-    rows = -(-tiles * PAIRS // 8) * 8
+    rows = tiles * PAIRS
     return pl.pallas_call(
         functools.partial(species_kernel, tiles),
         grid=(ranks // 8,),
@@ -152,11 +142,103 @@
         + [pl.BlockSpec((species, 8, width), lambda i: (0, i, 0))] * NARROW,
         out_specs=pl.BlockSpec((WIDE, rows, LANES), lambda i: (0, 0, 0)),
         out_shape=jax.ShapeDtypeStruct((WIDE, rows, LANES), jnp.float32),
-        compiler_params=pltpu.CompilerParams(vmem_limit_bytes=20 << 20),
+        compiler_params=pltpu.CompilerParams(vmem_limit_bytes=24 << 20),
         cost_estimate=pl.CostEstimate(
-            flops=SPECIES_COST, bytes_accessed=4 * width * 24 * 48, transcendentals=0),
+            flops=cost, bytes_accessed=4 * width * 24 * 48, transcendentals=0),
         name="species",
     )(weights, *parts)
+
+
+def place_of(tile, b):
+    if tile in CHUNKS[0]:
+        return CHUNKS[0].index(tile) * LOCAL2 + b
+    return len(CHUNKS[0]) * LOCAL2 + 1 + CHUNKS[1].index(tile) * LOCAL2 + b
+
+
+def mode2_kernel(factor_ref, part_ref, *outs):
+    f_high, f_low = split(factor_ref[...])
+    doubled = jnp.concatenate([f_high, f_high], axis=1)
+    stride = part_ref.shape[0] // WIDE
+    tails = []
+    for s in range(LOCAL4):
+        def piece(place):
+            return part_ref[pl.ds(place * LOCAL4 + s, WIDE, stride=stride), :]
+
+        last = piece(len(CHUNKS[0]) * LOCAL2)
+        cells = [
+            jnp.concatenate([piece(place_of(t, b)) for t in range(FULL)]
+                            + [last[:, b * TAIL:(b + 1) * TAIL]], axis=1)
+            for b in range(LOCAL2)]
+        v_high, v_low = split(jnp.concatenate(cells, axis=0))
+        core = product(doubled, jnp.concatenate([v_high, v_low], axis=0), ((1,), (0,)))
+        core = core + product(f_low, v_high, ((1,), (0,)))
+        for j, out in enumerate(outs):
+            rows = core[j * SHARE:(j + 1) * SHARE]
+            for t in range(FULL):
+                out[(s * FULL + t) * SHARE:(s * FULL + t + 1) * SHARE, :] = rows[:, t * LANES:(t + 1) * LANES]
+        tails.append(core[:, BODY:])
+        if s % 4 == 3:
+            four = jnp.concatenate(tails[-4:], axis=1)
+            start = (LOCAL4 * FULL + s // 4) * SHARE
+            for j, out in enumerate(outs):
+                out[start:start + SHARE, :] = four[j * SHARE:(j + 1) * SHARE]
+
+
+def mode2_sum(part, factor_rows):
+    rows = (LOCAL4 * FULL + LOCAL4 // 4) * SHARE
+    shape = jax.ShapeDtypeStruct((rows, LANES), jnp.float32)
+    args = [factor_rows, part]
+    return pl.pallas_call(
+        mode2_kernel, grid=(1,), in_specs=[whole(x) for x in args],
+        out_specs=[whole(shape)] * NARROW, out_shape=[shape] * NARROW,
+        compiler_params=pltpu.CompilerParams(vmem_limit_bytes=24 << 20),
+        cost_estimate=pl.CostEstimate(
+            flops=SPECIES_COST, bytes_accessed=6 << 20, transcendentals=0),
+        name="mode2",
+    )(*args)
+
+
+def other_gram_kernel(weights_ref, *refs):
+    parts, (out, high_ref, low_ref) = refs[:NARROW], refs[NARROW:]
+    for block in range(SHARE // 8):
+        rows = []
+        for part in parts:
+            for s in range(LOCAL4):
+                def piece(n):
+                    return part[n * SHARE + block * 8:n * SHARE + block * 8 + 8, :]
+
+                tail = piece(LOCAL4 * FULL + s // 4)
+                rows.append(jnp.concatenate(
+                    [piece(s * FULL + t) for t in range(FULL)]
+                    + [tail[:, s % 4 * TAIL:(s % 4 + 1) * TAIL]], axis=1))
+        high, low = split(left_product(weights_ref[...], jnp.concatenate(rows, axis=0)))
+        here = slice(block * R4 * 8, (block + 1) * R4 * 8)
+        high_ref[here, :] = high
+        low_ref[here, :] = low
+
+    def inner(left, right):
+        return inner_product(high_ref[:, left], low_ref[:, left], high_ref[:, right], low_ref[:, right])
+
+    top = inner(slice(0, 256), slice(0, I1))
+    middle = inner(slice(256, 512), slice(256, 512))
+    below = inner(slice(512, I1), slice(256, I1))
+    grid = {(i, j): tile_of(top, i, j) for i in range(2) for j in range(FULL)}
+    grid.update({(2 + i, 2 + j): tile_of(middle, i, j) for i in range(2) for j in range(2)})
+    grid.update({(4, 2 + j): tile_of(below, 0, j) for j in range(3)})
+    for n, pair in enumerate(EARLY_TILES + (None,) + LATE_TILES):
+        if pair is not None:
+            out[n * LANES:(n + 1) * LANES, :] = grid[pair]
+    put_edges(out, len(EARLY_TILES) * LANES, [top[:LANES, BODY:], top[LANES:, BODY:], below[:LANES, 256 + LANES:]],
+              below[LANES:, 256 + LANES:])
+    put_left(out, (len(EARLY_TILES) + 1) * LANES, below[LANES:, :256])
+
+
+def other_gram(parts, weights):
+    rows = SHARE * R4
+    out = jax.ShapeDtypeStruct((16 * LANES, LANES), jnp.float32)
+    args = [weights, *parts]
+    half = pltpu.VMEM((rows, I1), jnp.bfloat16)
+    return gram_call(other_gram_kernel, args, out, [half, half], 2 * SPECIES_COST)
 
 
 def core_columns(factor, parts, store):
@@ -171,7 +253,7 @@
         for b in range(LOCAL2):
             row = []
             for ref, count, tail in parts:
-                row += [piece(ref, (b * count + t) * PAIRS + i) for t in range(count)]
+                row += [piece(ref, (t * LOCAL2 + b) * PAIRS + i) for t in range(count)]
                 if tail:
                     last = piece(ref, LOCAL2 * count * PAIRS + i)
                     row.append(last[:, b * TAIL:(b + 1) * TAIL])
@@ -186,18 +268,30 @@
     return product(a_high, b_high, rows) + product(a_high, b_low, rows) + product(a_low, b_high, rows)
 
 
+def put_edges(out, place, edges, corner):
+    edges = edges + [jnp.concatenate([corner] * (LANES // TAIL), axis=0)]
+    out[place:place + LANES, :] = jnp.concatenate(edges, axis=1)
+
+
+def put_left(out, place, left):
+    for j, n in ((0, 6), (1, 8)):
+        corner = place + n * LANES + 64
+        out[corner:corner + TAIL, :64] = left[:, j * LANES:j * LANES + 64]
+        out[corner + TAIL:corner + 2 * TAIL, :64] = left[:, j * LANES + 64:(j + 1) * LANES]
+
+
 def tile_of(block, i, j):
     return block[i * LANES:(i + 1) * LANES, j * LANES:(j + 1) * LANES]
 
 
-def gram_first_kernel(factor_ref, edge_ref, part_ref, out, core_ref):
+def gram_first_kernel(factor_ref, part_ref, out, core_ref):
     half = PAIRS * R2
 
     def store(i, high, low):
         core_ref[i * R2:(i + 1) * R2, :] = high
         core_ref[half + i * R2:half + (i + 1) * R2, :] = low
 
-    core_columns(factor_ref[...], ((part_ref, 2, False), (edge_ref, 1, True)), store)
+    core_columns(factor_ref[...], ((part_ref, 3, True),), store)
     two = slice(0, LATE)
     rest = slice(LATE, EARLY)
     top = inner_product(core_ref[:half, two], core_ref[half:, two], core_ref[:half, :], core_ref[half:, :])
@@ -207,13 +301,11 @@
              tile_of(top, 0, 2), tile_of(top, 1, 2), own[:LANES, :LANES]]
     for n, tile in enumerate(tiles):
         out[n * LANES:(n + 1) * LANES, :] = tile
-    edges = [top[:LANES, 3 * LANES:], top[LANES:, 3 * LANES:], own[:LANES, LANES:]]
-    corner = own[LANES:, LANES:]
-    edges.append(jnp.concatenate([corner] * (LANES // TAIL), axis=0))
-    out[len(tiles) * LANES:, :] = jnp.concatenate(edges, axis=1)
-
-
-def gram_last_kernel(me_ref, factor_ref, part_ref, core_ref, early_ref, keep, give, high_ref, low_ref, out):
+    put_edges(out, len(tiles) * LANES,
+              [top[:LANES, 3 * LANES:], top[LANES:, 3 * LANES:], own[:LANES, LANES:]], own[LANES:, LANES:])
+
+
+def gram_last_kernel(me_ref, factor_ref, part_ref, core_ref, early_ref, other_ref, keep, give, high_ref, low_ref, out):
     half = PAIRS * R2
 
     def store(i, high, low):
@@ -230,15 +322,12 @@
     tiles += [tile_of(own, 0, 0), tile_of(own, 0, 1), tile_of(own, 1, 1)]
     for n, tile in enumerate(tiles):
         out[place + n * LANES:place + (n + 1) * LANES, :] = tile
-    left = above[3 * LANES:, :]
-    for j, n in ((0, 6), (1, 8)):
-        corner = place + n * LANES + 64
-        out[corner:corner + TAIL, :64] = left[:, j * LANES:j * LANES + 64]
-        out[corner + TAIL:corner + 2 * TAIL, :64] = left[:, j * LANES + 64:(j + 1) * LANES]
+    put_left(out, place, above[3 * LANES:, :])
     rows = keep.shape[0]
     me = me_ref[0]
-    keep[...] = out[pl.ds(pl.multiple_of(me * rows, rows), rows), :]
-    give[...] = out[pl.ds(pl.multiple_of((1 - me) * rows, rows), rows), :]
+    for ref, core in ((keep, me), (give, 1 - me)):
+        here = pl.ds(pl.multiple_of(core * rows, rows), rows)
+        ref[...] = out[here, :] + other_ref[here, :]
 
 
 def gram_call(kernel, args, out_shape, scratch, flops):
@@ -248,25 +337,25 @@
         in_specs=[pl.BlockSpec(memory_space=pltpu.SMEM) if x.ndim == 1 else whole(x) for x in args],
         out_specs=[whole(x) for x in out_shape] if some else whole(out_shape),
         out_shape=out_shape, scratch_shapes=scratch,
-        compiler_params=pltpu.CompilerParams(vmem_limit_bytes=48 << 20),
+        compiler_params=pltpu.CompilerParams(vmem_limit_bytes=24 << 20),
         cost_estimate=pl.CostEstimate(flops=flops, bytes_accessed=8 << 20, transcendentals=0),
         name="gram",
     )(*args)
 
 
-def gram_first(parts, factor_rows):
+def gram_first(part, factor_rows):
     rows = PAIRS * R2
     return gram_call(
-        gram_first_kernel, [factor_rows, *parts],
+        gram_first_kernel, [factor_rows, part],
         [jax.ShapeDtypeStruct(((len(EARLY_TILES) + 1) * LANES, LANES), jnp.float32),
          jax.ShapeDtypeStruct((2 * rows, EARLY), jnp.bfloat16)],
         [], 4 * rows * EARLY * EARLY)
 
 
-def gram_last(me, part, core, early, factor_rows):
+def gram_last(me, part, core, early, other, factor_rows):
     half = pltpu.VMEM((PAIRS * R2, LATE), jnp.bfloat16)
     return gram_call(
-        gram_last_kernel, [me, factor_rows, part, core, early],
+        gram_last_kernel, [me, factor_rows, part, core, early, other],
         [jax.ShapeDtypeStruct((8 * LANES, LANES), jnp.float32)] * 2,
         [half, half, pltpu.VMEM((16 * LANES, LANES), jnp.float32)],
         6 * PAIRS * R2 * I1 * LATE)
@@ -412,9 +501,11 @@
 
 
 def factors(mode2_factor, mode3_factor, mode4_factor, me):
-    turned = jnp.transpose(mode3_factor)
+    ranks = jnp.transpose(mode3_factor)
+    turned = ranks[:NARROW_RANKS]
     turned = lax.dynamic_slice_in_dim(
-        jnp.concatenate([turned, turned], axis=0), me * RANKS, R3, 0)
+        jnp.concatenate([turned, turned], axis=0), me * RANKS, NARROW_RANKS, 0)
+    turned = jnp.concatenate([turned, ranks[NARROW_RANKS:]], axis=0)
     species = mode4_factor.shape[0]
     local = species // NARROW
     blocks = mode4_factor.reshape(NARROW, local, R4)[::-1].reshape(species, R4)
@@ -423,12 +514,14 @@
     weights = jnp.transpose(blocks)[:, None, :, None] * jnp.eye(8, dtype=jnp.float32)[None, :, None, :]
     weights = weights.reshape(R4 * 8, species * 8)
     cells = jnp.transpose(mode2_factor.reshape(WIDE, LOCAL2, R2), (2, 1, 0)).reshape(R2, I2)
-    return turned, weights, cells
+    shares = lax.dynamic_slice_in_dim(
+        jnp.concatenate([cells, cells], axis=0), me * SHARE, R2, 0)
+    return turned, weights, cells, shares
 
 
 def body(tensor, mode2_factor, mode3_factor, mode4_factor, start_basis):
     me = lax.axis_index("narrow")
-    turned, weights, cells = factors(mode2_factor, mode3_factor, mode4_factor, me)
+    turned, weights, cells, shares = factors(mode2_factor, mode3_factor, mode4_factor, me)
     field = jnp.transpose(tensor, (0, 1, 3, 2))
 
     def send(blocks):
@@ -438,23 +531,27 @@
             got[j] = lax.ppermute(blocks[j], "narrow", ring)
         return got
 
-    count = len(CHUNKS)
-    got = send(mode3(field, turned, CHUNKS[0]))
-    parts = []
-    for index in range(count):
-        if index + 1 < count:
-            blocks = mode3(field, turned, CHUNKS[index + 1])
-            near = [got[1], got[3]]
-            near, blocks = lax.optimization_barrier((near, blocks))
-            got[1], got[3] = near
-            coming = send(blocks)
-        sums = lax.all_to_all(species_sum(got, weights), WIDE_AXES, 0, 0, tiled=True)
-        got = coming
-        parts.append(sums.reshape(-1, LANES))
-    early, core = gram_first(parts[:-1], cells)
+    def wide_exchange(x):
+        return lax.all_to_all(x, WIDE_AXES, 0, 0, tiled=True).reshape(-1, LANES)
+
+    blocks, rest = mode3(field, turned, CHUNKS[0])
+    first = send(blocks)
+    blocks, more = mode3(field, turned, CHUNKS[1])
+    raw = wide_exchange(jnp.concatenate([rest, more], axis=1))
+    first, blocks = lax.optimization_barrier((first, blocks))
+    second = send(blocks)
+    sums = species_sum(first, weights, SPECIES_COST)
+    raw, sums = lax.optimization_barrier((raw, sums))
+    part = wide_exchange(sums)
+    shared = mode2_sum(raw, shares)
+    second, shared = lax.optimization_barrier((second, shared))
+    third = send(shared)
+    last = wide_exchange(species_sum(second, weights, 10 ** 9))
+    early, core = gram_first(part, cells)
+    other = other_gram(third, weights)
     core_index = lax.axis_index("core").reshape(1)
     swap = [(0, 1), (1, 0)]
-    keep, give = gram_last(core_index, parts[-1], core, early, cells)
+    keep, give = gram_last(core_index, last, core, early, other, cells)
     half = keep + lax.ppermute(give, "core", swap)
     chips = ("y", "z", "narrow")
     half = half.reshape(CHIPS, -1, LANES)

time: 224 us -> 200 us (0.89)
  starting transfers between devices: 60.5 us -> 36.4 us
  Pallas kernels: 69.5 us -> 65.2 us
  waiting for transfers between devices: 46.2 us -> 49.9 us
    all_to_all x3, starting transfers between devices: 44.7 us -> 20 us  [wide_exchange(): return lax.all_to_all(x, WIDE_AXES, 0, 0, tiled=True).reshape(-1, LANES)]
    pallas_call x3 -> x2, Pallas kernels: 11.3 us -> 5.28 us  [species_sum(): pl.pallas_call(functools.partial(species_kernel, tiles), grid=(ranks // 8...]
    pallas_call x3 -> x2, Pallas kernels: 17.9 us -> 14.6 us  [mode3(): pl.pallas_call(mode3_kernel, grid=(species // some,), in_specs=in_specs,...]
    pallas_call x0 -> x1, Pallas kernels: none -> 2.5 us  [mode2_sum(): pl.pallas_call(mode2_kernel, grid=(1,), in_specs=[whole(x) for x in args]...]
    pallas_call x2 -> x3, Pallas kernels: 6.38 us -> 8.87 us  [gram_call(): pl.pallas_call(kernel, grid=(1,), in_specs=[pl.BlockSpec(memory_space=plt...]
    unnamed x22 -> x28, local copies, waits for them, and re-layouts: 8.42 us -> 7.75 us
  transfers between devices with their start and end apart: 14 -> 14, of which waited for: 5 -> 6; matrix products, arithmetic and copies ran while one was open for 2% -> 3% of each run, Pallas kernels for 13% -> 10%
where the time goes in v4:
time: 200 us
  Pallas kernels  65.2 us (33%)
  waiting for transfers between devices  49.9 us (25%)
  starting transfers between devices  36.4 us (18%)
  blocking collectives  32 us (16%)
  local copies, waits for them, and re-layouts  12.3 us (6%)
  other arithmetic  3.59 us (2%)
    all_to_all x3, waiting for transfers between devices, wide_exchange(): return lax.all_to_all(x, WIDE_AXES, 0, 0, tiled=True).reshape(-1, LANES)  35.6 us
    pallas_call x1, Pallas kernels, sweeps(): pl.pallas_call(sweep_kernel, in_specs=[pl.BlockSpec(memory_space=pltpu.SM...  33.8 us
    all_to_all x3, starting transfers between devices, wide_exchange(): return lax.all_to_all(x, WIDE_AXES, 0, 0, tiled=True).reshape(-1, LANES)  20 us
    all_to_all x1, blocking collectives, body(): half = add_parts(lax.all_to_all(half, chips, 0, 0, tiled=True))  16.5 us
    all_to_all x1, blocking collectives, body(): mine = lax.all_to_all(half, chips, 0, 0, tiled=True).reshape(-1, LANES)  15.4 us
    pallas_call x2, Pallas kernels, mode3(): pl.pallas_call(mode3_kernel, grid=(species // some,), in_specs=in_specs,...  14.6 us
    ppermute x9, starting transfers between devices, send(): got[j] = lax.ppermute(blocks[j], 'narrow', ring)  12.9 us
    ppermute x9, waiting for transfers between devices, send(): got[j] = lax.ppermute(blocks[j], 'narrow', ring)  10.9 us
  transfers between devices with their start and end apart: 14, of which 6 were waited for; matrix products, arithmetic and copies ran while one was open for 3% of the time, Pallas kernels for 10%

profile of v4, /device:TPU:1, one launch (start us, length us, event | category | flops | bytes accessed | tf_op | source)
XLA Modules:
  0.0 199.6 jit_solution(17754309673321313276)
XLA Ops:
  1.6 8.7 %mode3.2 = (f32[8,16,1664]{2,1,0:T(8,128)S(1)}, f32[8,16,1664]{2,1,0:T(8,128)}, f32[8,16,1664]{2,1,0:T(8,128)}, f32[8,16,1664]{2,1,0:T(8,128)}, f32[3328,128]{1,0:T(8,128)S(1)}) custom-call(f32[96,256]{1,0:T(8,128)S(1)} %pad_maximum_fusion.1.factor_ref, f32[8,4,672,256]{3,2,1,0:T(8,128)} %bitcast.29, f32[8,4,672,256]{3,2,1,0:T(8,128)} %bitcast.30, ...), custom_call_target="tpu_custom_call" | custom-call | flops 1962934272 | bytes 18743296 | tf_op jit(solution)/shard_map/mode3/pallas_call | solution.py:107
  11.3 2.0 %collective-permute-start = (f32[8,16,1664]{2,1,0:T(8,128)}, f32[8,16,1664]{2,1,0:T(8,128)}, u32[]{:S(2)}, u32[]{:S(2)}) collective-permute-start(f32[8,16,1664]{2,1,0:T(8,128)} %get-tuple-element.42), channel_id=1, source_target_pairs={{0,1},{1,2},{2,3},{3,0},{4,5},{5,6},{6,7},{7,4},{8,9},{9,10},{10,1... | collective-permute-start | bytes 2555912 | tf_op jit(solution)/shard_map/ppermute | solution.py:531
  13.3 2.5 %collective-permute-start.1 = (f32[8,16,1664]{2,1,0:T(8,128)}, f32[8,16,1664]{2,1,0:T(8,128)}, u32[]{:S(2)}, u32[]{:S(2)}) collective-permute-start(f32[8,16,1664]{2,1,0:T(8,128)} %get-tuple-element.43), channel_id=1, source_target_pairs={{0,2},{1,3},{2,0},{3,1},{4,6},{5,7},{6,4},{7,5},{8,10},{9,11},{10,... | collective-permute-start | bytes 2555912 | tf_op jit(solution)/shard_map/ppermute | solution.py:531
  15.8 1.1 collective-permute-start.2
  16.9 5.9 %mode3.3 = (f32[8,16,1024]{2,1,0:T(8,128)S(1)}, f32[8,16,1024]{2,1,0:T(8,128)S(1)}, f32[8,16,1024]{2,1,0:T(8,128)S(1)}, f32[8,16,1024]{2,1,0:T(8,128)S(1)}, f32[2048,128]{1,0:T(8,128)S(1)}) custom-call(f32[96,256]{1,0:T(8,128)S(1)} %pad_maximum_fusion.1.factor_ref, f32[8,4,672,256]{3,2,1,0:T(8,128)} %bitcast.33, f32[8,4,672,256]{3,2,1,0:T(8,128)} %bitcast.34), custom_call_target="tpu_custom_call" | custom-call | flops 1207959552 | bytes 11534336 | tf_op jit(solution)/shard_map/mode3/pallas_call | solution.py:107
  25.3 1.7 pad_maximum_fusion
  27.0 9.7 %all-to-all-start = ((f32[32,168,128]{2,1,0:T(8,128)}), f32[32,168,128]{2,1,0:T(8,128)S(1)}, u32[]{:S(2)}, u32[]{:S(2)}) async-start(f32[32,168,128]{2,1,0:T(8,128)} %pad_maximum_fusion), calls=%async_computation | async-start | bytes 5505024 | tf_op jit(solution)/shard_map/all_to_all | solution.py:535
  37.3 1.7 broadcast_multiply_fusion
  38.9 2.8 %mul.30.weights_ref = f32[128,256]{1,0:T(8,128)S(1)} reshape(f32[16,8,32,8]{3,2,1,0:T(8,128)} %broadcast_multiply_fusion) | data formatting | bytes 262144 | tf_op jit(solution)/shard_map/mul | solution.py:514
  41.8 10.9 %collective-permute-done.1.refs_2_ = f32[8,16,1664]{2,1,0:T(8,128)} collective-permute-done((f32[8,16,1664]{2,1,0:T(8,128)}, f32[8,16,1664]{2,1,0:T(8,128)}, u32[]{:S(2)}, u32[]{:S(2)}) %collective-permute-start.1) | collective-permute-done | bytes 852000 | tf_op jit(solution)/shard_map/ppermute | solution.py:531
  53.7 3.0 %collective-permute-start.4 = (f32[8,16,1024]{2,1,0:T(8,128)}, f32[8,16,1024]{2,1,0:T(8,128)}, u32[]{:S(2)}, u32[]{:S(2)}) collective-permute-start(f32[8,16,1024]{2,1,0:T(8,128)} %copy-done.7), channel_id=1, source_target_pairs={{0,2},{1,3},{2,0},{3,1},{4,6},{5,7},{6,4},{7,5},{8,10},{9,11},{10,... | collective-permute-start | bytes 1572872 | tf_op jit(solution)/shard_map/ppermute | solution.py:531
  56.9 1.2 copy-done.5
  58.0 2.4 %species.2 = f32[32,104,128]{2,1,0:T(8,128)S(1)} custom-call(f32[128,256]{1,0:T(8,128)S(1)} %mul.30.weights_ref, f32[8,16,1664]{2,1,0:T(8,128)S(1)} %copy-done.5, f32[8,16,1664]{2,1,0:T(8,128)} %collective-permute-done.refs_1_, f32[8,16,1664]{2,1,0:T(8,128)} %collective-permute-done.1.refs_2_, f32[8,16,1664]{2,1,0:T(8,128)} %collective-permute-done.2.refs_3_), custom_call_target="tpu_custom_call" | custom-call | flops 99999997952 | bytes 7667712 | tf_op jit(solution)/shard_map/species/pallas_call | solution.py:138
  60.5 1.2 copy-done
  61.6 10.4 %all-to-all-done = f32[32,168,128]{2,1,0:T(8,128)S(1)} async-done(((f32[32,168,128]{2,1,0:T(8,128)}), f32[32,168,128]{2,1,0:T(8,128)S(1)}, u32[]{:S(2)}, u32[]{:S(2)}) %all-to-all-start) | async-done | bytes 2752544 | tf_op jit(solution)/shard_map/all_to_all | solution.py:535
  72.1 5.3 %all-to-all-start.2 = ((f32[32,104,128]{2,1,0:T(8,128)}), f32[32,104,128]{2,1,0:T(8,128)}, u32[]{:S(2)}, u32[]{:S(2)}) async-start(f32[32,104,128]{2,1,0:T(8,128)} %copy-done), calls=%async_computation.2 | async-start | bytes 3407872 | tf_op jit(solution)/shard_map/all_to_all | solution.py:535
  77.4 2.5 %mode2.1 = (f32[1008,128]{1,0:T(8,128)S(1)}, f32[1008,128]{1,0:T(8,128)}, f32[1008,128]{1,0:T(8,128)}, f32[1008,128]{1,0:T(8,128)}) custom-call(f32[96,128]{1,0:T(8,128)S(1)} %fusion.1.factor_ref, f32[5376,128]{1,0:T(8,128)S(1)} %bitcast.23), custom_call_target="tpu_custom_call" | custom-call | flops 99999997952 | bytes 6291456 | tf_op jit(solution)/shard_map/mode2/pallas_call | solution.py:191
  81.4 2.3 %collective-permute-start.7 = (f32[1008,128]{1,0:T(8,128)}, f32[1008,128]{1,0:T(8,128)S(1)}, u32[]{:S(2)}, u32[]{:S(2)}) collective-permute-start(f32[1008,128]{1,0:T(8,128)} %get-tuple-element.73), channel_id=1, source_target_pairs={{0,2},{1,3},{2,0},{3,1},{4,6},{5,7},{6,4},{7,5},{8,10},{9,11},{10,... | collective-permute-start | bytes 1548296 | tf_op jit(solution)/shard_map/ppermute | solution.py:531
  83.8 2.9 %species.3 = f32[32,64,128]{2,1,0:T(8,128)} custom-call(f32[128,256]{1,0:T(8,128)S(1)} %mul.30.weights_ref, f32[8,16,1024]{2,1,0:T(8,128)S(1)} %get-tuple-element.64.refs_0_, f32[8,16,1024]{2,1,0:T(8,128)} %collective-permute-done.3.refs_1_, f32[8,16,1024]{2,1,0:T(8,128)} %collective-permute-done.4.refs_2_, f32[8,16,1024]{2,1,0:T(8,128)} %collective-permute-done.5.refs_3_), custom_call_target="tpu_custom_call" | custom-call | flops 1000000000 | bytes 4718592 | tf_op jit(solution)/shard_map/species/pallas_call | solution.py:138
  86.7 14.9 %all-to-all-done.2 = f32[32,104,128]{2,1,0:T(8,128)} async-done(((f32[32,104,128]{2,1,0:T(8,128)}), f32[32,104,128]{2,1,0:T(8,128)}, u32[]{:S(2)}, u32[]{:S(2)}) %all-to-all-start.2) | async-done | bytes 1703968 | tf_op jit(solution)/shard_map/all_to_all | solution.py:535
  101.6 5.0 %all-to-all-start.1 = ((f32[32,64,128]{2,1,0:T(8,128)}), f32[32,64,128]{2,1,0:T(8,128)}, u32[]{:S(2)}, u32[]{:S(2)}) async-start(f32[32,64,128]{2,1,0:T(8,128)} %species.3), calls=%async_computation.1 | async-start | bytes 2097152 | tf_op jit(solution)/shard_map/all_to_all | solution.py:535
  106.6 1.0 copy-done.10
  107.7 2.4 %gram.4.other_ref = f32[2048,128]{1,0:T(8,128)S(1)} custom-call(f32[128,256]{1,0:T(8,128)S(1)} %mul.30.weights_ref, f32[1008,128]{1,0:T(8,128)S(1)} %copy-done.10, f32[1008,128]{1,0:T(8,128)S(1)} %collective-permute-done.6.refs_1_, f32[1008,128]{1,0:T(8,128)S(1)} %collective-permute-done.7.refs_2_, f32[1008,128]{1,0:T(8,128)S(1)} %collective-permute-done.8.refs_3_), custom_call_target="tpu_custom_call" | custom-call | flops 199999995904 | bytes 8388608 | tf_op jit(solution)/shard_map/gram/pallas_call | solution.py:335
  110.0 3.3 %gram.3 = (f32[896,128]{1,0:T(8,128)S(1)}, bf16[1536,416]{1,0:T(8,128)(2,1)S(1)}) custom-call(f32[96,128]{1,0:T(8,128)S(1)} %copy-done.2, f32[3328,128]{1,0:T(8,128)} %bitcast.13.part_ref), custom_call_target="tpu_custom_call" | custom-call | flops 531628032 | bytes 8388608 | tf_op jit(solution)/shard_map/gram/pallas_call | solution.py:335
  113.3 10.3 %all-to-all-done.1 = f32[32,64,128]{2,1,0:T(8,128)} async-done(((f32[32,64,128]{2,1,0:T(8,128)}), f32[32,64,128]{2,1,0:T(8,128)}, u32[]{:S(2)}, u32[]{:S(2)}) %all-to-all-start.1) | async-done | bytes 1048608 | tf_op jit(solution)/shard_map/all_to_all | solution.py:535
  123.6 3.2 %gram.5 = (f32[1024,128]{1,0:T(8,128)S(1)}, f32[1024,128]{1,0:T(8,128)S(1)}) custom-call(s32[1]{0:T(128)} %bitcast.me_ref.core_ref, f32[96,128]{1,0:T(8,128)S(1)} %copy-done.2, f32[2048,128]{1,0:T(8,128)} %bitcast.12.part_ref, bf16[1536,416]{1,0:T(8,128)(2,1)S(1)} %get-tuple-element.69.core_ref, f32[896,128]{1,0:T(8,128)S(1)} %get-tuple-element.70.early_ref, ...), custom_call_target="tpu_custom_call" | custom-call | flops 792723456 | bytes 8388608 | tf_op jit(solution)/shard_map/gram/pallas_call | solution.py:335
  127.1 1.8 collective-permute-done.9
  128.9 16.5 %all_to_all.25.x_ref = f32[64,16,128]{2,1,0:T(8,128)S(1)} all-to-all(f32[64,16,128]{2,1,0:T(8,128)S(1)} %bitcast.35), channel_id=1, replica_groups=mesh['y'=4,'z'=4,'core'=2,'narrow'=4] {'y','z','narrow'}, dimensions={0} | all-to-all | bytes 1048576 | tf_op jit(solution)/shard_map/all_to_all | solution.py:558
  145.5 15.4 %all_to_all.26 = f32[64,16,128]{2,1,0:T(8,128)S(1)} all-to-all(f32[64,16,128]{2,1,0:T(8,128)S(1)} %add.17), channel_id=1, replica_groups=mesh['y'=4,'z'=4,'core'=2,'narrow'=4] {'y','z','narrow'}, dimensions={0} | all-to-all | bytes 1048576 | tf_op jit(solution)/shard_map/all_to_all | solution.py:559
  161.0 3.3 %collective-permute-start.10 = (f32[1024,128]{1,0:T(8,128)S(1)}, f32[1024,128]{1,0:T(8,128)S(1)}, u32[]{:S(2)}, u32[]{:S(2)}) collective-permute-start(f32[1024,128]{1,0:T(8,128)S(1)} %bitcast.24), channel_id=1, source_target_pairs={{0,4},{4,0},{1,5},{5,1},{2,6},{6,2},{3,7},{7,3},{8,12},{12,8},{9,1... | collective-permute-start | bytes 1572872 | tf_op jit(solution)/shard_map/ppermute | solution.py:560
  164.2 1.5 collective-permute-done.10.other_ref
  165.8 33.8 %sweeps.1 = f32[96,672]{1,0:T(8,128)} custom-call(s32[1]{0:T(128)} %bitcast.me_ref.core_ref, f32[1024,128]{1,0:T(8,128)S(1)} %bitcast.25, f32[1024,128]{1,0:T(8,128)S(1)} %collective-permute-done.10.other_ref, f32[96,672]{1,0:T(8,128)S(1)} %bitcast.28), custom_call_target="tpu_custom_call" | custom-call | tf_op jit(solution)/shard_map/sweeps/pallas_call | solution.py:491
  (51 shorter events, 8.7 us)
Async XLA Ops:
  10.3 0.9 copy-start.4
  11.3 30.5 %collective-permute-start = (f32[8,16,1664]{2,1,0:T(8,128)}, f32[8,16,1664]{2,1,0:T(8,128)}, u32[]{:S(2)}, u32[]{:S(2)}) collective-permute-start(f32[8,16,1664]{2,1,0:T(8,128)} %get-tuple-element.42), channel_id=1, source_target_pairs={{0,1},{1,2},{2,3},{3,0},{4,5},{5,6},{6,7},{7,4},{8,9},{9,10},{10,1... | collective-permute-start | bytes 2555912 | tf_op jit(solution)/shard_map/ppermute | solution.py:531
  13.3 39.4 %collective-permute-start.1 = (f32[8,16,1664]{2,1,0:T(8,128)}, f32[8,16,1664]{2,1,0:T(8,128)}, u32[]{:S(2)}, u32[]{:S(2)}) collective-permute-start(f32[8,16,1664]{2,1,0:T(8,128)} %get-tuple-element.43), channel_id=1, source_target_pairs={{0,2},{1,3},{2,0},{3,1},{4,6},{5,7},{6,4},{7,5},{8,10},{9,11},{10,... | collective-permute-start | bytes 2555912 | tf_op jit(solution)/shard_map/ppermute | solution.py:531
  15.8 36.9 %collective-permute-start.2 = (f32[8,16,1664]{2,1,0:T(8,128)}, f32[8,16,1664]{2,1,0:T(8,128)}, u32[]{:S(2)}, u32[]{:S(2)}) collective-permute-start(f32[8,16,1664]{2,1,0:T(8,128)} %get-tuple-element.44), channel_id=1, source_target_pairs={{0,3},{1,0},{2,1},{3,2},{4,7},{5,4},{6,5},{7,6},{8,11},{9,8},{10,9... | collective-permute-start | bytes 2555912 | tf_op jit(solution)/shard_map/ppermute | solution.py:531
  22.9 0.8 copy-start.6
  23.7 0.8 copy-start.7
  24.5 0.8 copy-start.8
  27.0 9.8 %copy-start.12 = (f32[32,16]{0,1:T(8,128)S(1)}, f32[32,16]{0,1:T(8,128)}, u32[]{:S(2)}) copy-start(f32[32,16]{0,1:T(8,128)} %param.8) | copy-start | bytes 6148
  27.0 9.9 %copy-start.11 = (f32[128,96]{0,1:T(8,128)S(1)}, f32[128,96]{0,1:T(8,128)}, u32[]{:S(2)}) copy-start(f32[128,96]{0,1:T(8,128)} %param.6) | copy-start | bytes 147460
  27.0 45.1 %all-to-all-start = ((f32[32,168,128]{2,1,0:T(8,128)}), f32[32,168,128]{2,1,0:T(8,128)S(1)}, u32[]{:S(2)}, u32[]{:S(2)}) async-start(f32[32,168,128]{2,1,0:T(8,128)} %pad_maximum_fusion), calls=%async_computation | async-start | bytes 5505024 | tf_op jit(solution)/shard_map/all_to_all | solution.py:535
  37.1 4.6 %copy-start.1 = (f32[96,128]{1,0:T(8,128)}, f32[96,128]{1,0:T(8,128)S(1)}, u32[]{:S(2)}) copy-start(f32[96,128]{1,0:T(8,128)S(1)} %copy.23.factor_ref) | copy-start | bytes 147460
  52.7 28.0 %collective-permute-start.3 = (f32[8,16,1024]{2,1,0:T(8,128)}, f32[8,16,1024]{2,1,0:T(8,128)}, u32[]{:S(2)}, u32[]{:S(2)}) collective-permute-start(f32[8,16,1024]{2,1,0:T(8,128)} %copy-done.8), channel_id=1, source_target_pairs={{0,1},{1,2},{2,3},{3,0},{4,5},{5,6},{6,7},{7,4},{8,9},{9,10},{10,1... | collective-permute-start | bytes 1572872 | tf_op jit(solution)/shard_map/ppermute | solution.py:531
  53.7 27.0 %collective-permute-start.4 = (f32[8,16,1024]{2,1,0:T(8,128)}, f32[8,16,1024]{2,1,0:T(8,128)}, u32[]{:S(2)}, u32[]{:S(2)}) collective-permute-start(f32[8,16,1024]{2,1,0:T(8,128)} %copy-done.7), channel_id=1, source_target_pairs={{0,2},{1,3},{2,0},{3,1},{4,6},{5,7},{6,4},{7,5},{8,10},{9,11},{10,... | collective-permute-start | bytes 1572872 | tf_op jit(solution)/shard_map/ppermute | solution.py:531
  56.7 23.9 %collective-permute-start.5 = (f32[8,16,1024]{2,1,0:T(8,128)}, f32[8,16,1024]{2,1,0:T(8,128)}, u32[]{:S(2)}, u32[]{:S(2)}) collective-permute-start(f32[8,16,1024]{2,1,0:T(8,128)} %copy-done.6), channel_id=1, source_target_pairs={{0,3},{1,0},{2,1},{3,2},{4,7},{5,4},{6,5},{7,6},{8,11},{9,8},{10,9... | collective-permute-start | bytes 1572872 | tf_op jit(solution)/shard_map/ppermute | solution.py:531
  56.9 1.2 copy-start.5
  60.4 1.2 copy-start
  72.1 29.5 %all-to-all-start.2 = ((f32[32,104,128]{2,1,0:T(8,128)}), f32[32,104,128]{2,1,0:T(8,128)}, u32[]{:S(2)}, u32[]{:S(2)}) async-start(f32[32,104,128]{2,1,0:T(8,128)} %copy-done), calls=%async_computation.2 | async-start | bytes 3407872 | tf_op jit(solution)/shard_map/all_to_all | solution.py:535
  79.9 0.8 copy-start.9
  80.7 25.9 %collective-permute-start.6 = (f32[1008,128]{1,0:T(8,128)}, f32[1008,128]{1,0:T(8,128)S(1)}, u32[]{:S(2)}, u32[]{:S(2)}) collective-permute-start(f32[1008,128]{1,0:T(8,128)} %get-tuple-element.72), channel_id=1, source_target_pairs={{0,1},{1,2},{2,3},{3,0},{4,5},{5,6},{6,7},{7,4},{8,9},{9,10},{10,1... | collective-permute-start | bytes 1548296 | tf_op jit(solution)/shard_map/ppermute | solution.py:531
  81.4 25.2 %collective-permute-start.7 = (f32[1008,128]{1,0:T(8,128)}, f32[1008,128]{1,0:T(8,128)S(1)}, u32[]{:S(2)}, u32[]{:S(2)}) collective-permute-start(f32[1008,128]{1,0:T(8,128)} %get-tuple-element.73), channel_id=1, source_target_pairs={{0,2},{1,3},{2,0},{3,1},{4,6},{5,7},{6,4},{7,5},{8,10},{9,11},{10,... | collective-permute-start | bytes 1548296 | tf_op jit(solution)/shard_map/ppermute | solution.py:531
  83.6 23.0 %collective-permute-start.8 = (f32[1008,128]{1,0:T(8,128)}, f32[1008,128]{1,0:T(8,128)S(1)}, u32[]{:S(2)}, u32[]{:S(2)}) collective-permute-start(f32[1008,128]{1,0:T(8,128)} %get-tuple-element.74), channel_id=1, source_target_pairs={{0,3},{1,0},{2,1},{3,2},{4,7},{5,4},{6,5},{7,6},{8,11},{9,8},{10,9... | collective-permute-start | bytes 1548296 | tf_op jit(solution)/shard_map/ppermute | solution.py:531
  101.6 22.0 %all-to-all-start.1 = ((f32[32,64,128]{2,1,0:T(8,128)}), f32[32,64,128]{2,1,0:T(8,128)}, u32[]{:S(2)}, u32[]{:S(2)}) async-start(f32[32,64,128]{2,1,0:T(8,128)} %species.3), calls=%async_computation.1 | async-start | bytes 2097152 | tf_op jit(solution)/shard_map/all_to_all | solution.py:535
  106.6 1.0 copy-start.10
  107.7 2.4 %copy-start.2 = (f32[96,128]{1,0:T(8,128)S(1)}, f32[96,128]{1,0:T(8,128)}, u32[]{:S(2)}) copy-start(f32[96,128]{1,0:T(8,128)} %copy-done.1) | copy-start | bytes 147460
  126.8 2.0 collective-permute-start.9
  128.8 36.9 %copy-start.3 = (f32[672,96]{0,1:T(8,128)S(1)}, f32[672,96]{0,1:T(8,128)}, u32[]{:S(2)}) copy-start(f32[672,96]{0,1:T(8,128)} %param.9) | copy-start | bytes 774148
  161.0 4.8 %collective-permute-start.10 = (f32[1024,128]{1,0:T(8,128)S(1)}, f32[1024,128]{1,0:T(8,128)S(1)}, u32[]{:S(2)}, u32[]{:S(2)}) collective-permute-start(f32[1024,128]{1,0:T(8,128)S(1)} %bitcast.24), channel_id=1, source_target_pairs={{0,4},{4,0},{1,5},{5,1},{2,6},{6,2},{3,7},{7,3},{8,12},{12,8},{9,1... | collective-permute-start | bytes 1572872 | tf_op jit(solution)/shard_map/ppermute | solution.py:560

commit v5 on v4

--- a/solution.py
+++ b/solution.py
@@ -71,12 +71,22 @@
     return both[:rows] + both[rows:] + product(w_high, v_low, ((1,), (0,)))
 
 
-def mode3_kernel(factor_ref, *refs):
-    outs, rest_out, slabs = refs[-NARROW - 1:-1], refs[-1], refs[:-NARROW - 1]
+def mode3_kernel(joined, factor_ref, *refs):
+    outs, rest_out, slabs = refs[-NARROW - 1:-1], refs[-1], refs[joined:-NARROW - 1]
     f_high, f_low = split(factor_ref[...])
     lanes = ((1,), (1,))
     some = outs[0].shape[0]
     stride = rest_out.shape[0] // WIDE
+    start = 0
+    if joined:
+        earlier = refs[0]
+        start = earlier.shape[0] // WIDE
+
+        @pl.when(pl.program_id(0) == 0)
+        def _():
+            for r in range(WIDE):
+                rest_out[r * stride:r * stride + start, :] = earlier[r * start:(r + 1) * start, :]
+
     for s in range(some):
         rows = jnp.concatenate([slab[s].reshape(-1, I3) for slab in slabs], axis=0)
         r_high, r_low = split(rows)
@@ -85,39 +95,46 @@
         for j, out in enumerate(outs):
             out[s] = done[j * RANKS:(j + 1) * RANKS]
         place = pl.program_id(0) * some + s
-        for u in range(stride // LOCAL4):
-            rest_out[pl.ds(u * LOCAL4 + place, WIDE, stride=stride), :] = done[
+        for u in range(done.shape[1] // LANES):
+            rest_out[pl.ds(start + u * LOCAL4 + place, WIDE, stride=stride), :] = done[
                 NARROW_RANKS:, u * LANES:(u + 1) * LANES]
 
 
-def mode3(field, factor_rows, chunk):
+def mode3(field, factor_rows, chunk, earlier=None):
     species = field.shape[0]
     count = len(chunk)
     width = LOCAL2 * LANES * count
     some = 2
     in_specs = [pl.BlockSpec((R3, I3), lambda s: (0, 0))]
+    args = [factor_rows]
+    joined = 0
+    if earlier is not None:
+        joined = 1
+        in_specs.append(pl.BlockSpec(earlier.shape, lambda s: (0, 0)))
+        args.append(earlier)
     for tile in chunk:
         in_specs.append(pl.BlockSpec((some, LOCAL2, LANES, I3), lambda s, tile=tile: (s, 0, tile, 0)))
+        args.append(field)
     if chunk == CHUNKS[0]:
         width += LANES
         in_specs.append(pl.BlockSpec((some, LOCAL2, TAIL, I3), lambda s: (s, 0, BODY // TAIL, 0)))
-    args = [factor_rows] + [field] * (len(in_specs) - 1)
+        args.append(field)
     shape = jax.ShapeDtypeStruct((species, RANKS, width), jnp.float32)
-    rest = (WIDE * species * width // LANES, LANES)
+    rest = (WIDE * species * width // LANES + (earlier.shape[0] if joined else 0), LANES)
     out = pl.pallas_call(
-        mode3_kernel,
+        functools.partial(mode3_kernel, joined),
         grid=(species // some,),
         in_specs=in_specs,
         out_specs=[pl.BlockSpec((some, RANKS, width), lambda s: (s, 0, 0))] * NARROW
         + [pl.BlockSpec(rest, lambda s: (0, 0))],
         out_shape=[shape] * NARROW + [jax.ShapeDtypeStruct(rest, jnp.float32)],
-        compiler_params=pltpu.CompilerParams(vmem_limit_bytes=48 << 20),
+        compiler_params=pltpu.CompilerParams(vmem_limit_bytes=58 << 20),
         cost_estimate=pl.CostEstimate(
             flops=6 * species * R3 * I3 * width,
             bytes_accessed=4 * species * width * (I3 + R3), transcendentals=0),
         name="mode3",
     )(*args)
-    return out[:NARROW], out[NARROW].reshape(WIDE, -1, LANES)
+    return out[:NARROW], out[NARROW]
 
 
 def species_kernel(tiles, weights_ref, *refs):
@@ -406,10 +423,12 @@
     lane = lax.broadcasted_iota(jnp.int32, (8, n), 1)
     sub = lax.broadcasted_iota(jnp.int32, (8, n), 0)
     spread = lambda x: jnp.broadcast_to(x, (8, n))
+    columns = lambda i, k: [spread(rows[i][:, 8 * k + j:8 * k + j + 1]) for j in range(8)]
     pivots = []
+    ahead = columns(0, 0)
     for k in range(blocks):
-        cols = [[spread(rows[i][:, 8 * k + j:8 * k + j + 1]) for j in range(8)]
-                for i in range(k, blocks)]
+        cols = [ahead] + [columns(i, k) for i in range(k + 1, blocks)]
+        ahead = columns(k + 1, k + 1) if k + 1 < blocks else []
         inside = (lane >= 8 * k) & (lane < 8 * k + 8)
         rows[k] = jnp.where(inside, jnp.where(lane - 8 * k == sub, 1.0, 0.0), rows[k])
         for i in range(k + 1, blocks):
@@ -426,12 +445,16 @@
             u0, u1, u2 = s * over_det, q * over_det, p * over_det
             pair = {m: (spread(cols[0][m][j:j + 1, :]), spread(cols[0][m][j + 1:j + 2, :]))
                     for m in range(j + 2, 8)}
+            cross = [(spread(cols[1][j][m:m + 1, :]), spread(cols[1][j + 1][m:m + 1, :]))
+                     for m in range(len(ahead))]
             for i in range(k, blocks):
                 c0, c1 = cols[i - k][j], cols[i - k][j + 1]
                 f0, f1 = c0 * u0 - c1 * u1, c1 * u2 - c0 * u1
                 if i == k:
                     f0 = jnp.where(sub > j + 1, f0, jnp.where(sub == j + 1, q * over_p, 0.0))
                     f1 = jnp.where(sub > j + 1, f1, 0.0)
+                if i == k + 1:
+                    ahead = [x - (f0 * c[0] + f1 * c[1]) for x, c in zip(ahead, cross)]
                 rows[i] = rows[i] - (f0 * row0 + f1 * row1)
                 for m in range(j + 2, 8):
                     cols[i - k][m] = cols[i - k][m] - (f0 * pair[m][0] + f1 * pair[m][1])
@@ -536,8 +559,8 @@
 
     blocks, rest = mode3(field, turned, CHUNKS[0])
     first = send(blocks)
-    blocks, more = mode3(field, turned, CHUNKS[1])
-    raw = wide_exchange(jnp.concatenate([rest, more], axis=1))
+    blocks, rest = mode3(field, turned, CHUNKS[1], rest)
+    raw = wide_exchange(rest.reshape(WIDE, -1, LANES))
     first, blocks = lax.optimization_barrier((first, blocks))
     second = send(blocks)
     sums = species_sum(first, weights, SPECIES_COST)

time: 200 us -> 194 us (0.970)
  local copies, waits for them, and re-layouts: 12.3 us -> 8.93 us
  Pallas kernels: 65.2 us -> 63.1 us
    all_to_all x3, waiting for transfers between devices: 35.6 us -> 30.2 us  [wide_exchange(): return lax.all_to_all(x, WIDE_AXES, 0, 0, tiled=True).reshape(-1, LANES)]
    pallas_call x1, Pallas kernels: 33.8 us -> 28.6 us  [sweeps(): pl.pallas_call(sweep_kernel, in_specs=[pl.BlockSpec(memory_space=pltpu.SM...]
    ppermute x9, waiting for transfers between devices: 10.9 us -> 15.6 us  [send(): got[j] = lax.ppermute(blocks[j], 'narrow', ring)]
    unnamed x28 -> x22, local copies, waits for them, and re-layouts: 7.75 us -> 4.37 us
    pallas_call x2, Pallas kernels: 14.6 us -> 17.8 us  [mode3(): pl.pallas_call(functools.partial(mode3_kernel, joined), grid=(species //...]
  transfers between devices with their start and end apart: 14 -> 14, of which waited for: 6 -> 8; matrix products, arithmetic and copies ran while one was open for 3% -> 3% of each run, Pallas kernels for 10% -> 11%
where the time goes in v5:
time: 194 us; the launch traced here: 193 us
  Pallas kernels  63.1 us (33%)
  waiting for transfers between devices  49.1 us (25%)
  starting transfers between devices  37.2 us (19%)
  blocking collectives  32 us (16%)
  local copies, waits for them, and re-layouts  8.93 us (5%)
  other arithmetic  2.54 us (1%)
    all_to_all x3, waiting for transfers between devices, wide_exchange(): return lax.all_to_all(x, WIDE_AXES, 0, 0, tiled=True).reshape(-1, LANES)  30.2 us
    pallas_call x1, Pallas kernels, sweeps(): pl.pallas_call(sweep_kernel, in_specs=[pl.BlockSpec(memory_space=pltpu.SM...  28.6 us
    all_to_all x3, starting transfers between devices, wide_exchange(): return lax.all_to_all(x, WIDE_AXES, 0, 0, tiled=True).reshape(-1, LANES)  19.9 us
    pallas_call x2, Pallas kernels, mode3(): pl.pallas_call(functools.partial(mode3_kernel, joined), grid=(species //...  17.8 us
    all_to_all x1, blocking collectives, body(): half = add_parts(lax.all_to_all(half, chips, 0, 0, tiled=True))  16.5 us
    ppermute x9, waiting for transfers between devices, send(): got[j] = lax.ppermute(blocks[j], 'narrow', ring)  15.6 us
    all_to_all x1, blocking collectives, body(): mine = lax.all_to_all(half, chips, 0, 0, tiled=True).reshape(-1, LANES)  15.4 us
    ppermute x9, starting transfers between devices, send(): got[j] = lax.ppermute(blocks[j], 'narrow', ring)  13.8 us
  transfers between devices with their start and end apart: 14, of which 8 were waited for; matrix products, arithmetic and copies ran while one was open for 3% of the time, Pallas kernels for 11%

profile of v5, /device:TPU:1, one launch (start us, length us, event | category | flops | bytes accessed | tf_op | source)
XLA Modules:
  0.0 193.0 jit_solution(8621929276252125363)
XLA Ops:
  2.3 9.5 %mode3.2 = (f32[8,16,1664]{2,1,0:T(8,128)}, f32[8,16,1664]{2,1,0:T(8,128)}, f32[8,16,1664]{2,1,0:T(8,128)}, f32[8,16,1664]{2,1,0:T(8,128)}, f32[3328,128]{1,0:T(8,128)}) custom-call(f32[96,256]{1,0:T(8,128)} %pad_maximum_fusion.factor_ref, f32[8,4,672,256]{3,2,1,0:T(8,128)} %bitcast.26, f32[8,4,672,256]{3,2,1,0:T(8,128)} %bitcast.27, ...), custom_call_target="tpu_custom_call" | custom-call | flops 1962934272 | bytes 18743296 | tf_op jit(solution)/shard_map/mode3/pallas_call | solution.py:124
  11.7 2.1 %collective-permute-start = (f32[8,16,1664]{2,1,0:T(8,128)}, f32[8,16,1664]{2,1,0:T(8,128)}, u32[]{:S(2)}, u32[]{:S(2)}) collective-permute-start(f32[8,16,1664]{2,1,0:T(8,128)} %get-tuple-element.42), channel_id=1, source_target_pairs={{0,1},{1,2},{2,3},{3,0},{4,5},{5,6},{6,7},{7,4},{8,9},{9,10},{10,1... | collective-permute-start | bytes 2555912 | tf_op jit(solution)/shard_map/ppermute | solution.py:554
  13.9 2.4 %collective-permute-start.1 = (f32[8,16,1664]{2,1,0:T(8,128)}, f32[8,16,1664]{2,1,0:T(8,128)}, u32[]{:S(2)}, u32[]{:S(2)}) collective-permute-start(f32[8,16,1664]{2,1,0:T(8,128)} %get-tuple-element.43), channel_id=1, source_target_pairs={{0,2},{1,3},{2,0},{3,1},{4,6},{5,7},{6,4},{7,5},{8,10},{9,11},{10,... | collective-permute-start | bytes 2555912 | tf_op jit(solution)/shard_map/ppermute | solution.py:554
  16.3 1.2 collective-permute-start.2
  17.5 8.3 %mode3.3 = (f32[8,16,1024]{2,1,0:T(8,128)}, f32[8,16,1024]{2,1,0:T(8,128)}, f32[8,16,1024]{2,1,0:T(8,128)}, f32[8,16,1024]{2,1,0:T(8,128)}, f32[5376,128]{1,0:T(8,128)}) custom-call(f32[96,256]{1,0:T(8,128)} %pad_maximum_fusion.factor_ref, f32[3328,128]{1,0:T(8,128)} %get-tuple-element.45.refs_0_, f32[8,4,672,256]{3,2,1,0:T(8,128)} %bitcast.30, ...), custom_call_target="tpu_custom_call" | custom-call | flops 1207959552 | bytes 11534336 | tf_op jit(solution)/shard_map/mode3/pallas_call | solution.py:124
  25.8 9.6 %all-to-all-start = ((f32[32,168,128]{2,1,0:T(8,128)}), f32[32,168,128]{2,1,0:T(8,128)S(1)}, u32[]{:S(2)}, u32[]{:S(2)}) async-start(f32[32,168,128]{2,1,0:T(8,128)} %bitcast.32), calls=%async_computation | async-start | bytes 5505024 | tf_op jit(solution)/shard_map/all_to_all | solution.py:558
  35.7 1.7 broadcast_multiply_fusion
  37.4 2.8 %mul.30.weights_ref = f32[128,256]{1,0:T(8,128)S(1)} reshape(f32[16,8,32,8]{3,2,1,0:T(8,128)} %broadcast_multiply_fusion) | data formatting | bytes 262144 | tf_op jit(solution)/shard_map/mul | solution.py:537
  40.4 12.8 %collective-permute-done.1.refs_2_ = f32[8,16,1664]{2,1,0:T(8,128)} collective-permute-done((f32[8,16,1664]{2,1,0:T(8,128)}, f32[8,16,1664]{2,1,0:T(8,128)}, u32[]{:S(2)}, u32[]{:S(2)}) %collective-permute-start.1) | collective-permute-done | bytes 852000 | tf_op jit(solution)/shard_map/ppermute | solution.py:554
  53.2 1.2 collective-permute-start.3
  54.4 3.0 %collective-permute-start.4 = (f32[8,16,1024]{2,1,0:T(8,128)}, f32[8,16,1024]{2,1,0:T(8,128)}, u32[]{:S(2)}, u32[]{:S(2)}) collective-permute-start(f32[8,16,1024]{2,1,0:T(8,128)} %get-tuple-element.52), channel_id=1, source_target_pairs={{0,2},{1,3},{2,0},{3,1},{4,6},{5,7},{6,4},{7,5},{8,10},{9,11},{10,... | collective-permute-start | bytes 1572872 | tf_op jit(solution)/shard_map/ppermute | solution.py:554
  58.6 2.4 %species.2 = f32[32,104,128]{2,1,0:T(8,128)S(1)} custom-call(f32[128,256]{1,0:T(8,128)S(1)} %mul.30.weights_ref, f32[8,16,1664]{2,1,0:T(8,128)S(1)} %copy-done.4, f32[8,16,1664]{2,1,0:T(8,128)} %collective-permute-done.refs_1_, f32[8,16,1664]{2,1,0:T(8,128)} %collective-permute-done.1.refs_2_, f32[8,16,1664]{2,1,0:T(8,128)} %collective-permute-done.2.refs_3_), custom_call_target="tpu_custom_call" | custom-call | flops 99999997952 | bytes 7667712 | tf_op jit(solution)/shard_map/species/pallas_call | solution.py:155
  61.0 1.2 copy-done
  62.2 8.5 %all-to-all-done = f32[32,168,128]{2,1,0:T(8,128)S(1)} async-done(((f32[32,168,128]{2,1,0:T(8,128)}), f32[32,168,128]{2,1,0:T(8,128)S(1)}, u32[]{:S(2)}, u32[]{:S(2)}) %all-to-all-start) | async-done | bytes 2752544 | tf_op jit(solution)/shard_map/all_to_all | solution.py:558
  70.7 5.3 %all-to-all-start.2 = ((f32[32,104,128]{2,1,0:T(8,128)}), f32[32,104,128]{2,1,0:T(8,128)}, u32[]{:S(2)}, u32[]{:S(2)}) async-start(f32[32,104,128]{2,1,0:T(8,128)} %copy-done), calls=%async_computation.2 | async-start | bytes 3407872 | tf_op jit(solution)/shard_map/all_to_all | solution.py:558
  76.0 2.5 %mode2.1 = (f32[1008,128]{1,0:T(8,128)S(1)}, f32[1008,128]{1,0:T(8,128)}, f32[1008,128]{1,0:T(8,128)}, f32[1008,128]{1,0:T(8,128)}) custom-call(f32[96,128]{1,0:T(8,128)S(1)} %fusion.1.factor_ref, f32[5376,128]{1,0:T(8,128)S(1)} %bitcast.22), custom_call_target="tpu_custom_call" | custom-call | flops 99999997952 | bytes 6291456 | tf_op jit(solution)/shard_map/mode2/pallas_call | solution.py:208
  80.4 1.5 collective-permute-start.6
  81.9 2.3 %collective-permute-start.7 = (f32[1008,128]{1,0:T(8,128)}, f32[1008,128]{1,0:T(8,128)S(1)}, u32[]{:S(2)}, u32[]{:S(2)}) collective-permute-start(f32[1008,128]{1,0:T(8,128)} %get-tuple-element.73), channel_id=1, source_target_pairs={{0,2},{1,3},{2,0},{3,1},{4,6},{5,7},{6,4},{7,5},{8,10},{9,11},{10,... | collective-permute-start | bytes 1548296 | tf_op jit(solution)/shard_map/ppermute | solution.py:554
  84.3 2.9 %species.3 = f32[32,64,128]{2,1,0:T(8,128)} custom-call(f32[128,256]{1,0:T(8,128)S(1)} %mul.30.weights_ref, f32[8,16,1024]{2,1,0:T(8,128)S(1)} %copy-done.5, f32[8,16,1024]{2,1,0:T(8,128)} %collective-permute-done.3.refs_1_, f32[8,16,1024]{2,1,0:T(8,128)} %collective-permute-done.4.refs_2_, f32[8,16,1024]{2,1,0:T(8,128)} %collective-permute-done.5.refs_3_), custom_call_target="tpu_custom_call" | custom-call | flops 1000000000 | bytes 4718592 | tf_op jit(solution)/shard_map/species/pallas_call | solution.py:155
  87.2 13.0 %all-to-all-done.2 = f32[32,104,128]{2,1,0:T(8,128)} async-done(((f32[32,104,128]{2,1,0:T(8,128)}), f32[32,104,128]{2,1,0:T(8,128)}, u32[]{:S(2)}, u32[]{:S(2)}) %all-to-all-start.2) | async-done | bytes 1703968 | tf_op jit(solution)/shard_map/all_to_all | solution.py:558
  100.2 5.0 %all-to-all-start.1 = ((f32[32,64,128]{2,1,0:T(8,128)}), f32[32,64,128]{2,1,0:T(8,128)}, u32[]{:S(2)}, u32[]{:S(2)}) async-start(f32[32,64,128]{2,1,0:T(8,128)} %species.3), calls=%async_computation.1 | async-start | bytes 2097152 | tf_op jit(solution)/shard_map/all_to_all | solution.py:558
  105.2 1.7 collective-permute-done.7.refs_2_
  107.9 2.4 %gram.4.other_ref = f32[2048,128]{1,0:T(8,128)S(1)} custom-call(f32[128,256]{1,0:T(8,128)S(1)} %mul.30.weights_ref, f32[1008,128]{1,0:T(8,128)S(1)} %copy-done.7, f32[1008,128]{1,0:T(8,128)S(1)} %collective-permute-done.6.refs_1_, f32[1008,128]{1,0:T(8,128)S(1)} %collective-permute-done.7.refs_2_, f32[1008,128]{1,0:T(8,128)S(1)} %collective-permute-done.8.refs_3_), custom_call_target="tpu_custom_call" | custom-call | flops 199999995904 | bytes 8388608 | tf_op jit(solution)/shard_map/gram/pallas_call | solution.py:352
  110.3 3.3 %gram.3 = (f32[896,128]{1,0:T(8,128)S(1)}, bf16[1536,416]{1,0:T(8,128)(2,1)S(1)}) custom-call(f32[96,128]{1,0:T(8,128)S(1)} %copy-done.2, f32[3328,128]{1,0:T(8,128)} %bitcast.12.part_ref), custom_call_target="tpu_custom_call" | custom-call | flops 531628032 | bytes 8388608 | tf_op jit(solution)/shard_map/gram/pallas_call | solution.py:352
  113.6 8.7 %all-to-all-done.1 = f32[32,64,128]{2,1,0:T(8,128)} async-done(((f32[32,64,128]{2,1,0:T(8,128)}), f32[32,64,128]{2,1,0:T(8,128)}, u32[]{:S(2)}, u32[]{:S(2)}) %all-to-all-start.1) | async-done | bytes 1048608 | tf_op jit(solution)/shard_map/all_to_all | solution.py:558
  122.3 3.2 %gram.5 = (f32[1024,128]{1,0:T(8,128)S(1)}, f32[1024,128]{1,0:T(8,128)S(1)}) custom-call(s32[1]{0:T(128)} %bitcast.me_ref.core_ref, f32[96,128]{1,0:T(8,128)S(1)} %copy-done.2, f32[2048,128]{1,0:T(8,128)} %bitcast.11.part_ref, bf16[1536,416]{1,0:T(8,128)(2,1)S(1)} %get-tuple-element.69.core_ref, f32[896,128]{1,0:T(8,128)S(1)} %get-tuple-element.70.early_ref, ...), custom_call_target="tpu_custom_call" | custom-call | flops 792723456 | bytes 8388608 | tf_op jit(solution)/shard_map/gram/pallas_call | solution.py:352
  125.7 1.8 collective-permute-done.9
  127.6 16.5 %all_to_all.25.x_ref = f32[64,16,128]{2,1,0:T(8,128)S(1)} all-to-all(f32[64,16,128]{2,1,0:T(8,128)S(1)} %bitcast.33), channel_id=1, replica_groups=mesh['y'=4,'z'=4,'core'=2,'narrow'=4] {'y','z','narrow'}, dimensions={0} | all-to-all | bytes 1048576 | tf_op jit(solution)/shard_map/all_to_all | solution.py:581
  144.2 15.4 %all_to_all.26 = f32[64,16,128]{2,1,0:T(8,128)S(1)} all-to-all(f32[64,16,128]{2,1,0:T(8,128)S(1)} %add.17), channel_id=1, replica_groups=mesh['y'=4,'z'=4,'core'=2,'narrow'=4] {'y','z','narrow'}, dimensions={0} | all-to-all | bytes 1048576 | tf_op jit(solution)/shard_map/all_to_all | solution.py:582
  159.6 3.3 %collective-permute-start.10 = (f32[1024,128]{1,0:T(8,128)S(1)}, f32[1024,128]{1,0:T(8,128)S(1)}, u32[]{:S(2)}, u32[]{:S(2)}) collective-permute-start(f32[1024,128]{1,0:T(8,128)S(1)} %bitcast.23), channel_id=1, source_target_pairs={{0,4},{4,0},{1,5},{5,1},{2,6},{6,2},{3,7},{7,3},{8,12},{12,8},{9,1... | collective-permute-start | bytes 1572872 | tf_op jit(solution)/shard_map/ppermute | solution.py:583
  162.9 1.5 collective-permute-done.10.other_ref
  164.4 28.6 %sweeps.1 = f32[96,672]{1,0:T(8,128)} custom-call(s32[1]{0:T(128)} %bitcast.me_ref.core_ref, f32[1024,128]{1,0:T(8,128)S(1)} %bitcast.24, f32[1024,128]{1,0:T(8,128)S(1)} %collective-permute-done.10.other_ref, f32[96,672]{1,0:T(8,128)S(1)} %bitcast.25), custom_call_target="tpu_custom_call" | custom-call | tf_op jit(solution)/shard_map/sweeps/pallas_call | solution.py:514
  (44 shorter events, 7.4 us)
Async XLA Ops:
  11.7 28.7 %collective-permute-start = (f32[8,16,1664]{2,1,0:T(8,128)}, f32[8,16,1664]{2,1,0:T(8,128)}, u32[]{:S(2)}, u32[]{:S(2)}) collective-permute-start(f32[8,16,1664]{2,1,0:T(8,128)} %get-tuple-element.42), channel_id=1, source_target_pairs={{0,1},{1,2},{2,3},{3,0},{4,5},{5,6},{6,7},{7,4},{8,9},{9,10},{10,1... | collective-permute-start | bytes 2555912 | tf_op jit(solution)/shard_map/ppermute | solution.py:554
  13.9 39.4 %collective-permute-start.1 = (f32[8,16,1664]{2,1,0:T(8,128)}, f32[8,16,1664]{2,1,0:T(8,128)}, u32[]{:S(2)}, u32[]{:S(2)}) collective-permute-start(f32[8,16,1664]{2,1,0:T(8,128)} %get-tuple-element.43), channel_id=1, source_target_pairs={{0,2},{1,3},{2,0},{3,1},{4,6},{5,7},{6,4},{7,5},{8,10},{9,11},{10,... | collective-permute-start | bytes 2555912 | tf_op jit(solution)/shard_map/ppermute | solution.py:554
  16.3 36.9 %collective-permute-start.2 = (f32[8,16,1664]{2,1,0:T(8,128)}, f32[8,16,1664]{2,1,0:T(8,128)}, u32[]{:S(2)}, u32[]{:S(2)}) collective-permute-start(f32[8,16,1664]{2,1,0:T(8,128)} %get-tuple-element.44), channel_id=1, source_target_pairs={{0,3},{1,0},{2,1},{3,2},{4,7},{5,4},{6,5},{7,6},{8,11},{9,8},{10,9... | collective-permute-start | bytes 2555912 | tf_op jit(solution)/shard_map/ppermute | solution.py:554
  25.8 9.6 %copy-start.9 = (f32[32,16]{0,1:T(8,128)S(1)}, f32[32,16]{0,1:T(8,128)}, u32[]{:S(2)}) copy-start(f32[32,16]{0,1:T(8,128)} %param.8) | copy-start | bytes 6148
  25.8 44.9 %all-to-all-start = ((f32[32,168,128]{2,1,0:T(8,128)}), f32[32,168,128]{2,1,0:T(8,128)S(1)}, u32[]{:S(2)}, u32[]{:S(2)}) async-start(f32[32,168,128]{2,1,0:T(8,128)} %bitcast.32), calls=%async_computation | async-start | bytes 5505024 | tf_op jit(solution)/shard_map/all_to_all | solution.py:558
  35.7 4.5 %copy-start.8 = (f32[128,96]{0,1:T(8,128)S(1)}, f32[128,96]{0,1:T(8,128)}, u32[]{:S(2)}) copy-start(f32[128,96]{0,1:T(8,128)} %param.6) | copy-start | bytes 147460
  40.4 20.6 %copy-start.1 = (f32[96,128]{1,0:T(8,128)}, f32[96,128]{1,0:T(8,128)S(1)}, u32[]{:S(2)}) copy-start(f32[96,128]{1,0:T(8,128)S(1)} %copy.23.factor_ref) | copy-start | bytes 147460
  53.2 26.1 %collective-permute-start.3 = (f32[8,16,1024]{2,1,0:T(8,128)}, f32[8,16,1024]{2,1,0:T(8,128)}, u32[]{:S(2)}, u32[]{:S(2)}) collective-permute-start(f32[8,16,1024]{2,1,0:T(8,128)} %get-tuple-element.51), channel_id=1, source_target_pairs={{0,1},{1,2},{2,3},{3,0},{4,5},{5,6},{6,7},{7,4},{8,9},{9,10},{10,1... | collective-permute-start | bytes 1572872 | tf_op jit(solution)/shard_map/ppermute | solution.py:554
  54.4 26.0 %collective-permute-start.4 = (f32[8,16,1024]{2,1,0:T(8,128)}, f32[8,16,1024]{2,1,0:T(8,128)}, u32[]{:S(2)}, u32[]{:S(2)}) collective-permute-start(f32[8,16,1024]{2,1,0:T(8,128)} %get-tuple-element.52), channel_id=1, source_target_pairs={{0,2},{1,3},{2,0},{3,1},{4,6},{5,7},{6,4},{7,5},{8,10},{9,11},{10,... | collective-permute-start | bytes 1572872 | tf_op jit(solution)/shard_map/ppermute | solution.py:554
  57.3 23.1 %collective-permute-start.5 = (f32[8,16,1024]{2,1,0:T(8,128)}, f32[8,16,1024]{2,1,0:T(8,128)}, u32[]{:S(2)}, u32[]{:S(2)}) collective-permute-start(f32[8,16,1024]{2,1,0:T(8,128)} %get-tuple-element.53), channel_id=1, source_target_pairs={{0,3},{1,0},{2,1},{3,2},{4,7},{5,4},{6,5},{7,6},{8,11},{9,8},{10,9... | collective-permute-start | bytes 1572872 | tf_op jit(solution)/shard_map/ppermute | solution.py:554
  57.4 1.2 copy-start.4
  61.0 1.2 copy-start
  70.7 29.5 %all-to-all-start.2 = ((f32[32,104,128]{2,1,0:T(8,128)}), f32[32,104,128]{2,1,0:T(8,128)}, u32[]{:S(2)}, u32[]{:S(2)}) async-start(f32[32,104,128]{2,1,0:T(8,128)} %copy-done), calls=%async_computation.2 | async-start | bytes 3407872 | tf_op jit(solution)/shard_map/all_to_all | solution.py:558
  76.0 8.3 %copy-start.5 = (f32[8,16,1024]{2,1,0:T(8,128)S(1)}, f32[8,16,1024]{2,1,0:T(8,128)}, u32[]{:S(2)}) copy-start(f32[8,16,1024]{2,1,0:T(8,128)} %get-tuple-element.64.refs_0_) | copy-start | bytes 1572868
  78.5 0.8 copy-start.6
  80.4 24.8 %collective-permute-start.6 = (f32[1008,128]{1,0:T(8,128)}, f32[1008,128]{1,0:T(8,128)S(1)}, u32[]{:S(2)}, u32[]{:S(2)}) collective-permute-start(f32[1008,128]{1,0:T(8,128)} %get-tuple-element.72), channel_id=1, source_target_pairs={{0,1},{1,2},{2,3},{3,0},{4,5},{5,6},{6,7},{7,4},{8,9},{9,10},{10,1... | collective-permute-start | bytes 1548296 | tf_op jit(solution)/shard_map/ppermute | solution.py:554
  81.9 25.0 %collective-permute-start.7 = (f32[1008,128]{1,0:T(8,128)}, f32[1008,128]{1,0:T(8,128)S(1)}, u32[]{:S(2)}, u32[]{:S(2)}) collective-permute-start(f32[1008,128]{1,0:T(8,128)} %get-tuple-element.73), channel_id=1, source_target_pairs={{0,2},{1,3},{2,0},{3,1},{4,6},{5,7},{6,4},{7,5},{8,10},{9,11},{10,... | collective-permute-start | bytes 1548296 | tf_op jit(solution)/shard_map/ppermute | solution.py:554
  84.2 22.6 %collective-permute-start.8 = (f32[1008,128]{1,0:T(8,128)}, f32[1008,128]{1,0:T(8,128)S(1)}, u32[]{:S(2)}, u32[]{:S(2)}) collective-permute-start(f32[1008,128]{1,0:T(8,128)} %get-tuple-element.74), channel_id=1, source_target_pairs={{0,3},{1,0},{2,1},{3,2},{4,7},{5,4},{6,5},{7,6},{8,11},{9,8},{10,9... | collective-permute-start | bytes 1548296 | tf_op jit(solution)/shard_map/ppermute | solution.py:554
  100.2 22.0 %all-to-all-start.1 = ((f32[32,64,128]{2,1,0:T(8,128)}), f32[32,64,128]{2,1,0:T(8,128)}, u32[]{:S(2)}, u32[]{:S(2)}) async-start(f32[32,64,128]{2,1,0:T(8,128)} %species.3), calls=%async_computation.1 | async-start | bytes 2097152 | tf_op jit(solution)/shard_map/all_to_all | solution.py:558
  106.9 1.0 copy-start.7
  107.9 2.4 %copy-start.2 = (f32[96,128]{1,0:T(8,128)S(1)}, f32[96,128]{1,0:T(8,128)}, u32[]{:S(2)}) copy-start(f32[96,128]{1,0:T(8,128)} %copy-done.1) | copy-start | bytes 147460
  125.5 2.0 %collective-permute-start.9 = (f32[1024,128]{1,0:T(8,128)S(1)}, f32[1024,128]{1,0:T(8,128)S(1)}, u32[]{:S(2)}, u32[]{:S(2)}) collective-permute-start(f32[1024,128]{1,0:T(8,128)S(1)} %get-tuple-element.76), channel_id=1, source_target_pairs={{0,4},{4,0},{1,5},{5,1},{2,6},{6,2},{3,7},{7,3},{8,12},{12,8},{9,1... | collective-permute-start | bytes 1572872 | tf_op jit(solution)/shard_map/ppermute | solution.py:578
  127.5 36.9 %copy-start.3 = (f32[672,96]{0,1:T(8,128)S(1)}, f32[672,96]{0,1:T(8,128)}, u32[]{:S(2)}) copy-start(f32[672,96]{0,1:T(8,128)} %param.9) | copy-start | bytes 774148
  159.6 4.8 %collective-permute-start.10 = (f32[1024,128]{1,0:T(8,128)S(1)}, f32[1024,128]{1,0:T(8,128)S(1)}, u32[]{:S(2)}, u32[]{:S(2)}) collective-permute-start(f32[1024,128]{1,0:T(8,128)S(1)} %bitcast.23), channel_id=1, source_target_pairs={{0,4},{4,0},{1,5},{5,1},{2,6},{6,2},{3,7},{7,3},{8,12},{12,8},{9,1... | collective-permute-start | bytes 1572872 | tf_op jit(solution)/shard_map/ppermute | solution.py:583
